TPU v7x, 32 devices: a whole 2x2x4 slice. The times are simulated.
32 devices in a mesh: dp: 4 (over y, x), seq: 8 (over z, core).
Axes of the slice: x: 2, y: 2, z: 4, core: 2. Of those that a mesh axis runs over, the one named last changes fastest.
Arguments:
- inputs: bfloat16 [4, 4096, 1024], P('dp', 'seq'), may hold values from -6 to 6
- out_grad: bfloat16 [4, 4096, 1024], P('dp', 'seq'), may hold values from -6 to 6
- w_in: bfloat16 [1024, 3072], replicated, may hold values from -0.1875 to 0.1875
- taps: float32 [3, 3072], replicated, may hold values from -3 to 3
- filt: bfloat16 [16, 256, 1024], P(None, 'seq'), may hold values from -4 to 4
Outputs:
- mixed: bfloat16 [4, 4096, 1024], P('dp', 'seq')
- in_grad: bfloat16 [4, 4096, 1024], P('dp', 'seq')
- w_in_grad: float32 [1024, 3072], P('dp', 'seq')
- taps_grad: float32 [3, 3072], replicated
All inputs are finite; a program needn't handle non-finite values.
Results may differ from a plain program's by a relative error of at most 0.012.
Values may be sent and summed in bfloat16 or wider, within the bound.
No kernel may reach another device: no remote copies, remote signals or barrier semaphores. Data moves between devices by JAX's collectives and lax.ppermute only.
A program may use at most 128 MiB of HBM per device.

v0:
```python
import math

import jax
import jax.numpy as jnp
from jax import lax
from jax.sharding import PartitionSpec as P

BLK = 256


def padded(cells, sides, width):
    for axis, dim in sides:
        count = lax.axis_size(axis)
        ends = count - 1
        head = lax.slice_in_dim(cells, 0, width, axis=dim)
        tail = lax.slice_in_dim(cells, cells.shape[dim] - width, cells.shape[dim], axis=dim)
        cells = jnp.concatenate(
            [
                lax.ppermute(tail, axis, [(i, (i + 1) % count) for i in range(ends)]),
                cells,
                lax.ppermute(head, axis, [((i + 1) % count, i) for i in range(ends)]),
            ],
            axis=dim,
        )
    return cells


def dct_table(count):
    rows = jnp.arange(count, dtype=jnp.float32)[:, None]
    cols = jnp.arange(count, dtype=jnp.float32)[None, :]
    first = jnp.where(rows == 0, jnp.float32(math.sqrt(0.5)), jnp.float32(1.0))
    table = (
        jnp.float32(math.sqrt(2.0 / count))
        * first
        * jnp.cos(jnp.float32(math.pi) * (cols + 0.5) * rows / count)
    )
    return table.astype(jnp.bfloat16)


def block_section(blocks, table_q):
    return jnp.einsum("rq,nbqd->nbrd", table_q, blocks, preferred_element_type=jnp.float32).astype(
        jnp.bfloat16
    )


def span_section(columns, filt, table_p):
    stack, span, narrow, width = columns.shape
    flat = columns.reshape(stack, span, narrow * width)
    second = jnp.einsum("ap,npk->nak", table_p, flat, preferred_element_type=jnp.float32)
    scaled = (filt.reshape(1, span, narrow * width).astype(jnp.float32) * second).astype(
        jnp.bfloat16
    )
    third = jnp.einsum("ap,nak->npk", table_p, scaled, preferred_element_type=jnp.float32).astype(
        jnp.bfloat16
    )
    return third.reshape(columns.shape)


def final_section(blocks, table_q):
    return jnp.einsum("rq,nbrd->nbqd", table_q, blocks, preferred_element_type=jnp.float32)


def shards(inputs, out_grad, w_in, taps, filt):
    tok = inputs.shape[1]
    width = inputs.shape[2]
    nseq = lax.axis_size("seq")
    ndata = lax.axis_size("dp")
    nblocks = tok // BLK
    table_q = dct_table(BLK)
    table_p = dct_table(filt.shape[0])
    factor = 1.0 / math.sqrt(ndata * nseq * tok)
    rows = inputs[0]
    z = jnp.dot(rows, w_in, preferred_element_type=jnp.float32).astype(jnp.bfloat16)
    zpad = padded(z, (("seq", 0),), 1)
    s = taps[0] * zpad[:-2] + taps[1] * zpad[1:-1] + taps[2] * zpad[2:]
    a_part = s[:, :width]
    g_part = s[:, width : 2 * width]
    v_part = s[:, 2 * width :]
    w = (a_part * v_part).astype(jnp.bfloat16)
    gradf = out_grad[0].astype(jnp.float32)
    e4 = (gradf * g_part).astype(jnp.bfloat16)
    columns = lax.all_to_all(
        block_section(w.reshape(1, nblocks, BLK, width), table_q),
        "seq",
        split_axis=2,
        concat_axis=1,
        tiled=True,
    )
    back = lax.all_to_all(
        span_section(columns, filt, table_p), "seq", split_axis=1, concat_axis=2, tiled=True
    )
    h4 = final_section(back, table_q).reshape(tok, width)
    grad_cols = lax.all_to_all(
        block_section(e4.reshape(1, nblocks, BLK, width), table_q),
        "seq",
        split_axis=2,
        concat_axis=1,
        tiled=True,
    )
    grad_back = lax.all_to_all(
        span_section(grad_cols, filt, table_p), "seq", split_axis=1, concat_axis=2, tiled=True
    )
    dw = final_section(grad_back, table_q).reshape(tok, width)
    mixed = (g_part * h4).astype(jnp.bfloat16)
    ds = jnp.concatenate([dw * v_part, gradf * h4, dw * a_part], axis=1).astype(jnp.bfloat16)
    dspad = padded(ds, (("seq", 0),), 1)
    du = (taps[0] * dspad[2:] + taps[1] * dspad[1:-1] + taps[2] * dspad[:-2]).astype(jnp.bfloat16)
    in_grad = jnp.dot(du, w_in.T, preferred_element_type=jnp.float32).astype(jnp.bfloat16)
    dsf = ds.astype(jnp.float32)
    zf = zpad.astype(jnp.float32)
    local_taps = jnp.stack([jnp.sum(dsf * zf[k : k + tok], axis=0) for k in range(3)])
    taps_grad = lax.psum(local_taps, ("dp", "seq")) * factor
    contract = (((0,), (0,)), ((), ()))
    partial_sum = lax.psum_scatter(
        lax.dot_general(rows, du, contract, preferred_element_type=jnp.float32),
        "dp",
        scatter_dimension=0,
        tiled=True,
    )
    w_grad = lax.psum_scatter(partial_sum, "seq", scatter_dimension=1, tiled=True) * factor
    return (mixed[None], in_grad[None], w_grad, taps_grad)


def solution(mesh):
    return jax.shard_map(
        shards,
        mesh=mesh,
        in_specs=(P("dp", "seq", None), P("dp", "seq", None), P(), P(), P(None, "seq", None)),
        out_specs=(P("dp", "seq", None), P("dp", "seq", None), P("dp", "seq"), P()),
        check_vma=False,
    )
```

profile of v0, /device:TPU:0, one launch (start us, length us, event | category | flops | bytes accessed | tf_op | source)
XLA Modules:
  0.0 388.7 jit_solution(16726972816561263020)
XLA Ops:
  8.4 6.4 %convolution_convert_fusion.2 = bf16[512,3072]{1,0:T(8,128)(2,1)S(1)} fusion(bf16[1024,3072]{1,0:T(8,128)(2,1)} %param.7, bf16[1,512,1024]{2,1,0:T(8,128)(2,1)S(1)} %copy-done), kind=kOutput, calls=%fused_computation.22 | convolution fusion | flops 3222798336 | bytes 10485760 | tf_op jit(solution)/shard_map/dot_general | solution.py:73
  14.9 2.6 collective-permute-start
  18.9 3.9 %collective-permute-done.1 = bf16[1,3072]{1,0:T(2,128)(2,1)S(1)} collective-permute-done((bf16[1,3072]{1,0:T(2,128)(2,1)S(1)}, bf16[1,3072]{1,0:T(2,128)(2,1)S(1)}, u32[]{:S(2)}, u32[]{:S(2)}) %collective-permute-start.1) | collective-permute-done | bytes 6176 | tf_op jit(solution)/shard_map/ppermute | solution.py:21
  22.7 2.5 multiply_add_fusion
  25.3 2.7 copy-done.2
  28.3 1.4 fusion.19
  29.7 2.1 copy.36
  31.8 5.9 %all-to-all-start.2 = ((bf16[1,2,256,1024]{3,1,0,2:T(2,128)(2,1)}), bf16[1,2,256,1024]{3,1,0,2:T(2,128)(2,1)S(1)}, u32[]{:S(2)}, u32[]{:S(2)}) async-start(bf16[1,2,256,1024]{3,1,0,2:T(2,128)(2,1)} %copy.36), calls=%async_computation.2 | async-start | bytes 2097152 | tf_op jit(solution)/shard_map/all_to_all | solution.py:93
  37.8 1.6 reshape.130
  39.4 24.9 %all-to-all-done.2 = bf16[1,2,256,1024]{3,1,0,2:T(2,128)(2,1)S(1)} async-done(((bf16[1,2,256,1024]{3,1,0,2:T(2,128)(2,1)}), bf16[1,2,256,1024]{3,1,0,2:T(2,128)(2,1)S(1)}, u32[]{:S(2)}, u32[]{:S(2)}) %all-to-all-start.2) | async-done | bytes 1048608 | tf_op jit(solution)/shard_map/all_to_all | solution.py:93
  64.7 1.5 copy.50
  66.3 3.8 convolution_convert_fusion
  70.0 1.8 copy.51
  71.9 29.3 %all_to_all.60 = bf16[1,16,32,1024]{3,2,0,1:T(8,128)(2,1)S(1)} all-to-all(bf16[1,16,32,1024]{3,2,0,1:T(8,128)(2,1)S(1)} %bitcast_bitcast_fusion), channel_id=1, replica_groups=mesh['dp'=4,'seq'=8] {'seq'}, dimensions={1} | all-to-all | bytes 2097152 | tf_op jit(solution)/shard_map/all_to_all | solution.py:100
  101.3 1.3 fusion.26
  102.7 2.3 fusion.14
  105.0 2.4 fusion.18
  107.4 3.7 copy.29
  111.0 30.1 %all_to_all.61 = bf16[1,2,256,1024]{3,1,0,2:T(2,128)(2,1)S(1)} all-to-all(bf16[1,2,256,1024]{3,1,0,2:T(2,128)(2,1)} %copy.29), channel_id=1, replica_groups=mesh['dp'=4,'seq'=8] {'seq'}, dimensions={2} | all-to-all | bytes 2097152 | tf_op jit(solution)/shard_map/all_to_all | solution.py:82
  141.5 1.5 copy.48
  143.0 2.9 convolution_convert_fusion.1
  146.0 1.9 copy.49
  147.9 29.0 %all_to_all.62 = bf16[1,16,32,1024]{3,2,0,1:T(8,128)(2,1)S(1)} all-to-all(bf16[1,16,32,1024]{3,2,0,1:T(8,128)(2,1)S(1)} %bitcast_bitcast_fusion.1), channel_id=1, replica_groups=mesh['dp'=4,'seq'=8] {'seq'}, dimensions={1} | all-to-all | bytes 2097152 | tf_op jit(solution)/shard_map/all_to_all | solution.py:89
  177.1 1.3 fusion.24
  178.4 3.2 fusion.13
  183.2 3.0 collective-permute-start.3
  187.1 12.4 %convolution_bitcast_fusion.2 = f32[1024,3072]{0,1:T(8,128)} fusion(bf16[1,512,1024]{2,1,0:T(8,128)(2,1)S(1)} %copy-done, bf16[1,3072]{1,0:T(2,128)(2,1)S(1)} %collective-permute-done.3, bf16[512,1024]{1,0:T(8,128)(2,1)S(1)} %copy-done.6, bf16[512,1024]{1,0:T(8,128)(2,1)S(1)} %get-tuple-element.26, bf16[512,1024]{1,0:T(8,128)(2,1)S(1)} %copy-done.5, ...), kind=kOutput, calls=%fused_computation.14 | convolution fusion | flops 3265265664 | bytes 16826368 | tf_op jit(solution)/shard_map/dot_general | solution.py:115
  199.5 121.5 %reduce-scatter.3.cloned.1.call-done = f32[256,3072]{0,1:T(8,128)} async-done(((f32[1024,3072]{0,1:T(8,128)}), f32[256,3072]{0,1:T(8,128)}) %reduce-scatter.3.cloned.1.call-update) | async-done | bytes 3145744 | tf_op jit(solution)/shard_map/reduce_scatter | solution.py:114
  321.1 2.9 maximum_convert_fusion
  324.0 2.4 fusion.9
  326.5 41.8 %psum.7 = f32[3,3072]{1,0:T(4,128)S(1)} all-reduce(f32[3,3072]{1,0:T(4,128)S(1)} %pad_maximum_fusion.9), channel_id=1, replica_groups=mesh['dp'=4,'seq'=8] {'dp','seq'}, use_global_device_ids=true, to_apply=%region_5.6 | all-reduce | flops 9216 | bytes 73728 | tf_op jit(solution)/shard_map/psum | solution.py:112
  368.9 11.0 %fusion.17 = bf16[1,512,1024]{2,1,0:T(8,128)(2,1)} fusion(bf16[1024,3072]{1,0:T(8,128)(2,1)} %param.7, bf16[1,3072]{1,0:T(2,128)(2,1)S(1)} %collective-permute-done.3, bf16[512,1024]{1,0:T(8,128)(2,1)S(1)} %copy-done.6, bf16[512,1024]{1,0:T(8,128)(2,1)} %copy-done.7, bf16[512,1024]{1,0:T(8,128)(2,1)S(1)} %copy-done.5, ...), kind=kOutput, calls=%fused_computation.47 | convolution fusion | flops 3265789952 | bytes 10534912 | tf_op jit(solution)/shard_map/dot_general | solution.py:108
  (59 shorter events, 9.1 us)
Async XLA Ops:
  7.2 1.2 copy-start
  7.2 11.6 %copy-start.12 = (f32[3,3072]{1,0:T(4,128)S(1)}, f32[3,3072]{1,0:T(4,128)}, u32[]{:S(2)}) copy-start(f32[3,3072]{1,0:T(4,128)} %param.8) | copy-start | bytes 110596
  14.8 13.5 %copy-start.4 = (bf16[512,3072]{1,0:T(8,128)(2,1)}, bf16[512,3072]{1,0:T(8,128)(2,1)S(1)}, u32[]{:S(2)}) copy-start(bf16[512,3072]{1,0:T(8,128)(2,1)S(1)} %convolution_convert_fusion.2) | copy-start | bytes 9437188
  14.8 13.1 %copy-start.9 = (bf16[1,512,1024]{2,1,0:T(8,128)(2,1)S(1)}, bf16[1,512,1024]{2,1,0:T(8,128)(2,1)}, u32[]{:S(2)}) copy-start(bf16[1,512,1024]{2,1,0:T(8,128)(2,1)} %param.6) | copy-start | bytes 3145732
  14.9 4.0 %collective-permute-start = (bf16[1,3072]{1,0:T(2,128)(2,1)S(1)}, bf16[1,3072]{1,0:T(2,128)(2,1)S(1)}, u32[]{:S(2)}, u32[]{:S(2)}) collective-permute-start(bf16[1,3072]{1,0:T(2,128)(2,1)S(1)} %get-tuple-element.24), channel_id=1, source_target_pairs={{0,1},{1,2},{2,3},{3,4},{4,5},{5,6},{6,7},{8,9},{9,10},{10,11},{11... | collective-permute-start | bytes 18440 | tf_op jit(solution)/shard_map/ppermute | solution.py:19
  17.5 5.3 %collective-permute-start.1 = (bf16[1,3072]{1,0:T(2,128)(2,1)S(1)}, bf16[1,3072]{1,0:T(2,128)(2,1)S(1)}, u32[]{:S(2)}, u32[]{:S(2)}) collective-permute-start(bf16[1,3072]{1,0:T(2,128)(2,1)S(1)} %get-tuple-element.25), channel_id=1, source_target_pairs={{1,0},{2,1},{3,2},{4,3},{5,4},{6,5},{7,6},{9,8},{10,9},{11,10},{12... | collective-permute-start | bytes 18440 | tf_op jit(solution)/shard_map/ppermute | solution.py:21
  25.3 2.7 copy-start.2
  27.9 9.8 %copy-start.11 = (bf16[16,32,1024]{2,1,0:T(8,128)(2,1)S(1)}, bf16[16,32,1024]{2,1,0:T(8,128)(2,1)}, u32[]{:S(2)}) copy-start(bf16[16,32,1024]{2,1,0:T(8,128)(2,1)} %param.9) | copy-start | bytes 3145732
  31.8 32.5 %all-to-all-start.2 = ((bf16[1,2,256,1024]{3,1,0,2:T(2,128)(2,1)}), bf16[1,2,256,1024]{3,1,0,2:T(2,128)(2,1)S(1)}, u32[]{:S(2)}, u32[]{:S(2)}) async-start(bf16[1,2,256,1024]{3,1,0,2:T(2,128)(2,1)} %copy.36), calls=%async_computation.2 | async-start | bytes 2097152 | tf_op jit(solution)/shard_map/all_to_all | solution.py:93
  37.7 283.3 %reduce-scatter.3.cloned.1.call-start = ((), (), s32[]{:S(2)}) async-start(), calls=%async_computation.6 | async-start | bytes 15728640 | tf_op jit(solution)/shard_map/reduce_scatter | solution.py:114
  66.3 36.4 %slice-start = ((s8[6291456]{0:T(1024)(128)(4,1)}), s8[2097152]{0:T(1024)(128)(4,1)S(1)}, s32[]{:S(2)}) async-start(s8[6291456]{0:T(1024)(128)(4,1)} %bitcast.140), calls=%async_computation.8 | async-start | bytes 4194304
  71.8 30.8 %slice-start.1 = ((s8[6291456]{0:T(1024)(128)(4,1)}), s8[4194304]{0:T(1024)(128)(4,1)S(1)}, s32[]{:S(2)}) async-start(s8[6291456]{0:T(1024)(128)(4,1)} %bitcast.140), calls=%async_computation.9 | async-start | bytes 8388608
  105.0 38.0 %copy-start.3 = (f32[1,16,32768]{2,1,0:T(8,128)S(1)}, f32[1,16,32768]{2,1,0:T(8,128)}, u32[]{:S(2)}) copy-start(f32[1,16,32768]{2,1,0:T(8,128)} %reshape.130) | copy-start | bytes 6291460
  146.0 32.5 %copy-start.10 = (bf16[1,512,1024]{2,1,0:T(8,128)(2,1)S(1)}, bf16[1,512,1024]{2,1,0:T(8,128)(2,1)}, u32[]{:S(2)}) copy-start(bf16[1,512,1024]{2,1,0:T(8,128)(2,1)} %param.6) | copy-start | bytes 3145732
  177.0 4.7 %copy-start.5 = (bf16[512,1024]{1,0:T(8,128)(2,1)S(1)}, bf16[512,1024]{1,0:T(8,128)(2,1)}, u32[]{:S(2)}) copy-start(bf16[512,1024]{1,0:T(8,128)(2,1)} %get-tuple-element.19) | copy-start | bytes 3145732
  177.0 4.7 %copy-start.6 = (bf16[512,1024]{1,0:T(8,128)(2,1)S(1)}, bf16[512,1024]{1,0:T(8,128)(2,1)}, u32[]{:S(2)}) copy-start(bf16[512,1024]{1,0:T(8,128)(2,1)} %get-tuple-element.20) | copy-start | bytes 3145732
  181.6 5.5 %copy-start.7 = (bf16[512,1024]{1,0:T(8,128)(2,1)}, bf16[512,1024]{1,0:T(8,128)(2,1)S(1)}, u32[]{:S(2)}) copy-start(bf16[512,1024]{1,0:T(8,128)(2,1)S(1)} %get-tuple-element.26) | copy-start | bytes 3145732
  181.9 4.3 %collective-permute-start.2 = (bf16[1,3072]{1,0:T(2,128)(2,1)S(1)}, bf16[1,3072]{1,0:T(2,128)(2,1)S(1)}, u32[]{:S(2)}, u32[]{:S(2)}) collective-permute-start(bf16[1,3072]{1,0:T(2,128)(2,1)S(1)} %get-tuple-element.22), channel_id=1, source_target_pairs={{1,0},{2,1},{3,2},{4,3},{5,4},{6,5},{7,6},{9,8},{10,9},{11,10},{12... | collective-permute-start | bytes 18440 | tf_op jit(solution)/shard_map/ppermute | solution.py:21
  183.2 3.9 collective-permute-start.3
  199.5 180.4 %reduce-scatter.5.cloned.1.call-start = ((), (), s32[]{:S(2)}) async-start(), calls=%async_computation.7 | async-start | bytes 3538944 | tf_op jit(solution)/shard_map/reduce_scatter | solution.py:120
  321.1 2.9 copy-start.8
  368.9 13.0 %copy-start.1 = (bf16[1,512,1024]{2,1,0:T(8,128)(2,1)S(1)}, bf16[1,512,1024]{2,1,0:T(8,128)(2,1)}, u32[]{:S(2)}) copy-start(bf16[1,512,1024]{2,1,0:T(8,128)(2,1)} %param.5) | copy-start | bytes 3145732
Sparse Core Ops, SparseCore 0:
  199.6 121.4 reduce-scatter.2
  323.4 41.3 reduce-scatter.4
where the time goes:
time: 389 us
  waiting for transfers between devices  151 us (39%)
  blocking collectives  130 us (33%)
  matrix products  43 us (11%)
  local copies, waits for them, and re-layouts  20.1 us (5%)
  other arithmetic  15.6 us (4%)
  between operations  14.4 us (4%)
  starting transfers between devices  14.2 us (4%)
    reduce_scatter x1, waiting for transfers between devices, shards(): lax.psum_scatter(lax.dot_general(rows, du, contract, preferred_element_ty...  122 us
    psum x1, blocking collectives, shards(): taps_grad = lax.psum(local_taps, ('dp', 'seq')) * factor  41.8 us
    all_to_all x1, blocking collectives, shards(): lax.all_to_all(block_section(w.reshape(1, nblocks, BLK, width), table_q),...  30.1 us
    all_to_all x1, blocking collectives, shards(): lax.all_to_all(span_section(grad_cols, filt, table_p), 'seq', split_axis=...  29.3 us
    all_to_all x1, blocking collectives, shards(): lax.all_to_all(span_section(columns, filt, table_p), 'seq', split_axis=1,...  29 us
    all_to_all x1, waiting for transfers between devices, shards(): lax.all_to_all(block_section(e4.reshape(1, nblocks, BLK, width), table_q)...  24.9 us
    dot_general x1, matrix products, shards(): lax.dot_general(rows, du, contract, preferred_element_type=jnp.float32)  12.4 us
    unnamed x35, local copies, waits for them, and re-layouts  11.6 us
  transfers between devices with their start and end apart: 7, of which 4 were waited for; matrix products, arithmetic and copies ran while one was open for 5% of the time, Pallas kernels for 0%

commit v1 on v0

v1 whole, which is shorter than its diff:
```python
import functools
import math

import jax
import jax.numpy as jnp
from jax import lax
from jax.experimental import pallas as pl
from jax.experimental.pallas import tpu as pltpu
from jax.sharding import Mesh
from jax.sharding import PartitionSpec as P

BLK = 256
BF = jnp.bfloat16
F32 = jnp.float32
PARAMS = dict(vmem_limit_bytes=48 * 1024 * 1024)


def dct_table(count):
    rows = jnp.arange(count, dtype=jnp.float32)[:, None]
    cols = jnp.arange(count, dtype=jnp.float32)[None, :]
    first = jnp.where(rows == 0, jnp.float32(math.sqrt(0.5)), jnp.float32(1.0))
    table = (
        jnp.float32(math.sqrt(2.0 / count))
        * first
        * jnp.cos(jnp.float32(math.pi) * (cols + 0.5) * rows / count)
    )
    return table.astype(jnp.bfloat16)


def dot(left, right):
    return jnp.dot(left, right, preferred_element_type=F32)


def dot_nt(left, right):
    return lax.dot_general(left, right, (((1,), (1,)), ((), ())), preferred_element_type=F32)


def neighbours(cells, before, after):
    count = cells.shape[0]
    row = lax.broadcasted_iota(jnp.int32, cells.shape, 0)
    earlier = jnp.where(row == 0, before, pltpu.roll(cells, 1, 0))
    later = jnp.where(row == count - 1, after, pltpu.roll(cells, count - 1, 0))
    return earlier, later


def short_conv(cells, edge, taps):
    earlier, later = neighbours(cells, edge[0:1], edge[1:2])
    return taps[0:1] * earlier + taps[1:2] * cells + taps[2:3] * later


def put_blocks(table, cells, out_ref):
    owners, blocks, each = out_ref.shape[0], out_ref.shape[1], out_ref.shape[2]
    for p in range(blocks):
        h = dot(table, cells[p * BLK : (p + 1) * BLK])
        if each % 16 == 0:
            h = h.astype(BF)
        for k in range(owners):
            out_ref[k, p] = h[k * each : (k + 1) * each].astype(BF)


def take_block(ref, p):
    owners, each, width = ref.shape[0], ref.shape[2], ref.shape[3]
    h = ref[:, p]
    if each % 16:
        return h.astype(F32).reshape(owners * each, width).astype(BF)
    return h.reshape(owners * each, width)


def grad_block_kernel(x_ref, xh_ref, w_ref, taps_ref, og_ref, tq_ref, h_ref, z_ref, zh_ref):
    z = dot(x_ref[...], w_ref[...]).astype(BF)
    zh = dot(xh_ref[...], w_ref[...]).astype(BF)
    z_ref[...] = z
    zh_ref[...] = zh
    g = short_conv(z.astype(F32), zh.astype(F32), taps_ref[...])
    e4 = (og_ref[...].astype(F32) * g).astype(BF)
    put_blocks(tq_ref[...], e4, h_ref)


def value_block_kernel(
    x_ref, xh_ref, wa_ref, wv_ref, ta_ref, tv_ref, tq_ref, h_ref, za_ref, zv_ref, zha_ref, zhv_ref
):
    parts = []
    for w_ref, t_ref, z_ref, zh_ref in (
        (wa_ref, ta_ref, za_ref, zha_ref),
        (wv_ref, tv_ref, zv_ref, zhv_ref),
    ):
        z = dot(x_ref[...], w_ref[...]).astype(BF)
        zh = dot(xh_ref[...], w_ref[...]).astype(BF)
        z_ref[...] = z
        zh_ref[...] = zh
        parts.append(short_conv(z.astype(F32), zh.astype(F32), t_ref[...]))
    put_blocks(tq_ref[...], (parts[0] * parts[1]).astype(BF), h_ref)


def span_kernel(h_ref, filt_ref, k_ref, kt_ref, out_ref):
    span, group, width = h_ref.shape
    h, filt = h_ref[...], filt_ref[...]
    if group % 16:
        h = h.astype(F32)
    second = dot(k_ref[...], h.reshape(span * group, width).astype(BF))
    scaled = (filt.astype(F32).reshape(span * group, width) * second).astype(BF)
    third = dot(kt_ref[...], scaled)
    if group % 16 == 0:
        third = third.astype(BF)
    out_ref[...] = third.reshape(span, group, width).astype(BF)


def tap_sums(ds, z, zh, out_ref):
    dsf = ds.astype(F32)
    zf = z.astype(F32)
    zhf = zh.astype(F32)
    earlier, later = neighbours(zf, zhf[0:1], zhf[1:2])
    out_ref[0:1] = jnp.sum(dsf * earlier, axis=0, keepdims=True)
    out_ref[1:2] = jnp.sum(dsf * zf, axis=0, keepdims=True)
    out_ref[2:3] = jnp.sum(dsf * later, axis=0, keepdims=True)


def inverse(h_ref, tqt_ref):
    blocks = h_ref.shape[1]
    return jnp.concatenate([dot(tqt_ref[...], take_block(h_ref, p)) for p in range(blocks)], axis=0)


def emit(ds, z_ref, zh_ref, ds_ref, edge_ref, sums_ref):
    tok = ds.shape[0]
    ds_ref[...] = ds
    dsf = ds.astype(F32)
    edge_ref[...] = jnp.concatenate([dsf[0:1], dsf[tok - 1 : tok]], axis=0).astype(BF)
    tap_sums(ds, z_ref[...], zh_ref[...], sums_ref)


def grad_out_kernel(
    h_ref, tqt_ref, za_ref, zv_ref, zha_ref, zhv_ref, ta_ref, tv_ref,
    dsa_ref, dsv_ref, ea_ref, ev_ref, sa_ref, sv_ref,
):
    dw = inverse(h_ref, tqt_ref)
    v = short_conv(zv_ref[...].astype(F32), zhv_ref[...].astype(F32), tv_ref[...])
    emit((dw * v).astype(BF), za_ref, zha_ref, dsa_ref, ea_ref, sa_ref)
    a = short_conv(za_ref[...].astype(F32), zha_ref[...].astype(F32), ta_ref[...])
    emit((dw * a).astype(BF), zv_ref, zhv_ref, dsv_ref, ev_ref, sv_ref)


def value_out_kernel(
    h_ref, tqt_ref, zg_ref, zhg_ref, tg_ref, og_ref, mixed_ref, dsg_ref, eg_ref, sg_ref
):
    h4 = inverse(h_ref, tqt_ref)
    g = short_conv(zg_ref[...].astype(F32), zhg_ref[...].astype(F32), tg_ref[...])
    mixed_ref[...] = (g * h4).astype(BF)
    emit((og_ref[...].astype(F32) * h4).astype(BF), zg_ref, zhg_ref, dsg_ref, eg_ref, sg_ref)


def du_of(ds_ref, dh_ref, taps_ref):
    ds = ds_ref[...].astype(F32)
    dh = dh_ref[...].astype(F32)
    taps = taps_ref[...]
    earlier, later = neighbours(ds, dh[0:1], dh[1:2])
    return (taps[0:1] * later + taps[1:2] * ds + taps[2:3] * earlier).astype(BF)


def du_first_kernel(
    dsa_ref, dsv_ref, dha_ref, dhv_ref, ta_ref, tv_ref, wa_ref, wv_ref, dua_ref, duv_ref, acc_ref
):
    dua = du_of(dsa_ref, dha_ref, ta_ref)
    duv = du_of(dsv_ref, dhv_ref, tv_ref)
    dua_ref[...] = dua
    duv_ref[...] = duv
    part = dot_nt(dua, wa_ref[...]) + dot_nt(duv, wv_ref[...])

    @pl.when(pl.program_id(0) == 0)
    def _():
        acc_ref[...] = part

    @pl.when(pl.program_id(0) > 0)
    def _():
        acc_ref[...] += part


def du_last_kernel(dsg_ref, dhg_ref, tg_ref, wg_ref, first_ref, dug_ref, out_ref, acc_ref):
    dug = du_of(dsg_ref, dhg_ref, tg_ref)
    dug_ref[...] = dug
    part = dot_nt(dug, wg_ref[...])

    @pl.when(pl.program_id(0) == 0)
    def _():
        acc_ref[...] = first_ref[...] + part

    @pl.when(pl.program_id(0) > 0)
    def _():
        acc_ref[...] += part

    @pl.when(pl.program_id(0) == pl.num_programs(0) - 1)
    def _():
        out_ref[...] = acc_ref[...].astype(BF)


def w_grad_kernel(xo_ref, xp_ref, do_ref, dp_ref, out_ref):
    part = dot(xo_ref[...], do_ref[...]) + dot(xp_ref[...], dp_ref[...])
    out_ref[...] = part.astype(BF).reshape(out_ref.shape)


def shards(inputs, out_grad, w_in, taps, filt):
    tok, width = inputs.shape[1], inputs.shape[2]
    ndp, nz, ncore = lax.axis_size("dp"), lax.axis_size("z"), lax.axis_size("core")
    nseq = nz * ncore
    span, each = filt.shape[0], filt.shape[1]
    nblocks = tok // BLK
    seq = ("z", "core")
    core = lax.axis_index("core")
    factor = 1.0 / math.sqrt(ndp * nseq * tok)
    cb = 256
    ncb = width // cb
    tq = dct_table(BLK)
    tp = dct_table(span)
    group = math.gcd(each, 16)
    kron = jnp.kron(tp, jnp.eye(group, dtype=BF))
    x = inputs[0]
    og = out_grad[0]

    fwd = [(i, i + 1) for i in range(nseq - 1)]
    bwd = [(i + 1, i) for i in range(nseq - 1)]

    def halo(first, last):
        return lax.ppermute(last, seq, fwd), lax.ppermute(first, seq, bwd)

    before, after = halo(x[0:1], x[tok - 1 : tok])
    xh = jnp.concatenate([before, after, jnp.zeros((14, width), BF)], axis=0)

    def S(shape, dtype=BF):
        return jax.ShapeDtypeStruct(shape, dtype)

    full = lambda *shape: pl.BlockSpec(shape, lambda j: (0,) * len(shape))
    col = lambda rows, off=0: pl.BlockSpec((rows, cb), lambda j: (0, off * ncb + j))
    chunk = pl.BlockSpec((nseq, nblocks, each, cb), lambda j: (0, 0, 0, j))
    hshape = S((nseq, nblocks, each, width))

    def call(kernel, name, ins, in_specs, outs, out_specs, flops, scratch=(), grid=None):
        moved = sum(a.size * a.dtype.itemsize for a in (*ins, *outs))
        return pl.pallas_call(
            kernel,
            out_shape=outs,
            grid=grid or (ncb,),
            in_specs=in_specs,
            out_specs=out_specs,
            scratch_shapes=scratch,
            compiler_params=pltpu.CompilerParams(**PARAMS),
            cost_estimate=pl.CostEstimate(flops=flops, bytes_accessed=moved, transcendentals=0),
            name=name,
        )(*ins)

    mm = 2 * tok * width * width
    he, zg, zhg = call(
        grad_block_kernel, "grad_block",
        (x, xh, w_in, taps, og, tq),
        [full(tok, width), full(16, width), col(width, 1), col(3, 1), col(tok), full(BLK, BLK)],
        (hshape, S((tok, width)), S((16, width))),
        (chunk, col(tok), col(16)),
        mm + mm // 4,
    )
    hw, za, zv, zha, zhv = call(
        value_block_kernel, "value_block",
        (x, xh, w_in, w_in, taps, taps, tq),
        [full(tok, width), full(16, width), col(width, 0), col(width, 2), col(3, 0), col(3, 2), full(BLK, BLK)],
        (hshape, S((tok, width)), S((tok, width)), S((16, width)), S((16, width))),
        (chunk, col(tok), col(tok), col(16), col(16)),
        2 * mm + mm // 4,
    )

    def swap(h):
        return lax.all_to_all(h, seq, 0, 0, tiled=True)

    def span_step(h):
        wide = 512
        block = pl.BlockSpec((span, group, wide), lambda i, j: (0, i, j))
        table = pl.BlockSpec(kron.shape, lambda i, j: (0, 0))
        out = call(
            span_kernel, "span",
            (h.reshape(span, each, width), filt, kron, kron.T),
            [block, block, table, table],
            (S((span, each, width)),),
            (block,),
            mm // 2,
            grid=(each // group, width // wide),
        )
        return out[0].reshape(h.shape)

    ce = swap(he)
    cw = swap(hw)
    be = swap(span_step(ce))
    bw = swap(span_step(cw))

    tqt = tq.T
    dsa, dsv, ea, ev, sa, sv = call(
        grad_out_kernel, "grad_out",
        (be, tqt, za, zv, zha, zhv, taps, taps),
        [chunk, full(BLK, BLK), col(tok), col(tok), col(16), col(16), col(3, 0), col(3, 2)],
        (S((tok, width)), S((tok, width)), S((2, width)), S((2, width)), S((3, width), F32), S((3, width), F32)),
        (col(tok), col(tok), col(2), col(2), col(3), col(3)),
        mm // 4,
    )

    def edges(*parts):
        both = jnp.concatenate(parts, axis=1)
        before, after = halo(both[0:1], both[1:2])
        return jnp.concatenate([before, after], axis=0)

    dh = edges(ea, ev)
    dua, duv, acc = call(
        du_first_kernel, "du_first",
        (dsa, dsv, dh, dh, taps, taps, w_in, w_in),
        [col(tok), col(tok), col(2, 0), col(2, 1), col(3, 0), col(3, 2), col(width, 0), col(width, 2)],
        (S((tok, width)), S((tok, width)), S((tok, width), F32)),
        (col(tok), col(tok), full(tok, width)),
        2 * mm,
    )

    half = width // ndp // ncore
    xt = x.T.reshape(ndp, ncore, half, tok)
    pick = lambda c: lax.dynamic_index_in_dim(xt, c, 1, keepdims=False).reshape(ndp * half, tok)
    flip = [(0, 1), (1, 0)]
    xo = pick(core)
    xp = lax.ppermute(pick(1 - core), "core", flip)
    rows = ndp * half

    def w_grad(du):
        other = lax.ppermute(du, "core", flip)
        part = call(
            w_grad_kernel, "w_grad",
            (xo, xp, du, other),
            [full(rows, tok), full(rows, tok), col(tok), col(tok)],
            (S((ndp, half, width)),),
            (pl.BlockSpec((ndp, half, cb), lambda j: (0, 0, j)),),
            mm,
        )[0]
        got = lax.all_to_all(part, "dp", 0, 0, tiled=True)
        return jnp.sum(got.astype(F32), axis=0).astype(BF)

    def all_sum(value):
        for axis, count in (("core", ncore), ("z", nz), ("dp", ndp)):
            step = 1
            while step < count:
                value = value + lax.ppermute(value, axis, [(i, i ^ step) for i in range(count)])
                step *= 2
        return value

    wa, wv = w_grad(dua), w_grad(duv)
    t_av = all_sum(jnp.concatenate([sa, sv], axis=0))

    mixed, dsg, eg, sg = call(
        value_out_kernel, "value_out",
        (bw, tqt, zg, zhg, taps, og),
        [chunk, full(BLK, BLK), col(tok), col(16), col(3, 1), col(tok)],
        (S((tok, width)), S((tok, width)), S((2, width)), S((3, width), F32)),
        (col(tok), col(tok), col(2), col(3)),
        mm // 4,
    )
    dhg = edges(eg)
    dug, in_grad = call(
        du_last_kernel, "du_last",
        (dsg, dhg, taps, w_in, acc),
        [col(tok), col(2), col(3, 1), col(width, 1), full(tok, width)],
        (S((tok, width)), S((tok, width))),
        (col(tok), full(tok, width)),
        mm,
        scratch=[pltpu.VMEM((tok, width), F32)],
    )
    wg = w_grad(dug)
    t_g = all_sum(sg)
    taps_grad = jnp.concatenate([t_av[0:3], t_g, t_av[3:6]], axis=1) * factor

    own = 3 * width // nseq
    wide = jnp.concatenate([wa, wg, wv], axis=1).reshape(half, nseq, own).transpose(1, 0, 2)
    got = lax.all_to_all(wide, seq, 0, 0, tiled=True).reshape(nz, ncore * half, own)
    w_in_grad = jnp.sum(got.astype(F32), axis=0) * factor
    return (mixed[None], in_grad[None], w_in_grad, taps_grad)


def solution(mesh):
    ndp, nseq = mesh.shape["dp"], mesh.shape["seq"]
    split = Mesh(mesh.devices.reshape(ndp, nseq // 2, 2), ("dp", "z", "core"))
    seq = ("z", "core")
    return jax.shard_map(
        shards,
        mesh=split,
        in_specs=(P("dp", seq, None), P("dp", seq, None), P(), P(), P(None, seq, None)),
        out_specs=(P("dp", seq, None), P("dp", seq, None), P("dp", seq), P()),
        check_vma=False,
    )
```

time: 389 us -> 279 us (0.72)
  blocking collectives: 130 us -> 0 us
  starting transfers between devices: 14.2 us -> 77.9 us
  Pallas kernels: 0 us -> 52.3 us
  matrix products: 43 us -> 0 us
  waiting for transfers between devices: 151 us -> 110 us
  between operations: 14.4 us -> 1.07 us
  local copies, waits for them, and re-layouts: 20.1 us -> 28.5 us
  other arithmetic: 15.6 us -> 8.04 us
    reduce_scatter x2 -> x0, waiting for transfers between devices: 122 us -> none  [the longest x1 122 us: shards(): lax.psum_scatter(lax.dot_general(rows, du, contract, preferred_element_ty...]
    all_to_all x3 -> x0, blocking collectives: 88.3 us -> none  [the longest x1 30.1 us: shards(): lax.all_to_all(block_section(w.reshape(1, nblocks, BLK, width), table_q),...]
    all_to_all x1 -> x8, waiting for transfers between devices: 24.9 us -> 85.6 us  [the longest x4 56.8 us: swap(): return lax.all_to_all(h, seq, 0, 0, tiled=True)]
    pallas_call x0 -> x11, Pallas kernels: none -> 52.3 us  [call(): pl.pallas_call(kernel, out_shape=outs, grid=grid or (ncb,), in_specs=in_s...]
    dot_general x9 -> x0, matrix products: 43 us -> none  [the longest x1 12.4 us: shards(): lax.dot_general(rows, du, contract, preferred_element_type=jnp.float32)]
    psum x1 -> x0, blocking collectives: 41.8 us -> none  [shards(): taps_grad = lax.psum(local_taps, ('dp', 'seq')) * factor]
    ppermute x4 -> x20, starting transfers between devices: 8.24 us -> 41.4 us  [the longest x3 14.8 us: w_grad(): other = lax.ppermute(du, 'core', flip)]
    all_to_all x1 -> x8, starting transfers between devices: 5.91 us -> 36.5 us  [the longest x4 18.2 us: swap(): return lax.all_to_all(h, seq, 0, 0, tiled=True)]
  transfers between devices with their start and end apart: 7 -> 28, of which waited for: 4 -> 16; matrix products, arithmetic and copies ran while one was open for 5% -> 7% of each run, Pallas kernels for 0% -> 17%
where the time goes in v1:
time: 279 us; the launch traced here: 278 us
  waiting for transfers between devices  110 us (39%)
  starting transfers between devices  77.9 us (28%)
  Pallas kernels  52.3 us (19%)
  local copies, waits for them, and re-layouts  28.5 us (10%)
  other arithmetic  8.04 us (3%)
    all_to_all x4, waiting for transfers between devices, swap(): return lax.all_to_all(h, seq, 0, 0, tiled=True)  56.8 us
    pallas_call x11, Pallas kernels, call(): pl.pallas_call(kernel, out_shape=outs, grid=grid or (ncb,), in_specs=in_s...  52.3 us
    all_to_all x3, waiting for transfers between devices, w_grad(): got = lax.all_to_all(part, 'dp', 0, 0, tiled=True)  28.8 us
    ppermute x10, waiting for transfers between devices, all_sum(): lax.ppermute(value, axis, [(i, i ^ step) for i in range(count)])  22.6 us
    all_to_all x4, starting transfers between devices, swap(): return lax.all_to_all(h, seq, 0, 0, tiled=True)  18.2 us
    unnamed x47, local copies, waits for them, and re-layouts  16.9 us
    ppermute x3, starting transfers between devices, w_grad(): other = lax.ppermute(du, 'core', flip)  14.8 us
    ppermute x10, starting transfers between devices, all_sum(): lax.ppermute(value, axis, [(i, i ^ step) for i in range(count)])  13.4 us
  transfers between devices with their start and end apart: 28, of which 16 were waited for; matrix products, arithmetic and copies ran while one was open for 7% of the time, Pallas kernels for 17%

profile of v1, /device:TPU:0, one launch (start us, length us, event | category | flops | bytes accessed | tf_op | source)
XLA Modules:
  0.0 277.5 jit_solution(3330535293880017170)
XLA Ops:
  2.7 3.0 %collective-permute-start = (bf16[1,1024]{1,0:T(2,128)(2,1)S(1)}, bf16[1,1024]{1,0:T(2,128)(2,1)S(1)}, u32[]{:S(2)}, u32[]{:S(2)}) collective-permute-start(bf16[1,1024]{1,0:T(2,128)(2,1)S(1)} %get-tuple-element.52), channel_id=1, source_target_pairs={{0,1},{1,2},{2,3},{3,4},{4,5},{5,6},{6,7},{8,9},{9,10},{10,11},{11... | collective-permute-start | bytes 6152 | tf_op jit(solution)/shard_map/ppermute | solution.py:222
  11.2 5.8 %grad_block.1 = (bf16[8,2,32,1024]{3,2,1,0:T(8,128)(2,1)}, bf16[512,1024]{1,0:T(8,128)(2,1)S(1)}, bf16[16,1024]{1,0:T(8,128)(2,1)S(1)}) custom-call(bf16[512,1024]{1,0:T(8,128)(2,1)S(1)} %bitcast.29, bf16[16,1024]{1,0:T(8,128)(2,1)S(1)} %maximum_maximum_fusion.xh_ref, bf16[1024,3072]{1,0:T(8,128)(2,1)} %wg_ref.1, f32[3,3072]{1,0:T(4,128)S(1)} %copy-done.6, ...), custom_call_target="tpu_custom_call" | custom-call | flops 1342177280 | bytes 10719232 | tf_op jit(solution)/shard_map/grad_block/pallas_call | solution.py:237
  17.9 6.9 %all-to-all-start.2 = ((bf16[8,2,32,1024]{3,2,1,0:T(8,128)(2,1)}), bf16[8,2,32,1024]{3,2,1,0:T(8,128)(2,1)S(1)}, u32[]{:S(2)}, u32[]{:S(2)}) async-start(bf16[8,2,32,1024]{3,2,1,0:T(8,128)(2,1)} %get-tuple-element.33), calls=%async_computation.2 | async-start | bytes 2097152 | tf_op jit(solution)/shard_map/all_to_all | solution.py:268
  24.8 7.1 %value_block.1 = (bf16[8,2,32,1024]{3,2,1,0:T(8,128)(2,1)}, bf16[512,1024]{1,0:T(8,128)(2,1)S(1)}, bf16[512,1024]{1,0:T(8,128)(2,1)S(1)}, bf16[16,1024]{1,0:T(8,128)(2,1)S(1)}, bf16[16,1024]{1,0:T(8,128)(2,1)S(1)}) custom-call(bf16[512,1024]{1,0:T(8,128)(2,1)S(1)} %bitcast.30, bf16[16,1024]{1,0:T(8,128)(2,1)S(1)} %maximum_maximum_fusion.xh_ref, ...), custom_call_target="tpu_custom_call" | custom-call | flops 2415919104 | bytes 17080320 | tf_op jit(solution)/shard_map/value_block/pallas_call | solution.py:237
  34.5 16.9 %all-to-all-done.2 = bf16[8,2,32,1024]{3,2,1,0:T(8,128)(2,1)S(1)} async-done(((bf16[8,2,32,1024]{3,2,1,0:T(8,128)(2,1)}), bf16[8,2,32,1024]{3,2,1,0:T(8,128)(2,1)S(1)}, u32[]{:S(2)}, u32[]{:S(2)}) %all-to-all-start.2) | async-done | bytes 1048608 | tf_op jit(solution)/shard_map/all_to_all | solution.py:268
  51.4 4.2 %all-to-all-start = ((bf16[8,2,32,1024]{3,2,1,0:T(8,128)(2,1)}), bf16[8,2,32,1024]{3,2,1,0:T(8,128)(2,1)}, u32[]{:S(2)}, u32[]{:S(2)}) async-start(bf16[8,2,32,1024]{3,2,1,0:T(8,128)(2,1)} %get-tuple-element.27), calls=%async_computation | async-start | bytes 2097152 | tf_op jit(solution)/shard_map/all_to_all | solution.py:268
  63.7 18.5 %all-to-all-done = bf16[8,2,32,1024]{3,2,1,0:T(8,128)(2,1)} async-done(((bf16[8,2,32,1024]{3,2,1,0:T(8,128)(2,1)}), bf16[8,2,32,1024]{3,2,1,0:T(8,128)(2,1)}, u32[]{:S(2)}, u32[]{:S(2)}) %all-to-all-start) | async-done | bytes 1048608 | tf_op jit(solution)/shard_map/all_to_all | solution.py:268
  82.2 3.6 %all-to-all-start.3 = ((bf16[8,2,32,1024]{3,2,1,0:T(8,128)(2,1)}), bf16[8,2,32,1024]{3,2,1,0:T(8,128)(2,1)S(1)}, u32[]{:S(2)}, u32[]{:S(2)}) async-start(bf16[8,2,32,1024]{3,2,1,0:T(8,128)(2,1)} %bitcast.36), calls=%async_computation.3 | async-start | bytes 2097152 | tf_op jit(solution)/shard_map/all_to_all | solution.py:268
  86.7 4.2 %span.2 = bf16[16,32,1024]{2,1,0:T(8,128)(2,1)} custom-call(bf16[16,32,1024]{2,1,0:T(8,128)(2,1)} %bitcast.3.h_ref, bf16[16,32,1024]{2,1,0:T(8,128)(2,1)S(1)} %copy-done.2, bf16[256,256]{1,0:T(8,128)(2,1)S(1)} %copy-done.10, bf16[256,256]{1,0:T(8,128)(2,1)S(1)} %bitcast.40), custom_call_target="tpu_custom_call" | custom-call | flops 536870912 | bytes 3407872 | tf_op jit(solution)/shard_map/span/pallas_call | solution.py:237
  90.9 21.4 %all-to-all-done.3.h_ref = bf16[8,2,32,1024]{3,2,1,0:T(8,128)(2,1)S(1)} async-done(((bf16[8,2,32,1024]{3,2,1,0:T(8,128)(2,1)}), bf16[8,2,32,1024]{3,2,1,0:T(8,128)(2,1)S(1)}, u32[]{:S(2)}, u32[]{:S(2)}) %all-to-all-start.3) | async-done | bytes 1048608 | tf_op jit(solution)/shard_map/all_to_all | solution.py:268
  112.3 3.6 %all-to-all-start.1 = ((bf16[8,2,32,1024]{3,2,1,0:T(8,128)(2,1)}), bf16[8,2,32,1024]{3,2,1,0:T(8,128)(2,1)S(1)}, u32[]{:S(2)}, u32[]{:S(2)}) async-start(bf16[8,2,32,1024]{3,2,1,0:T(8,128)(2,1)} %bitcast.5), calls=%async_computation.1 | async-start | bytes 2097152 | tf_op jit(solution)/shard_map/all_to_all | solution.py:268
  118.3 4.1 %grad_out.1 = (bf16[512,1024]{1,0:T(8,128)(2,1)S(1)}, bf16[512,1024]{1,0:T(8,128)(2,1)S(1)}, bf16[2,1024]{1,0:T(2,128)(2,1)S(1)}, bf16[2,1024]{1,0:T(2,128)(2,1)...) custom-call(bf16[8,2,32,1024]{3,2,1,0:T(8,128)(2,1)S(1)} %all-to-all-done.3.h_ref, ...), custom_call_target="tpu_custom_call" | custom-call | flops 268435456 | bytes 5545984 | tf_op jit(solution)/shard_map/grad_out/pallas_call | solution.py:237
  123.8 3.0 %collective-permute-start.4 = (bf16[1,2048]{1,0:T(2,128)(2,1)S(1)}, bf16[1,2048]{1,0:T(2,128)(2,1)S(1)}, u32[]{:S(2)}, u32[]{:S(2)}) collective-permute-start(bf16[1,2048]{1,0:T(2,128)(2,1)S(1)} %get-tuple-element.56), channel_id=1, source_target_pairs={{0,1},{1,2},{2,3},{3,4},{4,5},{5,6},{6,7},{8,9},{9,10},{10,11},{11... | collective-permute-start | bytes 12296 | tf_op jit(solution)/shard_map/ppermute | solution.py:222
  127.7 7.1 %du_first.1 = (bf16[512,1024]{1,0:T(8,128)(2,1)S(1)}, bf16[512,1024]{1,0:T(8,128)(2,1)}, f32[512,1024]{1,0:T(8,128)}) custom-call(bf16[512,1024]{1,0:T(8,128)(2,1)S(1)} %get-tuple-element.38.dsa_ref, bf16[512,1024]{1,0:T(8,128)(2,1)S(1)} %get-tuple-element.39.dsv_ref, bf16[2,2048]{1,0:T(2,128)(2,1)S(1)} %pad_maximum_fusion.2.dha_ref.dhv_ref, ...), custom_call_target="tpu_custom_call" | custom-call | flops 2147483648 | bytes 18964480 | tf_op jit(solution)/shard_map/du_first/pallas_call | solution.py:237
  134.8 6.2 %collective-permute-start.9 = (bf16[512,1024]{1,0:T(8,128)(2,1)}, bf16[512,1024]{1,0:T(8,128)(2,1)}, u32[]{:S(2)}, u32[]{:S(2)}) collective-permute-start(bf16[512,1024]{1,0:T(8,128)(2,1)} %get-tuple-element.46.do_ref), channel_id=1, source_target_pairs={{0,1},{1,0},{2,3},{3,2},{4,5},{5,4},{6,7},{7,6},{8,9},{9,8},{10,11... | collective-permute-start | bytes 3145736 | tf_op jit(solution)/shard_map/ppermute | solution.py:324
  142.5 4.7 %constant_dynamic-slice_fusion = (bf16[4,1,128,512]{2,1,0,3:T(2,128)(2,1)S(1)}, bf16[4,1,128,512]{2,1,0,3:T(2,128)(2,1)}) fusion(bf16[4,2,128,512]{2,1,0,3:T(2,128)(2,1)} %reshape.124, s32[]{:T(128)S(6)} %select_n.38, s32[]{:T(128)S(6)} %select_n.37), kind=kLoop, calls=%fused_computation.23 | loop fusion | bytes 2097160 | tf_op jit(solution)/shard_map/jit(dynamic_index_in_dim)/dynamic_slice | solution.py:317
  150.8 3.2 %value_out.1 = (bf16[512,1024]{1,0:T(8,128)(2,1)}, bf16[512,1024]{1,0:T(8,128)(2,1)S(1)}, bf16[2,1024]{1,0:T(2,128)(2,1)S(1)}, f32[3,1024]{1,0:T(4,128)S(1)}) custom-call(bf16[8,2,32,1024]{3,2,1,0:T(8,128)(2,1)S(1)} %all-to-all-done.1.h_ref, bf16[256,256]{1,0:T(8,128)(2,1)S(1)} %get-tuple-element.60.tqt_ref, bf16[512,1024]{1,0:T(8,128)(2,1)S(1)} %copy-done.12, ...), custom_call_target="tpu_custom_call" | custom-call | flops 268435456 | bytes 5459968 | tf_op jit(solution)/shard_map/value_out/pallas_call | solution.py:237
  159.4 5.6 %du_last.1 = (bf16[512,1024]{1,0:T(8,128)(2,1)S(1)}, bf16[512,1024]{1,0:T(8,128)(2,1)}) custom-call(bf16[512,1024]{1,0:T(8,128)(2,1)S(1)} %get-tuple-element.31.dsg_ref, bf16[2,1024]{1,0:T(2,128)(2,1)S(1)} %pad_maximum_fusion.3.dhg_ref, f32[3,3072]{1,0:T(4,128)S(1)} %copy-done.7, bf16[1024,3072]{1,0:T(8,128)(2,1)} %wg_ref.1, f32[512,1024]{1,0:T(8,128)S(1)} %copy-done.8), custom_call_target="tpu_custom_call" | custom-call | flops 1073741824 | bytes 11575296 | tf_op jit(solution)/shard_map/du_last/pallas_call | solution.py:237
  165.1 8.5 %collective-permute-start.8 = (bf16[512,1024]{1,0:T(8,128)(2,1)S(1)}, bf16[512,1024]{1,0:T(8,128)(2,1)}, u32[]{:S(2)}, u32[]{:S(2)}) collective-permute-start(bf16[512,1024]{1,0:T(8,128)(2,1)S(1)} %get-tuple-element.45.do_ref), channel_id=1, source_target_pairs={{0,1},{1,0},{2,3},{3,2},{4,5},{5,4},{6,7},{7,6},{8,9},{9,8},{10,11... | collective-permute-start | bytes 3145736 | tf_op jit(solution)/shard_map/ppermute | solution.py:324
  175.0 4.5 %w_grad.5 = bf16[4,128,1024]{2,1,0:T(8,128)(2,1)} custom-call(bf16[512,512]{1,0:T(8,128)(2,1)S(1)} %bitcast.32, bf16[512,512]{1,0:T(8,128)(2,1)S(1)} %collective-permute-done.6.xp_ref, bf16[512,1024]{1,0:T(8,128)(2,1)} %get-tuple-element.46.do_ref, bf16[512,1024]{1,0:T(8,128)(2,1)} %collective-permute-done.9.dp_ref), custom_call_target="tpu_custom_call" | custom-call | flops 1073741824 | bytes 4194304 | tf_op jit(solution)/shard_map/w_grad/pallas_call | solution.py:237
  179.4 4.4 %all-to-all-start.6 = ((bf16[4,128,1024]{2,1,0:T(8,128)(2,1)}), bf16[4,128,1024]{2,1,0:T(8,128)(2,1)}, u32[]{:S(2)}, u32[]{:S(2)}) async-start(bf16[4,128,1024]{2,1,0:T(8,128)(2,1)} %w_grad.5), calls=%async_computation.6 | async-start | bytes 2097152 | tf_op jit(solution)/shard_map/all_to_all | solution.py:333
  183.9 4.4 %w_grad.4 = bf16[4,128,1024]{2,1,0:T(8,128)(2,1)} custom-call(bf16[512,512]{1,0:T(8,128)(2,1)S(1)} %bitcast.33, bf16[512,512]{1,0:T(8,128)(2,1)S(1)} %collective-permute-done.6.xp_ref, bf16[512,1024]{1,0:T(8,128)(2,1)S(1)} %get-tuple-element.45.do_ref, bf16[512,1024]{1,0:T(8,128)(2,1)} %collective-permute-done.8.dp_ref), custom_call_target="tpu_custom_call" | custom-call | flops 1073741824 | bytes 4194304 | tf_op jit(solution)/shard_map/w_grad/pallas_call | solution.py:237
  188.3 9.7 %all-to-all-done.6 = bf16[4,128,1024]{2,1,0:T(8,128)(2,1)} async-done(((bf16[4,128,1024]{2,1,0:T(8,128)(2,1)}), bf16[4,128,1024]{2,1,0:T(8,128)(2,1)}, u32[]{:S(2)}, u32[]{:S(2)}) %all-to-all-start.6) | async-done | bytes 1048608 | tf_op jit(solution)/shard_map/all_to_all | solution.py:333
  198.0 4.3 %all-to-all-start.5 = ((bf16[4,128,1024]{2,1,0:T(8,128)(2,1)}), bf16[4,128,1024]{2,1,0:T(8,128)(2,1)}, u32[]{:S(2)}, u32[]{:S(2)}) async-start(bf16[4,128,1024]{2,1,0:T(8,128)(2,1)} %w_grad.4), calls=%async_computation.5 | async-start | bytes 2097152 | tf_op jit(solution)/shard_map/all_to_all | solution.py:333
  202.3 4.3 %w_grad.3 = bf16[4,128,1024]{2,1,0:T(8,128)(2,1)} custom-call(bf16[512,512]{1,0:T(8,128)(2,1)S(1)} %bitcast.34, bf16[512,512]{1,0:T(8,128)(2,1)S(1)} %collective-permute-done.6.xp_ref, bf16[512,1024]{1,0:T(8,128)(2,1)S(1)} %copy-done.18, bf16[512,1024]{1,0:T(8,128)(2,1)} %collective-permute-done.7.dp_ref), custom_call_target="tpu_custom_call" | custom-call | flops 1073741824 | bytes 4194304 | tf_op jit(solution)/shard_map/w_grad/pallas_call | solution.py:237
  206.6 8.9 %all-to-all-done.5 = bf16[4,128,1024]{2,1,0:T(8,128)(2,1)} async-done(((bf16[4,128,1024]{2,1,0:T(8,128)(2,1)}), bf16[4,128,1024]{2,1,0:T(8,128)(2,1)}, u32[]{:S(2)}, u32[]{:S(2)}) %all-to-all-start.5) | async-done | bytes 1048608 | tf_op jit(solution)/shard_map/all_to_all | solution.py:333
  215.5 3.5 %all-to-all-start.4 = ((bf16[4,128,1024]{2,1,0:T(8,128)(2,1)}), bf16[4,128,1024]{2,1,0:T(8,128)(2,1)S(1)}, u32[]{:S(2)}, u32[]{:S(2)}) async-start(bf16[4,128,1024]{2,1,0:T(8,128)(2,1)} %w_grad.3), calls=%async_computation.4 | async-start | bytes 2097152 | tf_op jit(solution)/shard_map/all_to_all | solution.py:333
  221.9 10.2 %all-to-all-done.4 = bf16[4,128,1024]{2,1,0:T(8,128)(2,1)S(1)} async-done(((bf16[4,128,1024]{2,1,0:T(8,128)(2,1)}), bf16[4,128,1024]{2,1,0:T(8,128)(2,1)S(1)}, u32[]{:S(2)}, u32[]{:S(2)}) %all-to-all-start.4) | async-done | bytes 1048608 | tf_op jit(solution)/shard_map/all_to_all | solution.py:333
  233.5 6.1 %all-to-all-start.7 = ((bf16[8,128,384]{1,2,0:T(8,128)(2,1)}), bf16[8,128,384]{1,2,0:T(8,128)(2,1)S(1)}, u32[]{:S(2)}, u32[]{:S(2)}) async-start(bf16[8,128,384]{1,2,0:T(8,128)(2,1)} %bitcast.15), calls=%async_computation.7 | async-start | bytes 1572864 | tf_op jit(solution)/shard_map/all_to_all | solution.py:371
  243.0 11.1 %collective-permute-done.11 = f32[6,1024]{1,0:T(8,128)S(1)} collective-permute-done((f32[6,1024]{1,0:T(8,128)S(1)}, f32[6,1024]{1,0:T(8,128)S(1)}, u32[]{:S(2)}, u32[]{:S(2)}) %collective-permute-start.11) | collective-permute-done | bytes 24608 | tf_op jit(solution)/shard_map/ppermute | solution.py:340
  254.1 4.5 %collective-permute-start.12 = (f32[6,1024]{1,0:T(8,128)S(1)}, f32[6,1024]{1,0:T(8,128)S(1)}, u32[]{:S(2)}, u32[]{:S(2)}) collective-permute-start(f32[6,1024]{1,0:T(8,128)S(1)} %add.73), channel_id=1, source_target_pairs={{0,4},{2,6},{4,0},{6,2},{1,5},{3,7},{5,1},{7,3},{8,12},{10,14},{12... | collective-permute-start | bytes 73736 | tf_op jit(solution)/shard_map/ppermute | solution.py:340
  265.0 3.3 %collective-permute-done.17 = f32[3,1024]{1,0:T(4,128)S(1)} collective-permute-done((f32[3,1024]{1,0:T(4,128)S(1)}, f32[3,1024]{1,0:T(4,128)S(1)}, u32[]{:S(2)}, u32[]{:S(2)}) %collective-permute-start.17) | collective-permute-done | bytes 12320 | tf_op jit(solution)/shard_map/ppermute | solution.py:340
  (122 shorter events, 59.7 us)
Async XLA Ops:
  1.4 6.4 %collective-permute-start.1 = (bf16[1,1024]{1,0:T(2,128)(2,1)S(1)}, bf16[1,1024]{1,0:T(2,128)(2,1)S(1)}, u32[]{:S(2)}, u32[]{:S(2)}) collective-permute-start(bf16[1,1024]{1,0:T(2,128)(2,1)S(1)} %get-tuple-element.53), channel_id=1, source_target_pairs={{1,0},{2,1},{3,2},{4,3},{5,4},{6,5},{7,6},{9,8},{10,9},{11,10},{12... | collective-permute-start | bytes 6152 | tf_op jit(solution)/shard_map/ppermute | solution.py:222
  2.7 5.2 %collective-permute-start = (bf16[1,1024]{1,0:T(2,128)(2,1)S(1)}, bf16[1,1024]{1,0:T(2,128)(2,1)S(1)}, u32[]{:S(2)}, u32[]{:S(2)}) collective-permute-start(bf16[1,1024]{1,0:T(2,128)(2,1)S(1)} %get-tuple-element.52), channel_id=1, source_target_pairs={{0,1},{1,2},{2,3},{3,4},{4,5},{5,6},{6,7},{8,9},{9,10},{10,11},{11... | collective-permute-start | bytes 6152 | tf_op jit(solution)/shard_map/ppermute | solution.py:222
  17.9 33.5 %all-to-all-start.2 = ((bf16[8,2,32,1024]{3,2,1,0:T(8,128)(2,1)}), bf16[8,2,32,1024]{3,2,1,0:T(8,128)(2,1)S(1)}, u32[]{:S(2)}, u32[]{:S(2)}) async-start(bf16[8,2,32,1024]{3,2,1,0:T(8,128)(2,1)} %get-tuple-element.33), calls=%async_computation.2 | async-start | bytes 2097152 | tf_op jit(solution)/shard_map/all_to_all | solution.py:268
  51.4 30.8 %all-to-all-start = ((bf16[8,2,32,1024]{3,2,1,0:T(8,128)(2,1)}), bf16[8,2,32,1024]{3,2,1,0:T(8,128)(2,1)}, u32[]{:S(2)}, u32[]{:S(2)}) async-start(bf16[8,2,32,1024]{3,2,1,0:T(8,128)(2,1)} %get-tuple-element.27), calls=%async_computation | async-start | bytes 2097152 | tf_op jit(solution)/shard_map/all_to_all | solution.py:268
  82.2 30.1 %all-to-all-start.3 = ((bf16[8,2,32,1024]{3,2,1,0:T(8,128)(2,1)}), bf16[8,2,32,1024]{3,2,1,0:T(8,128)(2,1)S(1)}, u32[]{:S(2)}, u32[]{:S(2)}) async-start(bf16[8,2,32,1024]{3,2,1,0:T(8,128)(2,1)} %bitcast.36), calls=%async_computation.3 | async-start | bytes 2097152 | tf_op jit(solution)/shard_map/all_to_all | solution.py:268
  90.9 25.0 %copy-start.20 = (bf16[16,1024]{1,0:T(8,128)(2,1)S(1)}, bf16[16,1024]{1,0:T(8,128)(2,1)}, u32[]{:S(2)}) copy-start(bf16[16,1024]{1,0:T(8,128)(2,1)} %copy-done.19) | copy-start | bytes 98308
  112.3 37.3 %all-to-all-start.1 = ((bf16[8,2,32,1024]{3,2,1,0:T(8,128)(2,1)}), bf16[8,2,32,1024]{3,2,1,0:T(8,128)(2,1)S(1)}, u32[]{:S(2)}, u32[]{:S(2)}) async-start(bf16[8,2,32,1024]{3,2,1,0:T(8,128)(2,1)} %bitcast.5), calls=%async_computation.1 | async-start | bytes 2097152 | tf_op jit(solution)/shard_map/all_to_all | solution.py:268
  122.5 4.3 %collective-permute-start.5 = (bf16[1,2048]{1,0:T(2,128)(2,1)S(1)}, bf16[1,2048]{1,0:T(2,128)(2,1)S(1)}, u32[]{:S(2)}, u32[]{:S(2)}) collective-permute-start(bf16[1,2048]{1,0:T(2,128)(2,1)S(1)} %get-tuple-element.57), channel_id=1, source_target_pairs={{1,0},{2,1},{3,2},{4,3},{5,4},{6,5},{7,6},{9,8},{10,9},{11,10},{12... | collective-permute-start | bytes 12296 | tf_op jit(solution)/shard_map/ppermute | solution.py:222
  123.8 3.8 %collective-permute-start.4 = (bf16[1,2048]{1,0:T(2,128)(2,1)S(1)}, bf16[1,2048]{1,0:T(2,128)(2,1)S(1)}, u32[]{:S(2)}, u32[]{:S(2)}) collective-permute-start(bf16[1,2048]{1,0:T(2,128)(2,1)S(1)} %get-tuple-element.56), channel_id=1, source_target_pairs={{0,1},{1,2},{2,3},{3,4},{4,5},{5,6},{6,7},{8,9},{9,10},{10,11},{11... | collective-permute-start | bytes 12296 | tf_op jit(solution)/shard_map/ppermute | solution.py:222
  134.8 7.7 %copy-start.17 = (bf16[512,1024]{1,0:T(8,128)(2,1)}, bf16[512,1024]{1,0:T(8,128)(2,1)S(1)}, u32[]{:S(2)}) copy-start(bf16[512,1024]{1,0:T(8,128)(2,1)S(1)} %get-tuple-element.44.do_ref) | copy-start | bytes 3145732
  134.8 40.1 %collective-permute-start.9 = (bf16[512,1024]{1,0:T(8,128)(2,1)}, bf16[512,1024]{1,0:T(8,128)(2,1)}, u32[]{:S(2)}, u32[]{:S(2)}) collective-permute-start(bf16[512,1024]{1,0:T(8,128)(2,1)} %get-tuple-element.46.do_ref), channel_id=1, source_target_pairs={{0,1},{1,0},{2,3},{3,2},{4,5},{5,4},{6,7},{7,6},{8,9},{9,8},{10,11... | collective-permute-start | bytes 3145736 | tf_op jit(solution)/shard_map/ppermute | solution.py:324
  149.6 25.4 %collective-permute-start.6 = (bf16[512,512]{1,0:T(8,128)(2,1)}, bf16[512,512]{1,0:T(8,128)(2,1)S(1)}, u32[]{:S(2)}, u32[]{:S(2)}) collective-permute-start(bf16[512,512]{1,0:T(8,128)(2,1)} %bitcast.42), channel_id=1, source_target_pairs={{0,1},{1,0},{2,3},{3,2},{4,5},{5,4},{6,7},{7,6},{8,9},{9,8},{10,11... | collective-permute-start | bytes 1572872 | tf_op jit(solution)/shard_map/ppermute | solution.py:320
  150.8 8.6 %copy-start.8 = (f32[512,1024]{1,0:T(8,128)S(1)}, f32[512,1024]{1,0:T(8,128)}, u32[]{:S(2)}) copy-start(f32[512,1024]{1,0:T(8,128)} %get-tuple-element.42.first_ref) | copy-start | bytes 6291460
  154.1 4.5 %collective-permute-start.3 = (bf16[1,1024]{1,0:T(2,128)(2,1)S(1)}, bf16[1,1024]{1,0:T(2,128)(2,1)S(1)}, u32[]{:S(2)}, u32[]{:S(2)}) collective-permute-start(bf16[1,1024]{1,0:T(2,128)(2,1)S(1)} %get-tuple-element.59), channel_id=1, source_target_pairs={{1,0},{2,1},{3,2},{4,3},{5,4},{6,5},{7,6},{9,8},{10,9},{11,10},{12... | collective-permute-start | bytes 6152 | tf_op jit(solution)/shard_map/ppermute | solution.py:222
  155.6 3.8 %collective-permute-start.2 = (bf16[1,1024]{1,0:T(2,128)(2,1)S(1)}, bf16[1,1024]{1,0:T(2,128)(2,1)S(1)}, u32[]{:S(2)}, u32[]{:S(2)}) collective-permute-start(bf16[1,1024]{1,0:T(2,128)(2,1)S(1)} %get-tuple-element.58), channel_id=1, source_target_pairs={{0,1},{1,2},{2,3},{3,4},{4,5},{5,6},{6,7},{8,9},{9,10},{10,11},{11... | collective-permute-start | bytes 6152 | tf_op jit(solution)/shard_map/ppermute | solution.py:222
  159.4 14.2 %copy-start.21 = (bf16[4,1,128,512]{2,1,0,3:T(2,128)(2,1)S(1)}, bf16[4,1,128,512]{2,1,0,3:T(2,128)(2,1)}, u32[]{:S(2)}) copy-start(bf16[4,1,128,512]{2,1,0,3:T(2,128)(2,1)} %get-tuple-element.51) | copy-start | bytes 1572868
  165.1 18.8 %collective-permute-start.8 = (bf16[512,1024]{1,0:T(8,128)(2,1)S(1)}, bf16[512,1024]{1,0:T(8,128)(2,1)}, u32[]{:S(2)}, u32[]{:S(2)}) collective-permute-start(bf16[512,1024]{1,0:T(8,128)(2,1)S(1)} %get-tuple-element.45.do_ref), channel_id=1, source_target_pairs={{0,1},{1,0},{2,3},{3,2},{4,5},{5,4},{6,7},{7,6},{8,9},{9,8},{10,11... | collective-permute-start | bytes 3145736 | tf_op jit(solution)/shard_map/ppermute | solution.py:324
  179.4 18.5 %all-to-all-start.6 = ((bf16[4,128,1024]{2,1,0:T(8,128)(2,1)}), bf16[4,128,1024]{2,1,0:T(8,128)(2,1)}, u32[]{:S(2)}, u32[]{:S(2)}) async-start(bf16[4,128,1024]{2,1,0:T(8,128)(2,1)} %w_grad.5), calls=%async_computation.6 | async-start | bytes 2097152 | tf_op jit(solution)/shard_map/all_to_all | solution.py:333
  183.8 18.4 %collective-permute-start.7 = (bf16[512,1024]{1,0:T(8,128)(2,1)S(1)}, bf16[512,1024]{1,0:T(8,128)(2,1)}, u32[]{:S(2)}, u32[]{:S(2)}) collective-permute-start(bf16[512,1024]{1,0:T(8,128)(2,1)S(1)} %copy-done.18), channel_id=1, source_target_pairs={{0,1},{1,0},{2,3},{3,2},{4,5},{5,4},{6,7},{7,6},{8,9},{9,8},{10,11... | collective-permute-start | bytes 3145736 | tf_op jit(solution)/shard_map/ppermute | solution.py:324
  198.0 17.6 %all-to-all-start.5 = ((bf16[4,128,1024]{2,1,0:T(8,128)(2,1)}), bf16[4,128,1024]{2,1,0:T(8,128)(2,1)}, u32[]{:S(2)}, u32[]{:S(2)}) async-start(bf16[4,128,1024]{2,1,0:T(8,128)(2,1)} %w_grad.4), calls=%async_computation.5 | async-start | bytes 2097152 | tf_op jit(solution)/shard_map/all_to_all | solution.py:333
  215.5 16.6 %all-to-all-start.4 = ((bf16[4,128,1024]{2,1,0:T(8,128)(2,1)}), bf16[4,128,1024]{2,1,0:T(8,128)(2,1)S(1)}, u32[]{:S(2)}, u32[]{:S(2)}) async-start(bf16[4,128,1024]{2,1,0:T(8,128)(2,1)} %w_grad.3), calls=%async_computation.4 | async-start | bytes 2097152 | tf_op jit(solution)/shard_map/all_to_all | solution.py:333
  233.5 42.9 %all-to-all-start.7 = ((bf16[8,128,384]{1,2,0:T(8,128)(2,1)}), bf16[8,128,384]{1,2,0:T(8,128)(2,1)S(1)}, u32[]{:S(2)}, u32[]{:S(2)}) async-start(bf16[8,128,384]{1,2,0:T(8,128)(2,1)} %bitcast.15), calls=%async_computation.7 | async-start | bytes 1572864 | tf_op jit(solution)/shard_map/all_to_all | solution.py:371
  239.7 1.4 collective-permute-start.10
  241.1 13.0 %collective-permute-start.11 = (f32[6,1024]{1,0:T(8,128)S(1)}, f32[6,1024]{1,0:T(8,128)S(1)}, u32[]{:S(2)}, u32[]{:S(2)}) collective-permute-start(f32[6,1024]{1,0:T(8,128)S(1)} %fusion.3), channel_id=1, source_target_pairs={{0,2},{2,0},{4,6},{6,4},{1,3},{3,1},{5,7},{7,5},{8,10},{10,8},{12,... | collective-permute-start | bytes 73736 | tf_op jit(solution)/shard_map/ppermute | solution.py:340
  254.1 7.9 %collective-permute-start.12 = (f32[6,1024]{1,0:T(8,128)S(1)}, f32[6,1024]{1,0:T(8,128)S(1)}, u32[]{:S(2)}, u32[]{:S(2)}) collective-permute-start(f32[6,1024]{1,0:T(8,128)S(1)} %add.73), channel_id=1, source_target_pairs={{0,4},{2,6},{4,0},{6,2},{1,5},{3,7},{5,1},{7,3},{8,12},{10,14},{12... | collective-permute-start | bytes 73736 | tf_op jit(solution)/shard_map/ppermute | solution.py:340
  258.7 1.2 collective-permute-start.15
  259.8 3.7 %collective-permute-start.16 = (f32[3,1024]{1,0:T(4,128)S(1)}, f32[3,1024]{1,0:T(4,128)S(1)}, u32[]{:S(2)}, u32[]{:S(2)}) collective-permute-start(f32[3,1024]{1,0:T(4,128)S(1)} %add.77), channel_id=1, source_target_pairs={{0,2},{2,0},{4,6},{6,4},{1,3},{3,1},{5,7},{7,5},{8,10},{10,8},{12,... | collective-permute-start | bytes 36872 | tf_op jit(solution)/shard_map/ppermute | solution.py:340
  262.0 7.6 %collective-permute-start.13 = (f32[6,1024]{1,0:T(8,128)S(1)}, f32[6,1024]{1,0:T(8,128)S(1)}, u32[]{:S(2)}, u32[]{:S(2)}) collective-permute-start(f32[6,1024]{1,0:T(8,128)S(1)} %add.74), channel_id=1, source_target_pairs={{0,8},{8,0},{16,24},{24,16},{1,9},{9,1},{17,25},{25,17},{2,10},{10... | collective-permute-start | bytes 73736 | tf_op jit(solution)/shard_map/ppermute | solution.py:340
  263.6 4.6 %collective-permute-start.17 = (f32[3,1024]{1,0:T(4,128)S(1)}, f32[3,1024]{1,0:T(4,128)S(1)}, u32[]{:S(2)}, u32[]{:S(2)}) collective-permute-start(f32[3,1024]{1,0:T(4,128)S(1)} %add.78), channel_id=1, source_target_pairs={{0,4},{2,6},{4,0},{6,2},{1,5},{3,7},{5,1},{7,3},{8,12},{10,14},{12... | collective-permute-start | bytes 36872 | tf_op jit(solution)/shard_map/ppermute | solution.py:340
  268.2 3.7 %collective-permute-start.18 = (f32[3,1024]{1,0:T(4,128)S(1)}, f32[3,1024]{1,0:T(4,128)S(1)}, u32[]{:S(2)}, u32[]{:S(2)}) collective-permute-start(f32[3,1024]{1,0:T(4,128)S(1)} %add.79), channel_id=1, source_target_pairs={{0,8},{8,0},{16,24},{24,16},{1,9},{9,1},{17,25},{25,17},{2,10},{10... | collective-permute-start | bytes 36872 | tf_op jit(solution)/shard_map/ppermute | solution.py:340
  269.7 6.1 %collective-permute-start.14 = (f32[6,1024]{1,0:T(8,128)S(1)}, f32[6,1024]{1,0:T(8,128)S(1)}, u32[]{:S(2)}, u32[]{:S(2)}) collective-permute-start(f32[6,1024]{1,0:T(8,128)S(1)} %add.75), channel_id=1, source_target_pairs={{0,16},{8,24},{16,0},{24,8},{1,17},{9,25},{17,1},{25,9},{2,18},{10... | collective-permute-start | bytes 73736 | tf_op jit(solution)/shard_map/ppermute | solution.py:340
  272.0 3.7 %collective-permute-start.19 = (f32[3,1024]{1,0:T(4,128)S(1)}, f32[3,1024]{1,0:T(4,128)S(1)}, u32[]{:S(2)}, u32[]{:S(2)}) collective-permute-start(f32[3,1024]{1,0:T(4,128)S(1)} %add.80), channel_id=1, source_target_pairs={{0,16},{8,24},{16,0},{24,8},{1,17},{9,25},{17,1},{25,9},{2,18},{10... | collective-permute-start | bytes 36872 | tf_op jit(solution)/shard_map/ppermute | solution.py:340
  (18 other events, 38.0 us)

commit v2 on v0

v2 whole, which is shorter than its diff:
```python
import functools
import math

import jax
import jax.numpy as jnp
import numpy as np
from jax import lax
from jax.experimental import pallas as pl
from jax.experimental.pallas import tpu as pltpu
from jax.sharding import Mesh
from jax.sharding import PartitionSpec as P

BLK = 256
BF = jnp.bfloat16
EDGE = 16
NW = 2
SHADE = 1000
AV_DONE = 3
E_WHOLE, W_WHOLE, AV_WHOLE, G_WHOLE = False, False, False, False
F32 = jnp.float32
PARAMS = dict(vmem_limit_bytes=48 * 1024 * 1024)


def dct_table(count):
    one = np.float32
    rows = np.arange(count, dtype=np.float32)[:, None]
    cols = np.arange(count, dtype=np.float32)[None, :]
    first = np.where(rows == 0, one(math.sqrt(0.5)), one(1.0))
    table = one(math.sqrt(2.0 / count)) * first * np.cos(one(math.pi) * (cols + one(0.5)) * rows / one(count))
    return table.astype(BF)


def dot(left, right):
    return jnp.dot(left, right, preferred_element_type=F32)


def dot_nt(left, right):
    return lax.dot_general(left, right, (((1,), (1,)), ((), ())), preferred_element_type=F32)


def neighbours(cells, before, after):
    count = cells.shape[0]
    row = lax.broadcasted_iota(jnp.int32, cells.shape, 0)
    earlier = jnp.where(row == 0, before, pltpu.roll(cells, 1, 0))
    later = jnp.where(row == count - 1, after, pltpu.roll(cells, count - 1, 0))
    return earlier, later


def short_conv(cells, edge, taps):
    earlier, later = neighbours(cells, edge[0:1], edge[1:2])
    return taps[0:1] * earlier + taps[1:2] * cells + taps[2:3] * later


def lanes(width):
    step = min(width, 256)
    return [(at, pl.ds(at, step)) for at in range(0, width, step)]


def mine(off, width, at, step):
    start = lax.axis_index("core") * width + (off + at)
    return pl.ds(pl.multiple_of(start, 128), step)


def part_of(core, size):
    if isinstance(core, int):
        return pl.ds(core * size, size)
    return pl.ds(pl.multiple_of(core * size, size), size)


def ordered(first, second):
    swap = lax.axis_index("core") == 1
    return jnp.where(swap, second, first), jnp.where(swap, first, second)


def pieces(refs, axis):
    size = lax.axis_size(axis)
    if len(refs) == 1:
        return [(k, refs[0].at[k]) for k in range(size)]
    return [(lax.axis_index(axis) ^ k, ref) for k, ref in enumerate(refs)]


def pack_kernel(x_ref, og_ref, ends_ref, send_ref):
    core, tok, width = lax.axis_index("core"), x_ref.shape[0], send_ref.shape[1]
    x_head, x_tail = x_ref[0:16, :].astype(F32)[0:2], x_ref[tok - 16 : tok, :].astype(F32)[14:16]
    g_head, g_tail = og_ref[0:16, :].astype(F32)[0:1], og_ref[tok - 16 : tok, :].astype(F32)[15:16]
    first = core == 0
    rows = [jnp.where(first, x_head, x_tail), jnp.where(first, g_head, g_tail)]
    rows.append(jnp.zeros((EDGE - 3, x_ref.shape[1]), F32))
    ends_ref[...] = jnp.concatenate(rows, axis=0).astype(BF)
    send_ref[...] = og_ref[:, part_of(1 - core, width)]


def edge_rows(first_ref, second_ref):
    before, after = ordered(first_ref[...].astype(F32), second_ref[...].astype(F32))
    pad = jnp.zeros((EDGE - 4, before.shape[1]), F32)
    return jnp.concatenate([before[1:2], after[0:1], before[0:1], after[1:2], pad], axis=0).astype(BF)


def project(x_ref, xs_ref, xh, w, z_ref, zh_ref, here):
    core, tok = lax.axis_index("core"), x_ref.shape[0]
    z_ref[part_of(core, tok), here] = dot(x_ref[...], w).astype(BF)
    z_ref[part_of(1 - core, tok), here] = dot(xs_ref[...], w).astype(BF)
    zh = dot(xh, w).astype(BF)
    zh_ref[:, here] = zh
    return z_ref[:, here].astype(F32), zh.astype(F32)


def put_blocks(table, cells, hold, here):
    for p in range(hold.shape[0]):
        hold[p, :, here] = dot(table, cells[p * BLK : (p + 1) * BLK]).astype(BF)


def hand_rows(hold, outs, cols):
    for there, out in pieces(outs, "z"):
        out[...] = hold[:, part_of(there, out.shape[1]), cols]


def grad_block_kernel(
    n, x_ref, xs_ref, h1_ref, h2_ref, w_ref, taps_ref, og_ref, ogs_ref, tq_ref, *refs
):
    outs, (z_ref, zh_ref, og_all_ref, hold) = refs[:n], refs[n:]
    core, tok = lax.axis_index("core"), x_ref.shape[0]
    width = z_ref.shape[1]
    og_all_ref[part_of(core, tok), :] = og_ref[:, part_of(core, width)]
    og_all_ref[part_of(1 - core, tok), :] = ogs_ref[...]
    xh = edge_rows(h1_ref, h2_ref)
    for at, here in lanes(width):
        cols = mine(2 * width, width, at, here.size)
        z, zh = project(x_ref, xs_ref, xh, w_ref[:, cols], z_ref, zh_ref, here)
        g = short_conv(z, zh, taps_ref[:, cols])
        e4 = (og_all_ref[:, here].astype(F32) * g).astype(BF)
        put_blocks(tq_ref[...], e4, hold, here)
    hand_rows(hold, outs, pl.ds(0, width))


def value_block_kernel(
    n, nw, x_ref, xs_ref, h1_ref, h2_ref, w_ref, taps_ref, tq_ref, after_ref, *refs
):
    outs, (za_ref, zv_ref, zha_ref, zhv_ref, xt_ref, hold) = refs[: n * nw], refs[n * nw :]
    core, tok = lax.axis_index("core"), x_ref.shape[0]
    width = za_ref.shape[1]
    xh = edge_rows(h1_ref, h2_ref)
    for at, here in lanes(width):
        parts = []
        for off, z_ref, zh_ref in ((0, za_ref, zha_ref), (4 * width, zv_ref, zhv_ref)):
            cols = mine(off, width, at, here.size)
            z, zh = project(x_ref, xs_ref, xh, w_ref[:, cols], z_ref, zh_ref, here)
            parts.append(short_conv(z, zh, taps_ref[:, cols]))
        put_blocks(tq_ref[...], (parts[0] * parts[1]).astype(BF), hold, here)
    for i in range(nw):
        hand_rows(hold, outs[i * n : (i + 1) * n], pl.ds(i * (width // nw), width // nw))
    xt_ref[:, part_of(core, tok)] = x_ref[...].T
    xt_ref[:, part_of(1 - core, tok)] = xs_ref[...].T


def span_kernel(n, skip, off, *refs):
    ins, refs = refs[:n], refs[n + skip :]
    (filt_ref, filts_ref, k_ref, kt_ref, tq_ref), outs, (hold, filts) = refs[:5], refs[5 : n + 5], refs[n + 5 :]
    core, place, places = lax.axis_index("core"), lax.axis_index("z"), lax.axis_size("z")
    span, rows, width = hold.shape
    each, blocks = filt_ref.shape[1], span // places
    half = filts_ref.shape[2]
    group = k_ref.shape[0] // span
    for there, ref in pieces(ins, "z"):
        hold[pl.ds(there * blocks, blocks)] = ref[...]
    mine_at = pl.ds(pl.multiple_of(core * half + off, 128), width)
    filts[:, part_of(core, each), :] = filt_ref[:, :, mine_at].astype(filts.dtype)
    filts[:, part_of(1 - core, each), :] = filts_ref[:, :, off : off + width].astype(filts.dtype)
    for _, here in lanes(width):
        for at in range(0, rows, group):
            some = pl.ds(at, group)
            flat = (span * group, here.size)
            second = dot(k_ref[...], hold[:, some, here].reshape(flat))
            scaled = (filts[:, some, here].reshape(flat).astype(F32) * second).astype(BF)
            third = dot(kt_ref[...], scaled).astype(BF)
            hold[:, some, here] = third.reshape(span, group, here.size)
    table = tq_ref[part_of(place, rows), :].astype(F32)
    first_q, last_q = table[:, 0:1], table[:, BLK - 1 : BLK]
    for there, out in pieces(outs, "z"):
        for p in range(blocks):
            out[p * rows : (p + 1) * rows, :] = hold[there * blocks + p]
        sums = []
        for p, column, inside in (
            (there * blocks - 1, last_q, there > 0),
            (there * blocks + blocks, first_q, there < places - 1),
        ):
            cells = hold[jnp.clip(p, 0, span - 1)].astype(F32)
            total = jnp.sum(cells * column, axis=0, keepdims=True)
            sums.append(jnp.where(inside, total, 0.0))
        both = jnp.concatenate(sums, axis=0)
        high = both.astype(BF).astype(F32)
        pad = jnp.zeros((EDGE - 4, width), F32)
        out[blocks * rows :, :] = jnp.concatenate([high, both - high, pad], axis=0).astype(BF)


def take_rows(ins, hold):
    blocks = hold.shape[0]
    rows = hold.shape[1] // lax.axis_size("z")
    for there, ref in pieces(ins, "z"):
        for p in range(blocks):
            hold[p, part_of(there, rows), :] = ref[p * rows : (p + 1) * rows, :]


def inverse(ins, hold, tqt_ref, here):
    cells = jnp.concatenate([dot(tqt_ref[...], hold[p, :, here]) for p in range(hold.shape[0])], axis=0)
    shares = [ref for _, ref in pieces(ins, "z")]
    at = shares[0].shape[0] - EDGE
    edge = shares[0][at : at + EDGE, here].astype(F32)
    for ref in shares[1:]:
        edge = edge + ref[at : at + EDGE, here].astype(F32)
    return cells, edge[0:1] + edge[2:3], edge[1:2] + edge[3:4]


def conv_wide(z, zh, taps):
    count = z.shape[0]
    before = taps[0:1] * zh[2:3] + taps[1:2] * zh[0:1] + taps[2:3] * z[0:1]
    after = taps[0:1] * z[count - 1 : count] + taps[1:2] * zh[1:2] + taps[2:3] * zh[3:4]
    return short_conv(z, zh, taps), before, after


def rounded(value):
    return value.astype(BF).astype(F32)


def emit(cells, gate, z, zh, taps, cols, du_ref, sums_ref):
    ds, before, after = (rounded(one * two) for one, two in zip(cells, gate))
    earlier, later = neighbours(ds, before, after)
    du_ref[:, cols] = (taps[0:1] * later + taps[1:2] * ds + taps[2:3] * earlier).astype(BF)
    earlier, later = neighbours(z, zh[0:1], zh[1:2])
    sums_ref[0:1, cols] = jnp.sum(ds * earlier, axis=0, keepdims=True)
    sums_ref[1:2, cols] = jnp.sum(ds * z, axis=0, keepdims=True)
    sums_ref[2:3, cols] = jnp.sum(ds * later, axis=0, keepdims=True)


def multiply(xt_ref, du_ref, outs, part):
    for _, here in lanes(du_ref.shape[1]):
        part[:, here] = dot(xt_ref[...], du_ref[:, here]).astype(BF)
    rows = part.shape[0] // lax.axis_size("dp")
    for there, out in pieces(outs, "dp"):
        out[0:rows, :] = part[part_of(there, rows), :]


def grad_out_kernel(n, nd, *refs):
    ins, refs = refs[:n], refs[n + 1 :]
    (tqt_ref, za_ref, zv_ref, zha_ref, zhv_ref, taps_ref, xt_ref), refs = refs[:7], refs[7:]
    (du_ref, send_ref, sums_ref), outs, (hold, part) = refs[:3], refs[3 : 3 + nd], refs[3 + nd :]
    width, tok = za_ref.shape[1], send_ref.shape[0]
    take_rows(ins, hold)
    for at, here in lanes(width):
        dw = inverse(ins, hold, tqt_ref, here)
        za, zha = za_ref[:, here].astype(F32), zha_ref[:, here].astype(F32)
        zv, zhv = zv_ref[:, here].astype(F32), zhv_ref[:, here].astype(F32)
        ta = taps_ref[:, mine(0, width, at, here.size)]
        tv = taps_ref[:, mine(4 * width, width, at, here.size)]
        emit(dw, conv_wide(zv, zhv, tv), za, zha, ta, here, du_ref, sums_ref)
        emit(dw, conv_wide(za, zha, ta), zv, zhv, tv, pl.ds(width + at, here.size), du_ref, sums_ref)
    send_ref[...] = du_ref[part_of(1 - lax.axis_index("core"), tok), :]
    multiply(xt_ref, du_ref, outs, part)


def three_parts(value):
    high = rounded(value)
    middle = rounded(value - high)
    return [high, middle, value - high - middle]


def value_out_kernel(n, skip, off, *refs):
    ins, refs = refs[:n], refs[n + skip :]
    (tqt_ref, zg_ref, zhg_ref, taps_ref, og_ref, h1_ref, h2_ref), refs = refs[:7], refs[7:]
    (mo_ref, ms_ref, du_ref, send_ref, sums_ref), (hold, mixed) = refs[:5], refs[5:]
    core, tok, half = lax.axis_index("core"), mo_ref.shape[0], zg_ref.shape[1]
    width = mo_ref.shape[1]
    take_rows(ins, hold)
    for at, here in lanes(width):
        there = pl.ds(off + at, here.size)
        h4 = inverse(ins, hold, tqt_ref, here)
        z, zh = zg_ref[:, there].astype(F32), zhg_ref[:, there].astype(F32)
        cols = mine(2 * half, half, off + at, here.size)
        whole = mine(0, half, off + at, here.size)
        taps = taps_ref[:, cols]
        mixed[:, here] = (short_conv(z, zh, taps) * h4[0]).astype(BF)
        before, after = ordered(h1_ref[:, whole].astype(F32), h2_ref[:, whole].astype(F32))
        og = (og_ref[:, there].astype(F32), before[2:3], after[2:3])
        emit(h4, og, z, zh, taps, here, du_ref, sums_ref)
    mo_ref[...] = mixed[part_of(core, tok), :]
    ms_ref[...] = mixed[part_of(1 - core, tok), :]
    send_ref[...] = du_ref[part_of(1 - core, tok), :]


def w_grad_kernel(skip, known, *refs):
    refs = refs[skip:]
    (xt_ref, du_ref), known, outs, part = refs[:2], refs[2 : 2 + known], refs[2 + known : -1], refs[-1]
    multiply(xt_ref, du_ref, outs, part)
    if known:
        width = du_ref.shape[1]
        av = known[0][...]
        half = av.shape[1] // 2
        every = [av[:, :half], *(ref[...] for ref in known[1:]), av[:, half:]]
        every = jnp.concatenate(every, axis=1)
        lines = []
        for at in range(0, 3 * half, width):
            lines += three_parts(every[:, at : at + width])
        rows = part.shape[0] // lax.axis_size("dp")
        extra = outs[0].shape[-2] - rows
        lines.append(jnp.zeros((extra - 3 * len(lines), width), F32))
        block = jnp.concatenate(lines, axis=0).astype(BF)
        for _, out in pieces(outs, "dp"):
            out[rows : rows + extra, :] = block


def in_part(du_ref, rows, w_ref, columns, width):
    total = None
    for run, start in enumerate(columns):
        w = w_ref[:, pl.ds(pl.multiple_of(start, 128), width)]
        part = dot_nt(du_ref[rows, run * width : (run + 1) * width], w)
        total = part if total is None else total + part
    return total


def in_first_kernel(du_ref, got_ref, w_ref, after_ref, acc_ref):
    core, tok, width = lax.axis_index("core"), got_ref.shape[0], w_ref.shape[1] // 6
    every = pl.ds(0, tok)
    own = in_part(du_ref, part_of(core, tok), w_ref, [core * width, (4 + core) * width], width)
    acc_ref[...] = own + in_part(got_ref, every, w_ref, [(1 - core) * width, (5 - core) * width], width)


def in_last_kernel(nw, *refs):
    dus, gots, owns, others = (refs[i * nw : (i + 1) * nw] for i in range(4))
    w_ref, acc_ref, after_ref, out_ref, mixed_ref = refs[4 * nw :]
    core, half = lax.axis_index("core"), w_ref.shape[1] // 6
    tok, width = gots[0].shape
    total = acc_ref[...]
    for i in range(nw):
        for ref, rows, owner in (
            (dus[i], part_of(core, tok), core),
            (gots[i], pl.ds(0, tok), 1 - core),
        ):
            total = total + in_part(ref, rows, w_ref, [(2 + owner) * half + i * width], width)
        for ref, owner in ((owns[i], core), (others[i], 1 - core)):
            at = pl.multiple_of(owner * half + i * width, 128)
            mixed_ref[:, pl.ds(at, width)] = ref[...]
    out_ref[...] = total.astype(BF)


def add_all(values):
    while len(values) > 1:
        values = [one + two for one, two in zip(values[::2], values[1::2])]
    return values[0]


def fold_kernel(na, n, nw, *refs):
    av, refs = [ref for _, ref in pieces(refs[:na], "dp")], refs[na:]
    gs = [[ref for _, ref in pieces(refs[i * n : (i + 1) * n], "dp")] for i in range(nw)]
    own_ref, send_ref, taps_ref, hold = refs[n * nw :]
    core, width = lax.axis_index("core"), gs[0][0].shape[1]
    half_cols = width * nw
    rows = av[0].shape[0]
    both = add_all([ref[...].astype(F32) for ref in av]).astype(BF)
    hold[:, 0:half_cols] = both[:, :half_cols]
    for i, parts in enumerate(gs):
        at = half_cols + i * width
        hold[:, at : at + width] = add_all([ref[0:rows, :].astype(F32) for ref in parts]).astype(BF)
    hold[:, 2 * half_cols :] = both[:, half_cols:]
    half = own_ref.shape[0]
    own_ref[...] = hold[part_of(core, half), :]
    send_ref[...] = hold[part_of(1 - core, half), :]
    extra = gs[-1][0].shape[0] - rows
    sums = add_all([ref[rows : rows + extra, :].astype(F32) for ref in gs[-1]])
    for group in range(3 * nw):
        at = 9 * group
        value = sums[at : at + 3] + sums[at + 3 : at + 6] + sums[at + 6 : at + 9]
        taps_ref[:, group * width : (group + 1) * width] = value


def spread(own_ref, got_ref, out_ref):
    core, width = lax.axis_index("core"), own_ref.shape[1] // 3
    for run in range(3):
        cols = pl.ds(run * width, width)
        for ref, owner in ((own_ref, core), (got_ref, 1 - core)):
            at = pl.multiple_of((2 * run + owner) * width, 128)
            out_ref[:, pl.ds(at, width)] = ref[:, cols]


def join_kernel(own_ref, got_ref, after_ref, *refs):
    outs, hold = refs[:-1], refs[-1]
    spread(own_ref, got_ref, hold)
    for there, out in pieces(outs, "z"):
        out[...] = hold[:, part_of(there, out.shape[1])]


def sum_kernel(n, *refs):
    ins, (own_ref, send_ref) = refs[:n], refs[n:]
    core, width = lax.axis_index("core"), own_ref.shape[1]
    for out, owner in ((own_ref, core), (send_ref, 1 - core)):
        cols = part_of(owner, width)
        out[...] = add_all([ref[:, cols].astype(F32) for ref in ins])


def last_kernel(factor, own_ref, got_ref, t_own_ref, t_got_ref, out_ref, taps_ref):
    core, rows = lax.axis_index("core"), own_ref.shape[0]
    out_ref[part_of(core, rows), :] = own_ref[...] * factor
    out_ref[part_of(1 - core, rows), :] = got_ref[...] * factor
    spread(t_own_ref, t_got_ref, taps_ref)
    taps_ref[...] = taps_ref[...] * factor


def shards(nw, inputs, out_grad, w_in, taps, filt):
    tok, width = inputs.shape[1], inputs.shape[2]
    ndp, nz, ncore = lax.axis_size("dp"), lax.axis_size("z"), lax.axis_size("core")
    nseq = nz * ncore
    span, each = filt.shape[0], filt.shape[1]
    seq = ("z", "core")
    core = lax.axis_index("core")
    factor = 1.0 / math.sqrt(ndp * nseq * tok)
    wide, count = width // ncore, tok * ncore
    blocks, rows = count // BLK, each * ncore
    group = math.gcd(rows, 16)
    tq, tp = dct_table(BLK), dct_table(span)
    kron = np.kron(tp.astype(np.float32), np.eye(group, dtype=np.float32)).astype(BF)
    tq, tqt, kron, kront = (jnp.asarray(table) for table in (tq, tq.T.copy(), kron, kron.T.copy()))
    x, og = inputs[0], out_grad[0]

    def S(shape, dtype=BF):
        return jax.ShapeDtypeStruct(shape, dtype)

    def call(kernel, name, ins, outs, flops, scratch=(), shade=1):
        moved = sum(a.size * a.dtype.itemsize for a in (*ins, *outs))
        whole = pl.BlockSpec(memory_space=pltpu.VMEM)
        return pl.pallas_call(
            kernel,
            out_shape=outs,
            in_specs=[whole] * len(ins),
            out_specs=[whole] * len(outs),
            scratch_shapes=scratch,
            compiler_params=pltpu.CompilerParams(**PARAMS),
            cost_estimate=pl.CostEstimate(flops=flops // shade, bytes_accessed=moved // shade, transcendentals=0),
            name=name,
        )(*ins)

    def flip(value):
        return lax.ppermute(value, "core", [(0, 1), (1, 0)])

    def swap(parts, axis):
        size = lax.axis_size(axis)
        if len(parts) == 1:
            return [lax.all_to_all(parts[0], axis, 0, 0, tiled=True)]
        return [parts[0]] + [
            lax.ppermute(parts[k], axis, [(i, i ^ k) for i in range(size)]) for k in range(1, size)
        ]

    def parts_of(whole, axis, shape):
        size = lax.axis_size(axis)
        return [S((size, *shape))] if whole else [S(shape)] * size

    mm = 2 * tok * width * width
    xs = flip(x)
    ends, og_send = call(pack_kernel, "pack", (x, og), [S((EDGE, width)), S((tok, wide))], mm // 999)
    odd = range(1, nseq - 1, 2)
    near = [(i, i + 1) for i in odd] + [(i + 1, i) for i in odd]
    far = [(i, i + 2) for i in odd] + [(i + 1, i - 1) for i in odd]
    h1, h2 = lax.ppermute(ends, seq, near), lax.ppermute(ends, seq, far)
    ogs = flip(og_send)

    def hold_of(cols):
        return pltpu.VMEM((blocks, BLK, cols), BF)

    act, edge = S((count, wide)), S((EDGE, wide))
    e_parts = parts_of(E_WHOLE, "z", (blocks, rows, wide))
    *he, zg, zhg, og_all = call(
        functools.partial(grad_block_kernel, len(e_parts)), "grad_block",
        (x, xs, h1, h2, w_in, taps, og, ogs, tq), e_parts + [act, edge, act],
        mm + mm // 4, [hold_of(wide)],
    )
    ce = swap(he, "z")
    some = wide // nw
    w_parts = parts_of(W_WHOLE, "z", (blocks, rows, some))
    *hw, za, zv, zha, zhv, xt = call(
        functools.partial(value_block_kernel, len(w_parts), nw), "value_block",
        (x, xs, h1, h2, w_in, taps, tq, zhg),
        w_parts * nw + [act, act, edge, edge, S((width, count))],
        2 * mm + mm // 4, [hold_of(wide)],
    )
    cw = [swap(hw[i * len(w_parts) : (i + 1) * len(w_parts)], "z") for i in range(nw)]
    filts = flip(lax.dynamic_slice_in_dim(filt, (1 - core) * wide, wide, axis=2))

    def span_step(parts, off, *after):
        cols = parts[0].shape[-1]
        return call(
            functools.partial(span_kernel, len(parts), len(after), off), "span",
            (*parts, *after, filt, filts, kron, kront, tq),
            parts_of(len(parts) == 1, "z", (blocks * rows + EDGE, cols)), mm // 2,
            [pltpu.VMEM((span, rows, cols), BF), pltpu.VMEM((span, rows, cols), BF if each % 16 == 0 else F32)],
        )

    se = span_step(ce, 0, zha)
    be = swap(se, "z")
    sw, bw, behind = [], [], se[0]
    for i in range(nw):
        sw.append(span_step(cw[i], i * some, behind))
        bw.append(swap(sw[i], "z"))
        behind = sw[i][0]

    high = width // ndp
    av_parts = parts_of(AV_WHOLE, "dp", (high, width))
    du, send, s_av, *p_av = call(
        functools.partial(grad_out_kernel, len(be), len(av_parts)), "grad_out",
        (*be, behind, tqt, za, zv, zha, zhv, taps, xt),
        [S((count, width)), S((tok, width)), S((3, width), F32)] + av_parts,
        2 * mm, [hold_of(wide), pltpu.VMEM((width, width), BF)], SHADE,
    )
    r_av = swap(p_av, "dp")
    du_av, got_av = du, flip(send)

    dus, gots, owns, others, known, r_g, behind = [], [], [], [], [s_av], [], r_av[1:AV_DONE]
    after = p_av[:1]
    for i in range(nw):
        ends_here = i == nw - 1
        extra = -(-9 * 3 * nw // 16) * 16 if ends_here else 0
        g_parts = parts_of(G_WHOLE, "dp", (high + extra, some))
        m_own, m_send, du, send, sums = call(
            functools.partial(value_out_kernel, len(bw[i]), len(after), i * some), "value_out",
            (*bw[i], *after, tqt, zg, zhg, taps, og_all, h1, h2),
            [S((tok, some))] * 2 + [S((count, some)), S((tok, some)), S((3, some), F32)],
            mm // 2, [hold_of(some), pltpu.VMEM((count, some), BF)],
        )
        known.append(sums)
        extra_in = known if ends_here else []
        p_g = call(
            functools.partial(w_grad_kernel, len(behind), len(extra_in)), "w_grad",
            (*behind, xt, du, *extra_in), g_parts, mm, [pltpu.VMEM((width, some), BF)],
        )
        r_g += swap(p_g, "dp")
        dus.append(du)
        gots.append(flip(send))
        owns.append(m_own)
        others.append(flip(m_send))
        after, behind = p_g[:1], p_g[:1]
    acc = call(in_first_kernel, "in_first", (du_av, got_av, w_in, *behind), [S((tok, width), F32)], 2 * mm)[0]
    in_grad, mixed = call(
        functools.partial(in_last_kernel, nw), "in_last",
        (*dus, *gots, *owns, *others, w_in, acc, *behind), [S((tok, width))] * 2, mm,
    )

    cols, half = 3 * wide, high // ncore
    w_own, w_send, t_own = call(
        functools.partial(fold_kernel, len(r_av), len(r_g) // nw, nw), "fold", (*r_av, *r_g),
        [S((half, cols)), S((half, cols)), S((3, cols), F32)], mm // 64, [pltpu.VMEM((high, cols), BF)],
    )

    w_got = flip(w_send)
    step = 1
    while step < nz:
        t_own = t_own + lax.ppermute(t_own, "z", [(i, i ^ step) for i in range(nz)])
        step *= 2
    t_got = flip(t_own)
    mine_of = 3 * width // nseq
    if mine_of % 128 == 0:
        sent = call(
            join_kernel, "join", (w_own, w_got, t_own), [S((half, ncore * mine_of))] * nz, mm // 64,
            [pltpu.VMEM((half, 3 * width), BF)],
        )
        total, send = call(
            functools.partial(sum_kernel, nz), "sum", swap(sent, "z"), [S((half, mine_of), F32)] * 2, mm // 64,
        )
        w_in_grad, taps_grad = call(
            functools.partial(last_kernel, factor), "last", (total, flip(send), t_own, t_got),
            [S((high, mine_of), F32), S((3, 3 * width), F32)], mm // 64,
        )
    else:

        def joined(own, got):
            own, got = own.reshape(-1, 3, 1, wide), got.reshape(-1, 3, 1, wide)
            low, high = jnp.where(core == 0, own, got), jnp.where(core == 0, got, own)
            return jnp.concatenate([low, high], axis=2).reshape(-1, 3 * width)

        taps_grad = joined(t_own, t_got) * factor
        sent = joined(w_own, w_got).reshape(half, nseq, mine_of).transpose(1, 0, 2)
        got = lax.all_to_all(sent, seq, 0, 0, tiled=True).reshape(nz, high, mine_of)
        w_in_grad = jnp.sum(got.astype(F32), axis=0) * factor
    return (mixed[None], in_grad[None], w_in_grad, taps_grad)


def solution(mesh):
    ndp, nseq = mesh.shape["dp"], mesh.shape["seq"]
    split = Mesh(mesh.devices.reshape(ndp, nseq // 2, 2), ("dp", "z", "core"))
    seq = ("z", "core")
    return jax.shard_map(
        functools.partial(shards, NW),
        mesh=split,
        in_specs=(P("dp", seq, None), P("dp", seq, None), P(), P(), P(None, seq, None)),
        out_specs=(P("dp", seq, None), P("dp", seq, None), P("dp", seq), P()),
        check_vma=False,
    )
```

time: 389 us -> 193 us (0.50)
  blocking collectives: 130 us -> 0 us
  waiting for transfers between devices: 151 us -> 74.7 us
  starting transfers between devices: 14.2 us -> 67.7 us
  Pallas kernels: 0 us -> 45.3 us
  matrix products: 43 us -> 0 us
  local copies, waits for them, and re-layouts: 20.1 us -> 3.49 us
  other arithmetic: 15.6 us -> 0.02 us
  between operations: 14.4 us -> 0.93 us
    reduce_scatter x2 -> x0, waiting for transfers between devices: 122 us -> none  [the longest x1 122 us: shards(): lax.psum_scatter(lax.dot_general(rows, du, contract, preferred_element_ty...]
    all_to_all x3 -> x0, blocking collectives: 88.3 us -> none  [the longest x1 30.1 us: shards(): lax.all_to_all(block_section(w.reshape(1, nblocks, BLK, width), table_q),...]
    ppermute x4 -> x45, waiting for transfers between devices: 4.71 us -> 74.7 us  [the longest x30 64.7 us: swap(): lax.ppermute(parts[k], axis, [(i, i ^ k) for i in range(size)])]
    ppermute x4 -> x45, starting transfers between devices: 8.24 us -> 67.7 us  [the longest x30 60.1 us: swap(): lax.ppermute(parts[k], axis, [(i, i ^ k) for i in range(size)])]
    pallas_call x0 -> x17, Pallas kernels: none -> 45.3 us  [call(): pl.pallas_call(kernel, out_shape=outs, in_specs=[whole] * len(ins), out_s...]
    dot_general x9 -> x0, matrix products: 43 us -> none  [the longest x1 12.4 us: shards(): lax.dot_general(rows, du, contract, preferred_element_type=jnp.float32)]
    psum x1 -> x0, blocking collectives: 41.8 us -> none  [shards(): taps_grad = lax.psum(local_taps, ('dp', 'seq')) * factor]
    all_to_all x1 -> x0, waiting for transfers between devices: 24.9 us -> none  [shards(): lax.all_to_all(block_section(e4.reshape(1, nblocks, BLK, width), table_q)...]
  transfers between devices with their start and end apart: 7 -> 45, of which waited for: 4 -> 12; matrix products, arithmetic and copies ran while one was open for 5% -> 0% of each run, Pallas kernels for 0% -> 18%
where the time goes in v2:
time: 193 us; the launch traced here: 192 us
  waiting for transfers between devices  74.7 us (39%)
  starting transfers between devices  67.7 us (35%)
  Pallas kernels  45.3 us (23%)
  local copies, waits for them, and re-layouts  3.49 us (2%)
    ppermute x30, waiting for transfers between devices, swap(): lax.ppermute(parts[k], axis, [(i, i ^ k) for i in range(size)])  64.7 us
    ppermute x30, starting transfers between devices, swap(): lax.ppermute(parts[k], axis, [(i, i ^ k) for i in range(size)])  60.1 us
    pallas_call x17, Pallas kernels, call(): pl.pallas_call(kernel, out_shape=outs, in_specs=[whole] * len(ins), out_s...  45.3 us
    ppermute x2, waiting for transfers between devices, shards(): t_own = t_own + lax.ppermute(t_own, 'z', [(i, i ^ step) for i in range(nz)])  5.52 us
    ppermute x2, waiting for transfers between devices, shards(): h1, h2 = (lax.ppermute(ends, seq, near), lax.ppermute(ends, seq, far))  4.49 us
  transfers between devices with their start and end apart: 45, of which 12 were waited for; matrix products, arithmetic and copies ran while one was open for 0% of the time, Pallas kernels for 18%

profile of v2, /device:TPU:0, one launch (start us, length us, event | category | flops | bytes accessed | tf_op | source)
XLA Modules:
  0.0 192.1 jit_solution(6274204348814393263)
XLA Ops:
  7.0 4.5 %collective-permute-done.2.h2_ref.refs_11_ = bf16[16,1024]{1,0:T(8,128)(2,1)S(1)} collective-permute-done((bf16[16,1024]{1,0:T(8,128)(2,1)S(1)}, bf16[16,1024]{1,0:T(8,128)(2,1)S(1)}, u32[]{:S(2)}, u32[]{:S(2)}) %collective-permute-start.2) | collective-permute-done | bytes 32800 | tf_op jit(solution)/shard_map/ppermute | solution.py:461
  11.6 5.8 %grad_block.1 = (bf16[4,64,512]{2,1,0:T(8,128)(2,1)S(1)}, bf16[4,64,512]{2,1,0:T(8,128)(2,1)S(1)}, bf16[4,64,512]{2,1,0:T(8,128)(2,1)S(1)}, bf16[4,64,512]{2,1,0...) custom-call(bf16[512,1024]{1,0:T(8,128)(2,1)S(1)} %bitcast.8, ...), custom_call_target="tpu_custom_call" | custom-call | flops 1342177280 | bytes 13357056 | tf_op jit(solution)/shard_map/grad_block/pallas_call | solution.py:429
  17.3 3.4 %collective-permute-start.7 = (bf16[4,64,512]{2,1,0:T(8,128)(2,1)S(1)}, bf16[4,64,512]{2,1,0:T(8,128)(2,1)S(1)}, u32[]{:S(2)}, u32[]{:S(2)}) collective-permute-start(bf16[4,64,512]{2,1,0:T(8,128)(2,1)S(1)} %get-tuple-element.84), channel_id=1, source_target_pairs={{0,2},{2,0},{4,6},{6,4},{1,3},{3,1},{5,7},{7,5},{8,10},{10,8},{12,... | collective-permute-start | bytes 786440 | tf_op jit(solution)/shard_map/ppermute | solution.py:448
  20.8 3.0 %collective-permute-start.8 = (bf16[4,64,512]{2,1,0:T(8,128)(2,1)S(1)}, bf16[4,64,512]{2,1,0:T(8,128)(2,1)S(1)}, u32[]{:S(2)}, u32[]{:S(2)}) collective-permute-start(bf16[4,64,512]{2,1,0:T(8,128)(2,1)S(1)} %get-tuple-element.85), channel_id=1, source_target_pairs={{0,4},{2,6},{4,0},{6,2},{1,5},{3,7},{5,1},{7,3},{8,12},{10,14},{12... | collective-permute-start | bytes 786440 | tf_op jit(solution)/shard_map/ppermute | solution.py:448
  23.8 8.2 %value_block.1 = (bf16[4,64,256]{2,1,0:T(8,128)(2,1)S(1)}, bf16[4,64,256]{2,1,0:T(8,128)(2,1)S(1)}, bf16[4,64,256]{2,1,0:T(8,128)(2,1)S(1)}, bf16[4,64,256]{2,1,...) custom-call(bf16[512,1024]{1,0:T(8,128)(2,1)S(1)} %bitcast.9, ...), custom_call_target="tpu_custom_call" | custom-call | flops 2415919104 | bytes 13914112 | tf_op jit(solution)/shard_map/value_block/pallas_call | solution.py:429
  33.5 3.8 %collective-permute-start.5 = (bf16[4,64,256]{2,1,0:T(8,128)(2,1)S(1)}, bf16[4,64,256]{2,1,0:T(8,128)(2,1)S(1)}, u32[]{:S(2)}, u32[]{:S(2)}) collective-permute-start(bf16[4,64,256]{2,1,0:T(8,128)(2,1)S(1)} %get-tuple-element.81), channel_id=1, source_target_pairs={{0,4},{2,6},{4,0},{6,2},{1,5},{3,7},{5,1},{7,3},{8,12},{10,14},{12... | collective-permute-start | bytes 393224 | tf_op jit(solution)/shard_map/ppermute | solution.py:448
  37.4 4.8 %collective-permute-start.17 = (bf16[4,64,256]{2,1,0:T(8,128)(2,1)S(1)}, bf16[4,64,256]{2,1,0:T(8,128)(2,1)S(1)}, u32[]{:S(2)}, u32[]{:S(2)}) collective-permute-start(bf16[4,64,256]{2,1,0:T(8,128)(2,1)S(1)} %get-tuple-element.97), channel_id=1, source_target_pairs={{0,2},{2,0},{4,6},{6,4},{1,3},{3,1},{5,7},{7,5},{8,10},{10,8},{12,... | collective-permute-start | bytes 393224 | tf_op jit(solution)/shard_map/ppermute | solution.py:448
  43.4 11.6 %collective-permute-start.14 = (bf16[272,512]{1,0:T(8,128)(2,1)S(1)}, bf16[272,512]{1,0:T(8,128)(2,1)S(1)}, u32[]{:S(2)}, u32[]{:S(2)}) collective-permute-start(bf16[272,512]{1,0:T(8,128)(2,1)S(1)} %get-tuple-element.93), channel_id=1, source_target_pairs={{0,2},{2,0},{4,6},{6,4},{1,3},{3,1},{5,7},{7,5},{8,10},{10,8},{12,... | collective-permute-start | bytes 835592 | tf_op jit(solution)/shard_map/ppermute | solution.py:448
  55.0 1.7 collective-permute-start.15
  56.7 2.3 %collective-permute-start.16 = (bf16[272,512]{1,0:T(8,128)(2,1)S(1)}, bf16[272,512]{1,0:T(8,128)(2,1)S(1)}, u32[]{:S(2)}, u32[]{:S(2)}) collective-permute-start(bf16[272,512]{1,0:T(8,128)(2,1)S(1)} %get-tuple-element.95), channel_id=1, source_target_pairs={{0,6},{2,4},{4,2},{6,0},{1,7},{3,5},{5,3},{7,1},{8,14},{10,12},{12... | collective-permute-start | bytes 835592 | tf_op jit(solution)/shard_map/ppermute | solution.py:448
  59.0 1.9 collective-permute-start.18
  62.5 29.4 %collective-permute-done.18.refs_2_ = bf16[4,64,256]{2,1,0:T(8,128)(2,1)S(1)} collective-permute-done((bf16[4,64,256]{2,1,0:T(8,128)(2,1)S(1)}, bf16[4,64,256]{2,1,0:T(8,128)(2,1)S(1)}, u32[]{:S(2)}, u32[]{:S(2)}) %collective-permute-start.18) | collective-permute-done | bytes 131104 | tf_op jit(solution)/shard_map/ppermute | solution.py:448
  92.7 10.7 %grad_out.1 = (bf16[1024,1024]{1,0:T(8,128)(2,1)}, bf16[512,1024]{1,0:T(8,128)(2,1)S(1)}, f32[3,1024]{1,0:T(4,128)S(1)}, bf16[256,1024]{1,0:T(8,128)(2,1)S(1)}, ...) custom-call(bf16[272,512]{1,0:T(8,128)(2,1)S(1)} %get-tuple-element.88.refs_4_.refs_0_, ...), custom_call_target="tpu_custom_call" | custom-call | flops 2147483 | bytes 10903 | tf_op jit(solution)/shard_map/grad_out/pallas_call | solution.py:429
  103.5 2.1 %collective-permute-start.23 = (bf16[256,1024]{1,0:T(8,128)(2,1)S(1)}, bf16[256,1024]{1,0:T(8,128)(2,1)S(1)}, u32[]{:S(2)}, u32[]{:S(2)}) collective-permute-start(bf16[256,1024]{1,0:T(8,128)(2,1)S(1)} %get-tuple-element.112), channel_id=1, source_target_pairs={{0,8},{8,0},{16,24},{24,16},{1,9},{9,1},{17,25},{25,17},{2,10},{10... | collective-permute-start | bytes 1572872 | tf_op jit(solution)/shard_map/ppermute | solution.py:448
  105.6 1.5 collective-permute-start.24
  107.1 2.6 %collective-permute-start.11 = (bf16[272,256]{1,0:T(8,128)(2,1)S(1)}, bf16[272,256]{1,0:T(8,128)(2,1)S(1)}, u32[]{:S(2)}, u32[]{:S(2)}) collective-permute-start(bf16[272,256]{1,0:T(8,128)(2,1)S(1)} %get-tuple-element.90), channel_id=1, source_target_pairs={{0,2},{2,0},{4,6},{6,4},{1,3},{3,1},{5,7},{7,5},{8,10},{10,8},{12,... | collective-permute-start | bytes 417800 | tf_op jit(solution)/shard_map/ppermute | solution.py:448
  111.2 2.8 %collective-permute-done.11.refs_1_ = bf16[272,256]{1,0:T(8,128)(2,1)S(1)} collective-permute-done((bf16[272,256]{1,0:T(8,128)(2,1)S(1)}, bf16[272,256]{1,0:T(8,128)(2,1)S(1)}, u32[]{:S(2)}, u32[]{:S(2)}) %collective-permute-start.11) | collective-permute-done | bytes 139296 | tf_op jit(solution)/shard_map/ppermute | solution.py:448
  114.0 2.3 %collective-permute-start.13 = (bf16[272,256]{1,0:T(8,128)(2,1)S(1)}, bf16[272,256]{1,0:T(8,128)(2,1)S(1)}, u32[]{:S(2)}, u32[]{:S(2)}) collective-permute-start(bf16[272,256]{1,0:T(8,128)(2,1)S(1)} %get-tuple-element.92), channel_id=1, source_target_pairs={{0,6},{2,4},{4,2},{6,0},{1,7},{3,5},{5,3},{7,1},{8,14},{10,12},{12... | collective-permute-start | bytes 417800 | tf_op jit(solution)/shard_map/ppermute | solution.py:448
  116.3 6.1 %collective-permute-done.12.refs_2_ = bf16[272,256]{1,0:T(8,128)(2,1)S(1)} collective-permute-done((bf16[272,256]{1,0:T(8,128)(2,1)S(1)}, bf16[272,256]{1,0:T(8,128)(2,1)S(1)}, u32[]{:S(2)}, u32[]{:S(2)}) %collective-permute-start.12) | collective-permute-done | bytes 139296 | tf_op jit(solution)/shard_map/ppermute | solution.py:448
  122.4 3.1 %collective-permute-start.21 = (bf16[272,256]{1,0:T(8,128)(2,1)S(1)}, bf16[272,256]{1,0:T(8,128)(2,1)S(1)}, u32[]{:S(2)}, u32[]{:S(2)}) collective-permute-start(bf16[272,256]{1,0:T(8,128)(2,1)S(1)} %get-tuple-element.110), channel_id=1, source_target_pairs={{0,4},{2,6},{4,0},{6,2},{1,5},{3,7},{5,1},{7,3},{8,12},{10,14},{12... | collective-permute-start | bytes 417800 | tf_op jit(solution)/shard_map/ppermute | solution.py:448
  130.7 4.9 %collective-permute-done.21.refs_2_ = bf16[272,256]{1,0:T(8,128)(2,1)S(1)} collective-permute-done((bf16[272,256]{1,0:T(8,128)(2,1)S(1)}, bf16[272,256]{1,0:T(8,128)(2,1)S(1)}, u32[]{:S(2)}, u32[]{:S(2)}) %collective-permute-start.21) | collective-permute-done | bytes 139296 | tf_op jit(solution)/shard_map/ppermute | solution.py:448
  139.1 1.7 collective-permute-start.34
  144.1 7.0 %collective-permute-done.33.refs_7_ = bf16[256,256]{1,0:T(8,128)(2,1)S(1)} collective-permute-done((bf16[256,256]{1,0:T(8,128)(2,1)S(1)}, bf16[256,256]{1,0:T(8,128)(2,1)S(1)}, u32[]{:S(2)}, u32[]{:S(2)}) %collective-permute-start.33) | collective-permute-done | bytes 131104 | tf_op jit(solution)/shard_map/ppermute | solution.py:448
  152.9 2.2 %collective-permute-start.38 = (f32[3,1536]{1,0:T(4,128)S(1)}, f32[3,1536]{1,0:T(4,128)S(1)}, u32[]{:S(2)}, u32[]{:S(2)}) collective-permute-start(f32[3,1536]{1,0:T(4,128)S(1)} %get-tuple-element.139), channel_id=1, source_target_pairs={{0,2},{2,0},{4,6},{6,4},{1,3},{3,1},{5,7},{7,5},{8,10},{10,8},{12,... | collective-permute-start | bytes 55304 | tf_op jit(solution)/shard_map/ppermute | solution.py:553
  155.1 1.8 collective-permute-done.38
  158.0 3.7 %collective-permute-done.39 = f32[3,1536]{1,0:T(4,128)S(1)} collective-permute-done((f32[3,1536]{1,0:T(4,128)S(1)}, f32[3,1536]{1,0:T(4,128)S(1)}, u32[]{:S(2)}, u32[]{:S(2)}) %collective-permute-start.39) | collective-permute-done | bytes 18464 | tf_op jit(solution)/shard_map/ppermute | solution.py:553
  161.9 2.0 %collective-permute-start.40 = (bf16[128,768]{1,0:T(8,128)(2,1)S(1)}, bf16[128,768]{1,0:T(8,128)(2,1)S(1)}, u32[]{:S(2)}, u32[]{:S(2)}) collective-permute-start(bf16[128,768]{1,0:T(8,128)(2,1)S(1)} %get-tuple-element.141), channel_id=1, source_target_pairs={{0,2},{2,0},{4,6},{6,4},{1,3},{3,1},{5,7},{7,5},{8,10},{10,8},{12,... | collective-permute-start | bytes 589832 | tf_op jit(solution)/shard_map/ppermute | solution.py:448
  163.9 2.4 %collective-permute-start.42 = (bf16[128,768]{1,0:T(8,128)(2,1)S(1)}, bf16[128,768]{1,0:T(8,128)(2,1)S(1)}, u32[]{:S(2)}, u32[]{:S(2)}) collective-permute-start(bf16[128,768]{1,0:T(8,128)(2,1)S(1)} %get-tuple-element.143), channel_id=1, source_target_pairs={{0,6},{2,4},{4,2},{6,0},{1,7},{3,5},{5,3},{7,1},{8,14},{10,12},{12... | collective-permute-start | bytes 589832 | tf_op jit(solution)/shard_map/ppermute | solution.py:448
  166.4 4.0 %collective-permute-done.40.refs_1_ = bf16[128,768]{1,0:T(8,128)(2,1)S(1)} collective-permute-done((bf16[128,768]{1,0:T(8,128)(2,1)S(1)}, bf16[128,768]{1,0:T(8,128)(2,1)S(1)}, u32[]{:S(2)}, u32[]{:S(2)}) %collective-permute-start.40) | collective-permute-done | bytes 196640 | tf_op jit(solution)/shard_map/ppermute | solution.py:448
  170.4 8.8 %collective-permute-done.41.refs_2_ = bf16[128,768]{1,0:T(8,128)(2,1)S(1)} collective-permute-done((bf16[128,768]{1,0:T(8,128)(2,1)S(1)}, bf16[128,768]{1,0:T(8,128)(2,1)S(1)}, u32[]{:S(2)}, u32[]{:S(2)}) %collective-permute-start.41) | collective-permute-done | bytes 196640 | tf_op jit(solution)/shard_map/ppermute | solution.py:448
  179.9 5.4 %in_first.1.refs_9_ = f32[512,1024]{1,0:T(8,128)S(1)} custom-call(bf16[1024,1024]{1,0:T(8,128)(2,1)S(1)} %copy-done.6, bf16[512,1024]{1,0:T(8,128)(2,1)S(1)} %collective-permute-done.29.got_ref, bf16[1024,3072]{1,0:T(8,128)(2,1)} %refs_8_.8, bf16[320,256]{1,0:T(8,128)(2,1)S(1)} %get-tuple-element.127.after_ref.refs_10_.refs_8_), custom_call_target="tpu_custom_call" | custom-call | flops 2147483648 | bytes 11698176 | tf_op jit(solution)/shard_map/in_first/pallas_call | solution.py:429
  185.9 5.4 %in_last.1 = (bf16[512,1024]{1,0:T(8,128)(2,1)}, bf16[512,1024]{1,0:T(8,128)(2,1)}) custom-call(bf16[1024,256]{1,0:T(8,128)(2,1)S(1)} %get-tuple-element.108.refs_3_.refs_0_, bf16[1024,256]{1,0:T(8,128)(2,1)S(1)} %get-tuple-element.115.refs_2_.refs_1_, bf16[512,256]{1,0:T(8,128)(2,1)S(1)} %collective-permute-done.25.refs_2_, ...), custom_call_target="tpu_custom_call" | custom-call | flops 1073741824 | bytes 13271040 | tf_op jit(solution)/shard_map/in_last/pallas_call | solution.py:429
  (102 shorter events, 29.9 us)
Async XLA Ops:
  0.6 10.9 %collective-permute-start = (bf16[512,1024]{1,0:T(8,128)(2,1)}, bf16[512,1024]{1,0:T(8,128)(2,1)S(1)}, u32[]{:S(2)}, u32[]{:S(2)}) collective-permute-start(bf16[512,1024]{1,0:T(8,128)(2,1)} %bitcast.6), channel_id=1, source_target_pairs={{0,1},{1,0},{2,3},{3,2},{4,5},{5,4},{6,7},{7,6},{8,9},{9,8},{10,11... | collective-permute-start | bytes 3145736 | tf_op jit(solution)/shard_map/ppermute | solution.py:441
  4.6 28.9 %collective-permute-start.10 = (bf16[16,32,512]{2,1,0:T(8,128)(2,1)S(1)}, bf16[16,32,512]{2,1,0:T(8,128)(2,1)S(1)}, u32[]{:S(2)}, u32[]{:S(2)}) collective-permute-start(bf16[16,32,512]{2,1,0:T(8,128)(2,1)S(1)} %constant_dynamic-slice_fusion), channel_id=1, source_target_pairs={{0,1},{1,0},{2,3},{3,2},{4,5},{5,4},{6,7},{7,6},{8,9},{9,8},{10,11... | collective-permute-start | bytes 1572872 | tf_op jit(solution)/shard_map/ppermute | solution.py:441
  17.3 20.0 %collective-permute-start.7 = (bf16[4,64,512]{2,1,0:T(8,128)(2,1)S(1)}, bf16[4,64,512]{2,1,0:T(8,128)(2,1)S(1)}, u32[]{:S(2)}, u32[]{:S(2)}) collective-permute-start(bf16[4,64,512]{2,1,0:T(8,128)(2,1)S(1)} %get-tuple-element.84), channel_id=1, source_target_pairs={{0,2},{2,0},{4,6},{6,4},{1,3},{3,1},{5,7},{7,5},{8,10},{10,8},{12,... | collective-permute-start | bytes 786440 | tf_op jit(solution)/shard_map/ppermute | solution.py:448
  20.8 16.6 %collective-permute-start.8 = (bf16[4,64,512]{2,1,0:T(8,128)(2,1)S(1)}, bf16[4,64,512]{2,1,0:T(8,128)(2,1)S(1)}, u32[]{:S(2)}, u32[]{:S(2)}) collective-permute-start(bf16[4,64,512]{2,1,0:T(8,128)(2,1)S(1)} %get-tuple-element.85), channel_id=1, source_target_pairs={{0,4},{2,6},{4,0},{6,2},{1,5},{3,7},{5,1},{7,3},{8,12},{10,14},{12... | collective-permute-start | bytes 786440 | tf_op jit(solution)/shard_map/ppermute | solution.py:448
  23.8 18.4 %collective-permute-start.9 = (bf16[4,64,512]{2,1,0:T(8,128)(2,1)S(1)}, bf16[4,64,512]{2,1,0:T(8,128)(2,1)S(1)}, u32[]{:S(2)}, u32[]{:S(2)}) collective-permute-start(bf16[4,64,512]{2,1,0:T(8,128)(2,1)S(1)} %get-tuple-element.86), channel_id=1, source_target_pairs={{0,6},{2,4},{4,2},{6,0},{1,7},{3,5},{5,3},{7,1},{8,14},{10,12},{12... | collective-permute-start | bytes 786440 | tf_op jit(solution)/shard_map/ppermute | solution.py:448
  33.0 22.1 %collective-permute-start.4 = (bf16[4,64,256]{2,1,0:T(8,128)(2,1)S(1)}, bf16[4,64,256]{2,1,0:T(8,128)(2,1)S(1)}, u32[]{:S(2)}, u32[]{:S(2)}) collective-permute-start(bf16[4,64,256]{2,1,0:T(8,128)(2,1)S(1)} %get-tuple-element.80), channel_id=1, source_target_pairs={{0,2},{2,0},{4,6},{6,4},{1,3},{3,1},{5,7},{7,5},{8,10},{10,8},{12,... | collective-permute-start | bytes 393224 | tf_op jit(solution)/shard_map/ppermute | solution.py:448
  33.5 23.2 %collective-permute-start.5 = (bf16[4,64,256]{2,1,0:T(8,128)(2,1)S(1)}, bf16[4,64,256]{2,1,0:T(8,128)(2,1)S(1)}, u32[]{:S(2)}, u32[]{:S(2)}) collective-permute-start(bf16[4,64,256]{2,1,0:T(8,128)(2,1)S(1)} %get-tuple-element.81), channel_id=1, source_target_pairs={{0,4},{2,6},{4,0},{6,2},{1,5},{3,7},{5,1},{7,3},{8,12},{10,14},{12... | collective-permute-start | bytes 393224 | tf_op jit(solution)/shard_map/ppermute | solution.py:448
  37.3 21.7 %collective-permute-start.6 = (bf16[4,64,256]{2,1,0:T(8,128)(2,1)S(1)}, bf16[4,64,256]{2,1,0:T(8,128)(2,1)S(1)}, u32[]{:S(2)}, u32[]{:S(2)}) collective-permute-start(bf16[4,64,256]{2,1,0:T(8,128)(2,1)S(1)} %get-tuple-element.82), channel_id=1, source_target_pairs={{0,6},{2,4},{4,2},{6,0},{1,7},{3,5},{5,3},{7,1},{8,14},{10,12},{12... | collective-permute-start | bytes 393224 | tf_op jit(solution)/shard_map/ppermute | solution.py:448
  37.4 23.6 %collective-permute-start.17 = (bf16[4,64,256]{2,1,0:T(8,128)(2,1)S(1)}, bf16[4,64,256]{2,1,0:T(8,128)(2,1)S(1)}, u32[]{:S(2)}, u32[]{:S(2)}) collective-permute-start(bf16[4,64,256]{2,1,0:T(8,128)(2,1)S(1)} %get-tuple-element.97), channel_id=1, source_target_pairs={{0,2},{2,0},{4,6},{6,4},{1,3},{3,1},{5,7},{7,5},{8,10},{10,8},{12,... | collective-permute-start | bytes 393224 | tf_op jit(solution)/shard_map/ppermute | solution.py:448
  43.4 49.3 %collective-permute-start.14 = (bf16[272,512]{1,0:T(8,128)(2,1)S(1)}, bf16[272,512]{1,0:T(8,128)(2,1)S(1)}, u32[]{:S(2)}, u32[]{:S(2)}) collective-permute-start(bf16[272,512]{1,0:T(8,128)(2,1)S(1)} %get-tuple-element.93), channel_id=1, source_target_pairs={{0,2},{2,0},{4,6},{6,4},{1,3},{3,1},{5,7},{7,5},{8,10},{10,8},{12,... | collective-permute-start | bytes 835592 | tf_op jit(solution)/shard_map/ppermute | solution.py:448
  55.0 37.7 %collective-permute-start.15 = (bf16[272,512]{1,0:T(8,128)(2,1)S(1)}, bf16[272,512]{1,0:T(8,128)(2,1)S(1)}, u32[]{:S(2)}, u32[]{:S(2)}) collective-permute-start(bf16[272,512]{1,0:T(8,128)(2,1)S(1)} %get-tuple-element.94), channel_id=1, source_target_pairs={{0,4},{2,6},{4,0},{6,2},{1,5},{3,7},{5,1},{7,3},{8,12},{10,14},{12... | collective-permute-start | bytes 835592 | tf_op jit(solution)/shard_map/ppermute | solution.py:448
  56.7 36.0 %collective-permute-start.16 = (bf16[272,512]{1,0:T(8,128)(2,1)S(1)}, bf16[272,512]{1,0:T(8,128)(2,1)S(1)}, u32[]{:S(2)}, u32[]{:S(2)}) collective-permute-start(bf16[272,512]{1,0:T(8,128)(2,1)S(1)} %get-tuple-element.95), channel_id=1, source_target_pairs={{0,6},{2,4},{4,2},{6,0},{1,7},{3,5},{5,3},{7,1},{8,14},{10,12},{12... | collective-permute-start | bytes 835592 | tf_op jit(solution)/shard_map/ppermute | solution.py:448
  59.0 32.8 %collective-permute-start.18 = (bf16[4,64,256]{2,1,0:T(8,128)(2,1)S(1)}, bf16[4,64,256]{2,1,0:T(8,128)(2,1)S(1)}, u32[]{:S(2)}, u32[]{:S(2)}) collective-permute-start(bf16[4,64,256]{2,1,0:T(8,128)(2,1)S(1)} %get-tuple-element.98), channel_id=1, source_target_pairs={{0,4},{2,6},{4,0},{6,2},{1,5},{3,7},{5,1},{7,3},{8,12},{10,14},{12... | collective-permute-start | bytes 393224 | tf_op jit(solution)/shard_map/ppermute | solution.py:448
  61.0 30.9 %collective-permute-start.19 = (bf16[4,64,256]{2,1,0:T(8,128)(2,1)S(1)}, bf16[4,64,256]{2,1,0:T(8,128)(2,1)S(1)}, u32[]{:S(2)}, u32[]{:S(2)}) collective-permute-start(bf16[4,64,256]{2,1,0:T(8,128)(2,1)S(1)} %get-tuple-element.99), channel_id=1, source_target_pairs={{0,6},{2,4},{4,2},{6,0},{1,7},{3,5},{5,3},{7,1},{8,14},{10,12},{12... | collective-permute-start | bytes 393224 | tf_op jit(solution)/shard_map/ppermute | solution.py:448
  103.5 22.0 %collective-permute-start.23 = (bf16[256,1024]{1,0:T(8,128)(2,1)S(1)}, bf16[256,1024]{1,0:T(8,128)(2,1)S(1)}, u32[]{:S(2)}, u32[]{:S(2)}) collective-permute-start(bf16[256,1024]{1,0:T(8,128)(2,1)S(1)} %get-tuple-element.112), channel_id=1, source_target_pairs={{0,8},{8,0},{16,24},{24,16},{1,9},{9,1},{17,25},{25,17},{2,10},{10... | collective-permute-start | bytes 1572872 | tf_op jit(solution)/shard_map/ppermute | solution.py:448
  105.6 23.5 %collective-permute-start.24 = (bf16[256,1024]{1,0:T(8,128)(2,1)S(1)}, bf16[256,1024]{1,0:T(8,128)(2,1)S(1)}, u32[]{:S(2)}, u32[]{:S(2)}) collective-permute-start(bf16[256,1024]{1,0:T(8,128)(2,1)S(1)} %get-tuple-element.113), channel_id=1, source_target_pairs={{0,16},{8,24},{16,0},{24,8},{1,17},{9,25},{17,1},{25,9},{2,18},{10... | collective-permute-start | bytes 1572872 | tf_op jit(solution)/shard_map/ppermute | solution.py:448
  109.8 31.1 %collective-permute-start.30 = (bf16[256,1024]{1,0:T(8,128)(2,1)S(1)}, bf16[256,1024]{1,0:T(8,128)(2,1)S(1)}, u32[]{:S(2)}, u32[]{:S(2)}) collective-permute-start(bf16[256,1024]{1,0:T(8,128)(2,1)S(1)} %get-tuple-element.130), channel_id=1, source_target_pairs={{0,24},{8,16},{16,8},{24,0},{1,25},{9,17},{17,9},{25,1},{2,26},{10... | collective-permute-start | bytes 1572872 | tf_op jit(solution)/shard_map/ppermute | solution.py:448
  109.9 12.5 %collective-permute-start.12 = (bf16[272,256]{1,0:T(8,128)(2,1)S(1)}, bf16[272,256]{1,0:T(8,128)(2,1)S(1)}, u32[]{:S(2)}, u32[]{:S(2)}) collective-permute-start(bf16[272,256]{1,0:T(8,128)(2,1)S(1)} %get-tuple-element.91), channel_id=1, source_target_pairs={{0,4},{2,6},{4,0},{6,2},{1,5},{3,7},{5,1},{7,3},{8,12},{10,14},{12... | collective-permute-start | bytes 417800 | tf_op jit(solution)/shard_map/ppermute | solution.py:448
  122.4 13.3 %collective-permute-start.21 = (bf16[272,256]{1,0:T(8,128)(2,1)S(1)}, bf16[272,256]{1,0:T(8,128)(2,1)S(1)}, u32[]{:S(2)}, u32[]{:S(2)}) collective-permute-start(bf16[272,256]{1,0:T(8,128)(2,1)S(1)} %get-tuple-element.110), channel_id=1, source_target_pairs={{0,4},{2,6},{4,0},{6,2},{1,5},{3,7},{5,1},{7,3},{8,12},{10,14},{12... | collective-permute-start | bytes 417800 | tf_op jit(solution)/shard_map/ppermute | solution.py:448
  125.5 11.4 %collective-permute-start.22 = (bf16[272,256]{1,0:T(8,128)(2,1)S(1)}, bf16[272,256]{1,0:T(8,128)(2,1)S(1)}, u32[]{:S(2)}, u32[]{:S(2)}) collective-permute-start(bf16[272,256]{1,0:T(8,128)(2,1)S(1)} %get-tuple-element.111), channel_id=1, source_target_pairs={{0,6},{2,4},{4,2},{6,0},{1,7},{3,5},{5,3},{7,1},{8,14},{10,12},{12... | collective-permute-start | bytes 417800 | tf_op jit(solution)/shard_map/ppermute | solution.py:448
  129.1 50.8 %collective-permute-start.29 = (bf16[512,1024]{1,0:T(8,128)(2,1)S(1)}, bf16[512,1024]{1,0:T(8,128)(2,1)S(1)}, u32[]{:S(2)}, u32[]{:S(2)}) collective-permute-start(bf16[512,1024]{1,0:T(8,128)(2,1)S(1)} %get-tuple-element.123), channel_id=1, source_target_pairs={{0,1},{1,0},{2,3},{3,2},{4,5},{5,4},{6,7},{7,6},{8,9},{9,8},{10,11... | collective-permute-start | bytes 3145736 | tf_op jit(solution)/shard_map/ppermute | solution.py:441
  129.8 11.3 %collective-permute-start.31 = (bf16[256,256]{1,0:T(8,128)(2,1)S(1)}, bf16[256,256]{1,0:T(8,128)(2,1)S(1)}, u32[]{:S(2)}, u32[]{:S(2)}) collective-permute-start(bf16[256,256]{1,0:T(8,128)(2,1)S(1)} %get-tuple-element.131), channel_id=1, source_target_pairs={{0,8},{8,0},{16,24},{24,16},{1,9},{9,1},{17,25},{25,17},{2,10},{10... | collective-permute-start | bytes 393224 | tf_op jit(solution)/shard_map/ppermute | solution.py:448
  139.1 12.0 %collective-permute-start.34 = (bf16[320,256]{1,0:T(8,128)(2,1)S(1)}, bf16[320,256]{1,0:T(8,128)(2,1)S(1)}, u32[]{:S(2)}, u32[]{:S(2)}) collective-permute-start(bf16[320,256]{1,0:T(8,128)(2,1)S(1)} %get-tuple-element.134), channel_id=1, source_target_pairs={{0,8},{8,0},{16,24},{24,16},{1,9},{9,1},{17,25},{25,17},{2,10},{10... | collective-permute-start | bytes 491528 | tf_op jit(solution)/shard_map/ppermute | solution.py:448
  140.8 11.1 %collective-permute-start.35 = (bf16[320,256]{1,0:T(8,128)(2,1)S(1)}, bf16[320,256]{1,0:T(8,128)(2,1)S(1)}, u32[]{:S(2)}, u32[]{:S(2)}) collective-permute-start(bf16[320,256]{1,0:T(8,128)(2,1)S(1)} %get-tuple-element.135), channel_id=1, source_target_pairs={{0,16},{8,24},{16,0},{24,8},{1,17},{9,25},{17,1},{25,9},{2,18},{10... | collective-permute-start | bytes 491528 | tf_op jit(solution)/shard_map/ppermute | solution.py:448
  141.2 10.8 %collective-permute-start.36 = (bf16[320,256]{1,0:T(8,128)(2,1)S(1)}, bf16[320,256]{1,0:T(8,128)(2,1)S(1)}, u32[]{:S(2)}, u32[]{:S(2)}) collective-permute-start(bf16[320,256]{1,0:T(8,128)(2,1)S(1)} %get-tuple-element.136), channel_id=1, source_target_pairs={{0,24},{8,16},{16,8},{24,0},{1,25},{9,17},{17,9},{25,1},{2,26},{10... | collective-permute-start | bytes 491528 | tf_op jit(solution)/shard_map/ppermute | solution.py:448
  152.8 8.9 %collective-permute-start.37 = (bf16[128,1536]{1,0:T(8,128)(2,1)S(1)}, bf16[128,1536]{1,0:T(8,128)(2,1)S(1)}, u32[]{:S(2)}, u32[]{:S(2)}) collective-permute-start(bf16[128,1536]{1,0:T(8,128)(2,1)S(1)} %get-tuple-element.138), channel_id=1, source_target_pairs={{0,1},{1,0},{2,3},{3,2},{4,5},{5,4},{6,7},{7,6},{8,9},{9,8},{10,11... | collective-permute-start | bytes 1179656 | tf_op jit(solution)/shard_map/ppermute | solution.py:441
  161.9 8.5 %collective-permute-start.40 = (bf16[128,768]{1,0:T(8,128)(2,1)S(1)}, bf16[128,768]{1,0:T(8,128)(2,1)S(1)}, u32[]{:S(2)}, u32[]{:S(2)}) collective-permute-start(bf16[128,768]{1,0:T(8,128)(2,1)S(1)} %get-tuple-element.141), channel_id=1, source_target_pairs={{0,2},{2,0},{4,6},{6,4},{1,3},{3,1},{5,7},{7,5},{8,10},{10,8},{12,... | collective-permute-start | bytes 589832 | tf_op jit(solution)/shard_map/ppermute | solution.py:448
  163.9 15.3 %collective-permute-start.41 = (bf16[128,768]{1,0:T(8,128)(2,1)S(1)}, bf16[128,768]{1,0:T(8,128)(2,1)S(1)}, u32[]{:S(2)}, u32[]{:S(2)}) collective-permute-start(bf16[128,768]{1,0:T(8,128)(2,1)S(1)} %get-tuple-element.142), channel_id=1, source_target_pairs={{0,4},{2,6},{4,0},{6,2},{1,5},{3,7},{5,1},{7,3},{8,12},{10,14},{12... | collective-permute-start | bytes 589832 | tf_op jit(solution)/shard_map/ppermute | solution.py:448
  163.9 15.3 %collective-permute-start.42 = (bf16[128,768]{1,0:T(8,128)(2,1)S(1)}, bf16[128,768]{1,0:T(8,128)(2,1)S(1)}, u32[]{:S(2)}, u32[]{:S(2)}) collective-permute-start(bf16[128,768]{1,0:T(8,128)(2,1)S(1)} %get-tuple-element.143), channel_id=1, source_target_pairs={{0,6},{2,4},{4,2},{6,0},{1,7},{3,5},{5,3},{7,1},{8,14},{10,12},{12... | collective-permute-start | bytes 589832 | tf_op jit(solution)/shard_map/ppermute | solution.py:448
  166.4 18.9 %collective-permute-start.25 = (bf16[512,256]{1,0:T(8,128)(2,1)S(1)}, bf16[512,256]{1,0:T(8,128)(2,1)S(1)}, u32[]{:S(2)}, u32[]{:S(2)}) collective-permute-start(bf16[512,256]{1,0:T(8,128)(2,1)S(1)} %get-tuple-element.116), channel_id=1, source_target_pairs={{0,1},{1,0},{2,3},{3,2},{4,5},{5,4},{6,7},{7,6},{8,9},{9,8},{10,11... | collective-permute-start | bytes 786440 | tf_op jit(solution)/shard_map/ppermute | solution.py:441
  170.4 15.5 %collective-permute-start.27 = (bf16[512,256]{1,0:T(8,128)(2,1)S(1)}, bf16[512,256]{1,0:T(8,128)(2,1)S(1)}, u32[]{:S(2)}, u32[]{:S(2)}) collective-permute-start(bf16[512,256]{1,0:T(8,128)(2,1)S(1)} %get-tuple-element.120), channel_id=1, source_target_pairs={{0,1},{1,0},{2,3},{3,2},{4,5},{5,4},{6,7},{7,6},{8,9},{9,8},{10,11... | collective-permute-start | bytes 786440 | tf_op jit(solution)/shard_map/ppermute | solution.py:441
  179.9 11.5 %collective-permute-start.43 = (f32[128,384]{1,0:T(8,128)S(1)}, f32[128,384]{1,0:T(8,128)S(1)}, u32[]{:S(2)}, u32[]{:S(2)}) collective-permute-start(f32[128,384]{1,0:T(8,128)S(1)} %get-tuple-element.145), channel_id=1, source_target_pairs={{0,1},{1,0},{2,3},{3,2},{4,5},{5,4},{6,7},{7,6},{8,9},{9,8},{10,11... | collective-permute-start | bytes 589832 | tf_op jit(solution)/shard_map/ppermute | solution.py:441
  (25 other events, 237.5 us)

commit v3 on v2

--- a/solution.py
+++ b/solution.py
@@ -40,10 +40,14 @@
 
 def neighbours(cells, before, after):
     count = cells.shape[0]
-    row = lax.broadcasted_iota(jnp.int32, cells.shape, 0)
-    earlier = jnp.where(row == 0, before, pltpu.roll(cells, 1, 0))
-    later = jnp.where(row == count - 1, after, pltpu.roll(cells, count - 1, 0))
-    return earlier, later
+    row = lax.broadcasted_iota(jnp.int32, (8, cells.shape[1]), 0)
+    earlier, later = pltpu.roll(cells, 1, 0), pltpu.roll(cells, count - 1, 0)
+    head = jnp.where(row == 0, before, earlier[0:8])
+    tail = jnp.where(row == 7, after, later[count - 8 :])
+    return (
+        jnp.concatenate([head, earlier[8:]], axis=0),
+        jnp.concatenate([later[: count - 8], tail], axis=0),
+    )
 
 
 def short_conv(cells, edge, taps):
@@ -116,9 +120,9 @@
 
 
 def grad_block_kernel(
-    n, x_ref, xs_ref, h1_ref, h2_ref, w_ref, taps_ref, og_ref, ogs_ref, tq_ref, *refs
+    n, x_ref, xs_ref, h1_ref, h2_ref, w_ref, taps_ref, og_ref, ogs_ref, tq_ref, filt_ref, *refs
 ):
-    outs, (z_ref, zh_ref, og_all_ref, hold) = refs[:n], refs[n:]
+    outs, (z_ref, zh_ref, og_all_ref, send_ref, hold) = refs[:n], refs[n:]
     core, tok = lax.axis_index("core"), x_ref.shape[0]
     width = z_ref.shape[1]
     og_all_ref[part_of(core, tok), :] = og_ref[:, part_of(core, width)]
@@ -131,6 +135,7 @@
         e4 = (og_all_ref[:, here].astype(F32) * g).astype(BF)
         put_blocks(tq_ref[...], e4, hold, here)
     hand_rows(hold, outs, pl.ds(0, width))
+    send_ref[...] = filt_ref[:, :, part_of(1 - core, width)]
 
 
 def value_block_kernel(
@@ -258,10 +263,24 @@
     multiply(xt_ref, du_ref, outs, part)
 
 
-def three_parts(value):
+def two_parts(value):
     high = rounded(value)
-    middle = rounded(value - high)
-    return [high, middle, value - high - middle]
+    return [high, value - high]
+
+
+def tap_rows(every, width, rows):
+    lines = []
+    for at in range(0, every.shape[1], width):
+        lines += two_parts(every[:, at : at + width])
+    if rows > 3 * len(lines):
+        lines.append(jnp.zeros((rows - 3 * len(lines), width), F32))
+    return jnp.concatenate(lines, axis=0).astype(BF)
+
+
+def taps_of(sums, out_ref):
+    width = sums.shape[1]
+    for run in range(out_ref.shape[1] // width):
+        out_ref[:, run * width : (run + 1) * width] = sums[6 * run : 6 * run + 3] + sums[6 * run + 3 : 6 * run + 6]
 
 
 def value_out_kernel(n, skip, off, *refs):
@@ -296,14 +315,9 @@
         av = known[0][...]
         half = av.shape[1] // 2
         every = [av[:, :half], *(ref[...] for ref in known[1:]), av[:, half:]]
-        every = jnp.concatenate(every, axis=1)
-        lines = []
-        for at in range(0, 3 * half, width):
-            lines += three_parts(every[:, at : at + width])
         rows = part.shape[0] // lax.axis_size("dp")
         extra = outs[0].shape[-2] - rows
-        lines.append(jnp.zeros((extra - 3 * len(lines), width), F32))
-        block = jnp.concatenate(lines, axis=0).astype(BF)
+        block = tap_rows(jnp.concatenate(every, axis=1), width, extra)
         for _, out in pieces(outs, "dp"):
             out[rows : rows + extra, :] = block
 
@@ -366,10 +380,7 @@
     send_ref[...] = hold[part_of(1 - core, half), :]
     extra = gs[-1][0].shape[0] - rows
     sums = add_all([ref[rows : rows + extra, :].astype(F32) for ref in gs[-1]])
-    for group in range(3 * nw):
-        at = 9 * group
-        value = sums[at : at + 3] + sums[at + 3 : at + 6] + sums[at + 6 : at + 9]
-        taps_ref[:, group * width : (group + 1) * width] = value
+    taps_of(sums, taps_ref)
 
 
 def spread(own_ref, got_ref, out_ref):
@@ -381,19 +392,23 @@
             out_ref[:, pl.ds(at, width)] = ref[:, cols]
 
 
-def join_kernel(own_ref, got_ref, after_ref, *refs):
+def join_kernel(own_ref, got_ref, taps_ref, *refs):
     outs, hold = refs[:-1], refs[-1]
     spread(own_ref, got_ref, hold)
+    rows, width = hold.shape[0], outs[0].shape[1]
+    block = tap_rows(taps_ref[...], width, outs[0].shape[0] - rows)
     for there, out in pieces(outs, "z"):
-        out[...] = hold[:, part_of(there, out.shape[1])]
+        out[0:rows, :] = hold[:, part_of(there, width)]
+        out[rows:, :] = block
 
 
 def sum_kernel(n, *refs):
-    ins, (own_ref, send_ref) = refs[:n], refs[n:]
-    core, width = lax.axis_index("core"), own_ref.shape[1]
+    ins, (own_ref, send_ref, taps_ref) = refs[:n], refs[n + 1 :]
+    core, (rows, width) = lax.axis_index("core"), own_ref.shape
     for out, owner in ((own_ref, core), (send_ref, 1 - core)):
         cols = part_of(owner, width)
-        out[...] = add_all([ref[:, cols].astype(F32) for ref in ins])
+        out[...] = add_all([ref[0:rows, cols].astype(F32) for ref in ins])
+    taps_of(add_all([ref[rows:, :].astype(F32) for ref in ins]), taps_ref)
 
 
 def last_kernel(factor, own_ref, got_ref, t_own_ref, t_got_ref, out_ref, taps_ref):
@@ -466,9 +481,9 @@
 
     act, edge = S((count, wide)), S((EDGE, wide))
     e_parts = parts_of(E_WHOLE, "z", (blocks, rows, wide))
-    *he, zg, zhg, og_all = call(
+    *he, zg, zhg, og_all, filt_send = call(
         functools.partial(grad_block_kernel, len(e_parts)), "grad_block",
-        (x, xs, h1, h2, w_in, taps, og, ogs, tq), e_parts + [act, edge, act],
+        (x, xs, h1, h2, w_in, taps, og, ogs, tq, filt), e_parts + [act, edge, act, S((span, each, wide))],
         mm + mm // 4, [hold_of(wide)],
     )
     ce = swap(he, "z")
@@ -481,7 +496,7 @@
         2 * mm + mm // 4, [hold_of(wide)],
     )
     cw = [swap(hw[i * len(w_parts) : (i + 1) * len(w_parts)], "z") for i in range(nw)]
-    filts = flip(lax.dynamic_slice_in_dim(filt, (1 - core) * wide, wide, axis=2))
+    filts = flip(filt_send)
 
     def span_step(parts, off, *after):
         cols = parts[0].shape[-1]
@@ -515,7 +530,7 @@
     after = p_av[:1]
     for i in range(nw):
         ends_here = i == nw - 1
-        extra = -(-9 * 3 * nw // 16) * 16 if ends_here else 0
+        extra = -(-6 * 3 * nw // 16) * 16 if ends_here else 0
         g_parts = parts_of(G_WHOLE, "dp", (high + extra, some))
         m_own, m_send, du, send, sums = call(
             functools.partial(value_out_kernel, len(bw[i]), len(after), i * some), "value_out",
@@ -548,22 +563,20 @@
     )
 
     w_got = flip(w_send)
-    step = 1
-    while step < nz:
-        t_own = t_own + lax.ppermute(t_own, "z", [(i, i ^ step) for i in range(nz)])
-        step *= 2
-    t_got = flip(t_own)
     mine_of = 3 * width // nseq
     if mine_of % 128 == 0:
+        runs = cols // (ncore * mine_of)
+        lines = half + -(-6 * runs // 16) * 16
         sent = call(
-            join_kernel, "join", (w_own, w_got, t_own), [S((half, ncore * mine_of))] * nz, mm // 64,
+            join_kernel, "join", (w_own, w_got, t_own), [S((lines, ncore * mine_of))] * nz, mm // 64,
             [pltpu.VMEM((half, 3 * width), BF)],
         )
-        total, send = call(
-            functools.partial(sum_kernel, nz), "sum", swap(sent, "z"), [S((half, mine_of), F32)] * 2, mm // 64,
+        total, send, t_own = call(
+            functools.partial(sum_kernel, nz), "sum", (*swap(sent, "z"), in_grad),
+            [S((half, mine_of), F32)] * 2 + [S((3, cols), F32)], mm // 64,
         )
         w_in_grad, taps_grad = call(
-            functools.partial(last_kernel, factor), "last", (total, flip(send), t_own, t_got),
+            functools.partial(last_kernel, factor), "last", (total, flip(send), t_own, flip(t_own)),
             [S((high, mine_of), F32), S((3, 3 * width), F32)], mm // 64,
         )
     else:
@@ -573,7 +586,11 @@
             low, high = jnp.where(core == 0, own, got), jnp.where(core == 0, got, own)
             return jnp.concatenate([low, high], axis=2).reshape(-1, 3 * width)
 
-        taps_grad = joined(t_own, t_got) * factor
+        step = 1
+        while step < nz:
+            t_own = t_own + lax.ppermute(t_own, "z", [(i, i ^ step) for i in range(nz)])
+            step *= 2
+        taps_grad = joined(t_own, flip(t_own)) * factor
         sent = joined(w_own, w_got).reshape(half, nseq, mine_of).transpose(1, 0, 2)
         got = lax.all_to_all(sent, seq, 0, 0, tiled=True).reshape(nz, high, mine_of)
         w_in_grad = jnp.sum(got.astype(F32), axis=0) * factor

time: 193 us -> 179 us (0.927)
  waiting for transfers between devices: 74.7 us -> 63.7 us
  starting transfers between devices: 67.7 us -> 60.6 us
  local copies, waits for them, and re-layouts: 3.49 us -> 6.86 us
    ppermute x30, waiting for transfers between devices: 64.7 us -> 57 us  [swap(): lax.ppermute(parts[k], axis, [(i, i ^ k) for i in range(size)])]
    ppermute x30, starting transfers between devices: 60.1 us -> 53.1 us  [swap(): lax.ppermute(parts[k], axis, [(i, i ^ k) for i in range(size)])]
    ppermute x2 -> x0, waiting for transfers between devices: 5.52 us -> none  [shards(): t_own = t_own + lax.ppermute(t_own, 'z', [(i, i ^ step) for i in range(nz)])]
    unnamed x24 -> x28, local copies, waits for them, and re-layouts: 3.45 us -> 6.86 us
    ppermute x2 -> x0, starting transfers between devices: 3.3 us -> none  [shards(): t_own = t_own + lax.ppermute(t_own, 'z', [(i, i ^ step) for i in range(nz)])]
    ppermute x11, starting transfers between devices: 2.31 us -> 5.6 us  [flip(): return lax.ppermute(value, 'core', [(0, 1), (1, 0)])]
  transfers between devices with their start and end apart: 45 -> 43, of which waited for: 12 -> 14; matrix products, arithmetic and copies ran while one was open for 0% -> 0% of each run, Pallas kernels for 18% -> 15%
where the time goes in v3:
time: 179 us; the launch traced here: 177 us
  waiting for transfers between devices  63.7 us (36%)
  starting transfers between devices  60.6 us (34%)
  Pallas kernels  45.1 us (25%)
  local copies, waits for them, and re-layouts  6.86 us (4%)
    ppermute x30, waiting for transfers between devices, swap(): lax.ppermute(parts[k], axis, [(i, i ^ k) for i in range(size)])  57 us
    ppermute x30, starting transfers between devices, swap(): lax.ppermute(parts[k], axis, [(i, i ^ k) for i in range(size)])  53.1 us
    pallas_call x17, Pallas kernels, call(): pl.pallas_call(kernel, out_shape=outs, in_specs=[whole] * len(ins), out_s...  45.1 us
    unnamed x28, local copies, waits for them, and re-layouts  6.86 us
    ppermute x11, starting transfers between devices, flip(): return lax.ppermute(value, 'core', [(0, 1), (1, 0)])  5.6 us
    ppermute x2, waiting for transfers between devices, shards(): h1, h2 = (lax.ppermute(ends, seq, near), lax.ppermute(ends, seq, far))  4.85 us
  transfers between devices with their start and end apart: 43, of which 14 were waited for; matrix products, arithmetic and copies ran while one was open for 0% of the time, Pallas kernels for 15%

profile of v3, /device:TPU:0, one launch (start us, length us, event | category | flops | bytes accessed | tf_op | source)
XLA Modules:
  0.0 177.2 jit_solution(2487085801673247825)
XLA Ops:
  5.7 4.8 %collective-permute-done.2.h2_ref.refs_11_ = bf16[16,1024]{1,0:T(8,128)(2,1)S(1)} collective-permute-done((bf16[16,1024]{1,0:T(8,128)(2,1)S(1)}, bf16[16,1024]{1,0:T(8,128)(2,1)S(1)}, u32[]{:S(2)}, u32[]{:S(2)}) %collective-permute-start.2) | collective-permute-done | bytes 32800 | tf_op jit(solution)/shard_map/ppermute | solution.py:476
  11.6 6.3 %grad_block.1 = (bf16[4,64,512]{2,1,0:T(8,128)(2,1)S(1)}, bf16[4,64,512]{2,1,0:T(8,128)(2,1)S(1)}, bf16[4,64,512]{2,1,0:T(8,128)(2,1)S(1)}, bf16[4,64,512]{2,1,0...) custom-call(bf16[512,1024]{1,0:T(8,128)(2,1)S(1)} %bitcast.8, ...), custom_call_target="tpu_custom_call" | custom-call | flops 1342177280 | bytes 14929920 | tf_op jit(solution)/shard_map/grad_block/pallas_call | solution.py:444
  17.9 3.2 %collective-permute-start.10 = (bf16[16,32,512]{2,1,0:T(8,128)(2,1)S(1)}, bf16[16,32,512]{2,1,0:T(8,128)(2,1)S(1)}, u32[]{:S(2)}, u32[]{:S(2)}) collective-permute-start(bf16[16,32,512]{2,1,0:T(8,128)(2,1)S(1)} %get-tuple-element.90), channel_id=1, source_target_pairs={{0,1},{1,0},{2,3},{3,2},{4,5},{5,4},{6,7},{7,6},{8,9},{9,8},{10,11... | collective-permute-start | bytes 1572872 | tf_op jit(solution)/shard_map/ppermute | solution.py:456
  21.0 1.6 collective-permute-start.7
  22.6 1.8 %collective-permute-start.8 = (bf16[4,64,512]{2,1,0:T(8,128)(2,1)S(1)}, bf16[4,64,512]{2,1,0:T(8,128)(2,1)S(1)}, u32[]{:S(2)}, u32[]{:S(2)}) collective-permute-start(bf16[4,64,512]{2,1,0:T(8,128)(2,1)S(1)} %get-tuple-element.87), channel_id=1, source_target_pairs={{0,4},{2,6},{4,0},{6,2},{1,5},{3,7},{5,1},{7,3},{8,12},{10,14},{12... | collective-permute-start | bytes 786440 | tf_op jit(solution)/shard_map/ppermute | solution.py:463
  26.7 8.2 %value_block.1 = (bf16[4,64,256]{2,1,0:T(8,128)(2,1)S(1)}, bf16[4,64,256]{2,1,0:T(8,128)(2,1)S(1)}, bf16[4,64,256]{2,1,0:T(8,128)(2,1)S(1)}, bf16[4,64,256]{2,1,...) custom-call(bf16[512,1024]{1,0:T(8,128)(2,1)S(1)} %bitcast.9, ...), custom_call_target="tpu_custom_call" | custom-call | flops 2415919104 | bytes 13914112 | tf_op jit(solution)/shard_map/value_block/pallas_call | solution.py:444
  36.5 2.7 %collective-permute-start.5 = (bf16[4,64,256]{2,1,0:T(8,128)(2,1)S(1)}, bf16[4,64,256]{2,1,0:T(8,128)(2,1)S(1)}, u32[]{:S(2)}, u32[]{:S(2)}) collective-permute-start(bf16[4,64,256]{2,1,0:T(8,128)(2,1)S(1)} %get-tuple-element.83), channel_id=1, source_target_pairs={{0,4},{2,6},{4,0},{6,2},{1,5},{3,7},{5,1},{7,3},{8,12},{10,14},{12... | collective-permute-start | bytes 393224 | tf_op jit(solution)/shard_map/ppermute | solution.py:463
  39.2 4.7 %collective-permute-done.8.refs_2_ = bf16[4,64,512]{2,1,0:T(8,128)(2,1)S(1)} collective-permute-done((bf16[4,64,512]{2,1,0:T(8,128)(2,1)S(1)}, bf16[4,64,512]{2,1,0:T(8,128)(2,1)S(1)}, u32[]{:S(2)}, u32[]{:S(2)}) %collective-permute-start.8) | collective-permute-done | bytes 262176 | tf_op jit(solution)/shard_map/ppermute | solution.py:463
  44.0 3.0 %collective-permute-start.6 = (bf16[4,64,256]{2,1,0:T(8,128)(2,1)S(1)}, bf16[4,64,256]{2,1,0:T(8,128)(2,1)S(1)}, u32[]{:S(2)}, u32[]{:S(2)}) collective-permute-start(bf16[4,64,256]{2,1,0:T(8,128)(2,1)S(1)} %get-tuple-element.84), channel_id=1, source_target_pairs={{0,6},{2,4},{4,2},{6,0},{1,7},{3,5},{5,3},{7,1},{8,14},{10,12},{12... | collective-permute-start | bytes 393224 | tf_op jit(solution)/shard_map/ppermute | solution.py:463
  47.0 8.8 %collective-permute-start.17 = (bf16[4,64,256]{2,1,0:T(8,128)(2,1)S(1)}, bf16[4,64,256]{2,1,0:T(8,128)(2,1)S(1)}, u32[]{:S(2)}, u32[]{:S(2)}) collective-permute-start(bf16[4,64,256]{2,1,0:T(8,128)(2,1)S(1)} %get-tuple-element.100), channel_id=1, source_target_pairs={{0,2},{2,0},{4,6},{6,4},{1,3},{3,1},{5,7},{7,5},{8,10},{10,8},{12,... | collective-permute-start | bytes 393224 | tf_op jit(solution)/shard_map/ppermute | solution.py:463
  57.1 3.0 %collective-permute-start.15 = (bf16[272,512]{1,0:T(8,128)(2,1)S(1)}, bf16[272,512]{1,0:T(8,128)(2,1)S(1)}, u32[]{:S(2)}, u32[]{:S(2)}) collective-permute-start(bf16[272,512]{1,0:T(8,128)(2,1)S(1)} %get-tuple-element.97), channel_id=1, source_target_pairs={{0,4},{2,6},{4,0},{6,2},{1,5},{3,7},{5,1},{7,3},{8,12},{10,14},{12... | collective-permute-start | bytes 835592 | tf_op jit(solution)/shard_map/ppermute | solution.py:463
  66.0 27.4 %collective-permute-done.18.refs_2_ = bf16[4,64,256]{2,1,0:T(8,128)(2,1)S(1)} collective-permute-done((bf16[4,64,256]{2,1,0:T(8,128)(2,1)S(1)}, bf16[4,64,256]{2,1,0:T(8,128)(2,1)S(1)}, u32[]{:S(2)}, u32[]{:S(2)}) %collective-permute-start.18) | collective-permute-done | bytes 131104 | tf_op jit(solution)/shard_map/ppermute | solution.py:463
  94.3 10.7 %grad_out.1 = (bf16[1024,1024]{1,0:T(8,128)(2,1)}, bf16[512,1024]{1,0:T(8,128)(2,1)S(1)}, f32[3,1024]{1,0:T(4,128)S(1)}, bf16[256,1024]{1,0:T(8,128)(2,1)S(1)}, ...) custom-call(bf16[272,512]{1,0:T(8,128)(2,1)S(1)} %get-tuple-element.91.refs_4_.refs_0_, ...), custom_call_target="tpu_custom_call" | custom-call | flops 2147483 | bytes 10903 | tf_op jit(solution)/shard_map/grad_out/pallas_call | solution.py:444
  105.0 1.5 collective-permute-start.23
  106.5 1.6 collective-permute-start.24
  108.0 2.0 %collective-permute-start.11 = (bf16[272,256]{1,0:T(8,128)(2,1)S(1)}, bf16[272,256]{1,0:T(8,128)(2,1)S(1)}, u32[]{:S(2)}, u32[]{:S(2)}) collective-permute-start(bf16[272,256]{1,0:T(8,128)(2,1)S(1)} %get-tuple-element.93), channel_id=1, source_target_pairs={{0,2},{2,0},{4,6},{6,4},{1,3},{3,1},{5,7},{7,5},{8,10},{10,8},{12,... | collective-permute-start | bytes 417800 | tf_op jit(solution)/shard_map/ppermute | solution.py:463
  111.5 2.0 %collective-permute-done.11.refs_1_ = bf16[272,256]{1,0:T(8,128)(2,1)S(1)} collective-permute-done((bf16[272,256]{1,0:T(8,128)(2,1)S(1)}, bf16[272,256]{1,0:T(8,128)(2,1)S(1)}, u32[]{:S(2)}, u32[]{:S(2)}) %collective-permute-start.11) | collective-permute-done | bytes 139296 | tf_op jit(solution)/shard_map/ppermute | solution.py:463
  113.4 3.5 %collective-permute-start.13 = (bf16[272,256]{1,0:T(8,128)(2,1)S(1)}, bf16[272,256]{1,0:T(8,128)(2,1)S(1)}, u32[]{:S(2)}, u32[]{:S(2)}) collective-permute-start(bf16[272,256]{1,0:T(8,128)(2,1)S(1)} %get-tuple-element.95), channel_id=1, source_target_pairs={{0,6},{2,4},{4,2},{6,0},{1,7},{3,5},{5,3},{7,1},{8,14},{10,12},{12... | collective-permute-start | bytes 417800 | tf_op jit(solution)/shard_map/ppermute | solution.py:463
  116.9 4.1 %collective-permute-done.12.refs_2_ = bf16[272,256]{1,0:T(8,128)(2,1)S(1)} collective-permute-done((bf16[272,256]{1,0:T(8,128)(2,1)S(1)}, bf16[272,256]{1,0:T(8,128)(2,1)S(1)}, u32[]{:S(2)}, u32[]{:S(2)}) %collective-permute-start.12) | collective-permute-done | bytes 139296 | tf_op jit(solution)/shard_map/ppermute | solution.py:463
  121.0 2.0 %collective-permute-start.20 = (bf16[272,256]{1,0:T(8,128)(2,1)S(1)}, bf16[272,256]{1,0:T(8,128)(2,1)S(1)}, u32[]{:S(2)}, u32[]{:S(2)}) collective-permute-start(bf16[272,256]{1,0:T(8,128)(2,1)S(1)} %get-tuple-element.112), channel_id=1, source_target_pairs={{0,2},{2,0},{4,6},{6,4},{1,3},{3,1},{5,7},{7,5},{8,10},{10,8},{12,... | collective-permute-start | bytes 417800 | tf_op jit(solution)/shard_map/ppermute | solution.py:463
  124.5 3.1 %collective-permute-done.24.refs_1_.refs_2_ = bf16[256,1024]{1,0:T(8,128)(2,1)S(1)} collective-permute-done((bf16[256,1024]{1,0:T(8,128)(2,1)S(1)}, bf16[256,1024]{1,0:T(8,128)(2,1)S(1)}, u32[]{:S(2)}, u32[]{:S(2)}) %collective-permute-start.24) | collective-permute-done | bytes 524320 | tf_op jit(solution)/shard_map/ppermute | solution.py:463
  127.6 2.8 %collective-permute-start.22 = (bf16[272,256]{1,0:T(8,128)(2,1)S(1)}, bf16[272,256]{1,0:T(8,128)(2,1)S(1)}, u32[]{:S(2)}, u32[]{:S(2)}) collective-permute-start(bf16[272,256]{1,0:T(8,128)(2,1)S(1)} %get-tuple-element.114), channel_id=1, source_target_pairs={{0,6},{2,4},{4,2},{6,0},{1,7},{3,5},{5,3},{7,1},{8,14},{10,12},{12... | collective-permute-start | bytes 417800 | tf_op jit(solution)/shard_map/ppermute | solution.py:463
  132.7 2.7 %collective-permute-done.21.refs_2_ = bf16[272,256]{1,0:T(8,128)(2,1)S(1)} collective-permute-done((bf16[272,256]{1,0:T(8,128)(2,1)S(1)}, bf16[272,256]{1,0:T(8,128)(2,1)S(1)}, u32[]{:S(2)}, u32[]{:S(2)}) %collective-permute-start.21) | collective-permute-done | bytes 139296 | tf_op jit(solution)/shard_map/ppermute | solution.py:463
  135.4 1.4 value_out.3
  137.6 1.9 %collective-permute-start.34 = (bf16[304,256]{1,0:T(8,128)(2,1)S(1)}, bf16[304,256]{1,0:T(8,128)(2,1)S(1)}, u32[]{:S(2)}, u32[]{:S(2)}) collective-permute-start(bf16[304,256]{1,0:T(8,128)(2,1)S(1)} %get-tuple-element.137), channel_id=1, source_target_pairs={{0,8},{8,0},{16,24},{24,16},{1,9},{9,1},{17,25},{25,17},{2,10},{10... | collective-permute-start | bytes 466952 | tf_op jit(solution)/shard_map/ppermute | solution.py:463
  141.3 2.0 %collective-permute-done.32.refs_6_ = bf16[256,256]{1,0:T(8,128)(2,1)S(1)} collective-permute-done((bf16[256,256]{1,0:T(8,128)(2,1)S(1)}, bf16[256,256]{1,0:T(8,128)(2,1)S(1)}, u32[]{:S(2)}, u32[]{:S(2)}) %collective-permute-start.32) | collective-permute-done | bytes 131104 | tf_op jit(solution)/shard_map/ppermute | solution.py:463
  144.7 4.4 %collective-permute-done.33.refs_7_ = bf16[256,256]{1,0:T(8,128)(2,1)S(1)} collective-permute-done((bf16[256,256]{1,0:T(8,128)(2,1)S(1)}, bf16[256,256]{1,0:T(8,128)(2,1)S(1)}, u32[]{:S(2)}, u32[]{:S(2)}) %collective-permute-start.33) | collective-permute-done | bytes 131104 | tf_op jit(solution)/shard_map/ppermute | solution.py:463
  152.2 2.6 %collective-permute-start.38 = (bf16[144,768]{1,0:T(8,128)(2,1)S(1)}, bf16[144,768]{1,0:T(8,128)(2,1)S(1)}, u32[]{:S(2)}, u32[]{:S(2)}) collective-permute-start(bf16[144,768]{1,0:T(8,128)(2,1)S(1)} %get-tuple-element.144), channel_id=1, source_target_pairs={{0,2},{2,0},{4,6},{6,4},{1,3},{3,1},{5,7},{7,5},{8,10},{10,8},{12,... | collective-permute-start | bytes 663560 | tf_op jit(solution)/shard_map/ppermute | solution.py:463
  154.8 2.7 %collective-permute-start.40 = (bf16[144,768]{1,0:T(8,128)(2,1)S(1)}, bf16[144,768]{1,0:T(8,128)(2,1)S(1)}, u32[]{:S(2)}, u32[]{:S(2)}) collective-permute-start(bf16[144,768]{1,0:T(8,128)(2,1)S(1)} %get-tuple-element.146), channel_id=1, source_target_pairs={{0,6},{2,4},{4,2},{6,0},{1,7},{3,5},{5,3},{7,1},{8,14},{10,12},{12... | collective-permute-start | bytes 663560 | tf_op jit(solution)/shard_map/ppermute | solution.py:463
  157.5 5.4 %in_first.1.refs_9_ = f32[512,1024]{1,0:T(8,128)S(1)} custom-call(bf16[1024,1024]{1,0:T(8,128)(2,1)S(1)} %copy-done.4, bf16[512,1024]{1,0:T(8,128)(2,1)S(1)} %collective-permute-done.29.got_ref, bf16[1024,3072]{1,0:T(8,128)(2,1)} %refs_8_.8, bf16[304,256]{1,0:T(8,128)(2,1)S(1)} %get-tuple-element.130.after_ref.refs_10_.refs_8_), custom_call_target="tpu_custom_call" | custom-call | flops 2147483648 | bytes 11689984 | tf_op jit(solution)/shard_map/in_first/pallas_call | solution.py:444
  163.0 5.4 %in_last.1 = (bf16[512,1024]{1,0:T(8,128)(2,1)}, bf16[512,1024]{1,0:T(8,128)(2,1)}) custom-call(bf16[1024,256]{1,0:T(8,128)(2,1)S(1)} %get-tuple-element.111.refs_3_.refs_0_, bf16[1024,256]{1,0:T(8,128)(2,1)S(1)} %get-tuple-element.118.refs_2_.refs_1_, bf16[512,256]{1,0:T(8,128)(2,1)S(1)} %collective-permute-done.25.refs_2_, ...), custom_call_target="tpu_custom_call" | custom-call | flops 1073741824 | bytes 13262848 | tf_op jit(solution)/shard_map/in_last/pallas_call | solution.py:444
  168.4 5.1 %collective-permute-done.39.refs_2_ = bf16[144,768]{1,0:T(8,128)(2,1)S(1)} collective-permute-done((bf16[144,768]{1,0:T(8,128)(2,1)S(1)}, bf16[144,768]{1,0:T(8,128)(2,1)S(1)}, u32[]{:S(2)}, u32[]{:S(2)}) %collective-permute-start.39) | collective-permute-done | bytes 221216 | tf_op jit(solution)/shard_map/ppermute | solution.py:463
  (99 shorter events, 33.7 us)
Async XLA Ops:
  0.6 10.0 %collective-permute-start = (bf16[512,1024]{1,0:T(8,128)(2,1)}, bf16[512,1024]{1,0:T(8,128)(2,1)S(1)}, u32[]{:S(2)}, u32[]{:S(2)}) collective-permute-start(bf16[512,1024]{1,0:T(8,128)(2,1)} %bitcast.6), channel_id=1, source_target_pairs={{0,1},{1,0},{2,3},{3,2},{4,5},{5,4},{6,7},{7,6},{8,9},{9,8},{10,11... | collective-permute-start | bytes 3145736 | tf_op jit(solution)/shard_map/ppermute | solution.py:456
  17.9 37.9 %collective-permute-start.10 = (bf16[16,32,512]{2,1,0:T(8,128)(2,1)S(1)}, bf16[16,32,512]{2,1,0:T(8,128)(2,1)S(1)}, u32[]{:S(2)}, u32[]{:S(2)}) collective-permute-start(bf16[16,32,512]{2,1,0:T(8,128)(2,1)S(1)} %get-tuple-element.90), channel_id=1, source_target_pairs={{0,1},{1,0},{2,3},{3,2},{4,5},{5,4},{6,7},{7,6},{8,9},{9,8},{10,11... | collective-permute-start | bytes 1572872 | tf_op jit(solution)/shard_map/ppermute | solution.py:456
  21.0 15.5 %collective-permute-start.7 = (bf16[4,64,512]{2,1,0:T(8,128)(2,1)S(1)}, bf16[4,64,512]{2,1,0:T(8,128)(2,1)S(1)}, u32[]{:S(2)}, u32[]{:S(2)}) collective-permute-start(bf16[4,64,512]{2,1,0:T(8,128)(2,1)S(1)} %get-tuple-element.86), channel_id=1, source_target_pairs={{0,2},{2,0},{4,6},{6,4},{1,3},{3,1},{5,7},{7,5},{8,10},{10,8},{12,... | collective-permute-start | bytes 786440 | tf_op jit(solution)/shard_map/ppermute | solution.py:463
  22.6 21.4 %collective-permute-start.8 = (bf16[4,64,512]{2,1,0:T(8,128)(2,1)S(1)}, bf16[4,64,512]{2,1,0:T(8,128)(2,1)S(1)}, u32[]{:S(2)}, u32[]{:S(2)}) collective-permute-start(bf16[4,64,512]{2,1,0:T(8,128)(2,1)S(1)} %get-tuple-element.87), channel_id=1, source_target_pairs={{0,4},{2,6},{4,0},{6,2},{1,5},{3,7},{5,1},{7,3},{8,12},{10,14},{12... | collective-permute-start | bytes 786440 | tf_op jit(solution)/shard_map/ppermute | solution.py:463
  24.4 22.6 %collective-permute-start.9 = (bf16[4,64,512]{2,1,0:T(8,128)(2,1)S(1)}, bf16[4,64,512]{2,1,0:T(8,128)(2,1)S(1)}, u32[]{:S(2)}, u32[]{:S(2)}) collective-permute-start(bf16[4,64,512]{2,1,0:T(8,128)(2,1)S(1)} %get-tuple-element.88), channel_id=1, source_target_pairs={{0,6},{2,4},{4,2},{6,0},{1,7},{3,5},{5,3},{7,1},{8,14},{10,12},{12... | collective-permute-start | bytes 786440 | tf_op jit(solution)/shard_map/ppermute | solution.py:463
  35.9 21.3 %collective-permute-start.4 = (bf16[4,64,256]{2,1,0:T(8,128)(2,1)S(1)}, bf16[4,64,256]{2,1,0:T(8,128)(2,1)S(1)}, u32[]{:S(2)}, u32[]{:S(2)}) collective-permute-start(bf16[4,64,256]{2,1,0:T(8,128)(2,1)S(1)} %get-tuple-element.82), channel_id=1, source_target_pairs={{0,2},{2,0},{4,6},{6,4},{1,3},{3,1},{5,7},{7,5},{8,10},{10,8},{12,... | collective-permute-start | bytes 393224 | tf_op jit(solution)/shard_map/ppermute | solution.py:463
  36.5 23.6 %collective-permute-start.5 = (bf16[4,64,256]{2,1,0:T(8,128)(2,1)S(1)}, bf16[4,64,256]{2,1,0:T(8,128)(2,1)S(1)}, u32[]{:S(2)}, u32[]{:S(2)}) collective-permute-start(bf16[4,64,256]{2,1,0:T(8,128)(2,1)S(1)} %get-tuple-element.83), channel_id=1, source_target_pairs={{0,4},{2,6},{4,0},{6,2},{1,5},{3,7},{5,1},{7,3},{8,12},{10,14},{12... | collective-permute-start | bytes 393224 | tf_op jit(solution)/shard_map/ppermute | solution.py:463
  44.0 17.5 %collective-permute-start.6 = (bf16[4,64,256]{2,1,0:T(8,128)(2,1)S(1)}, bf16[4,64,256]{2,1,0:T(8,128)(2,1)S(1)}, u32[]{:S(2)}, u32[]{:S(2)}) collective-permute-start(bf16[4,64,256]{2,1,0:T(8,128)(2,1)S(1)} %get-tuple-element.84), channel_id=1, source_target_pairs={{0,6},{2,4},{4,2},{6,0},{1,7},{3,5},{5,3},{7,1},{8,14},{10,12},{12... | collective-permute-start | bytes 393224 | tf_op jit(solution)/shard_map/ppermute | solution.py:463
  47.0 16.8 %collective-permute-start.17 = (bf16[4,64,256]{2,1,0:T(8,128)(2,1)S(1)}, bf16[4,64,256]{2,1,0:T(8,128)(2,1)S(1)}, u32[]{:S(2)}, u32[]{:S(2)}) collective-permute-start(bf16[4,64,256]{2,1,0:T(8,128)(2,1)S(1)} %get-tuple-element.100), channel_id=1, source_target_pairs={{0,2},{2,0},{4,6},{6,4},{1,3},{3,1},{5,7},{7,5},{8,10},{10,8},{12,... | collective-permute-start | bytes 393224 | tf_op jit(solution)/shard_map/ppermute | solution.py:463
  57.0 37.2 %collective-permute-start.14 = (bf16[272,512]{1,0:T(8,128)(2,1)S(1)}, bf16[272,512]{1,0:T(8,128)(2,1)S(1)}, u32[]{:S(2)}, u32[]{:S(2)}) collective-permute-start(bf16[272,512]{1,0:T(8,128)(2,1)S(1)} %get-tuple-element.96), channel_id=1, source_target_pairs={{0,2},{2,0},{4,6},{6,4},{1,3},{3,1},{5,7},{7,5},{8,10},{10,8},{12,... | collective-permute-start | bytes 835592 | tf_op jit(solution)/shard_map/ppermute | solution.py:463
  57.1 37.1 %collective-permute-start.15 = (bf16[272,512]{1,0:T(8,128)(2,1)S(1)}, bf16[272,512]{1,0:T(8,128)(2,1)S(1)}, u32[]{:S(2)}, u32[]{:S(2)}) collective-permute-start(bf16[272,512]{1,0:T(8,128)(2,1)S(1)} %get-tuple-element.97), channel_id=1, source_target_pairs={{0,4},{2,6},{4,0},{6,2},{1,5},{3,7},{5,1},{7,3},{8,12},{10,14},{12... | collective-permute-start | bytes 835592 | tf_op jit(solution)/shard_map/ppermute | solution.py:463
  60.2 34.1 %collective-permute-start.16 = (bf16[272,512]{1,0:T(8,128)(2,1)S(1)}, bf16[272,512]{1,0:T(8,128)(2,1)S(1)}, u32[]{:S(2)}, u32[]{:S(2)}) collective-permute-start(bf16[272,512]{1,0:T(8,128)(2,1)S(1)} %get-tuple-element.98), channel_id=1, source_target_pairs={{0,6},{2,4},{4,2},{6,0},{1,7},{3,5},{5,3},{7,1},{8,14},{10,12},{12... | collective-permute-start | bytes 835592 | tf_op jit(solution)/shard_map/ppermute | solution.py:463
  61.5 32.0 %collective-permute-start.18 = (bf16[4,64,256]{2,1,0:T(8,128)(2,1)S(1)}, bf16[4,64,256]{2,1,0:T(8,128)(2,1)S(1)}, u32[]{:S(2)}, u32[]{:S(2)}) collective-permute-start(bf16[4,64,256]{2,1,0:T(8,128)(2,1)S(1)} %get-tuple-element.101), channel_id=1, source_target_pairs={{0,4},{2,6},{4,0},{6,2},{1,5},{3,7},{5,1},{7,3},{8,12},{10,14},{12... | collective-permute-start | bytes 393224 | tf_op jit(solution)/shard_map/ppermute | solution.py:463
  63.8 29.6 %collective-permute-start.19 = (bf16[4,64,256]{2,1,0:T(8,128)(2,1)S(1)}, bf16[4,64,256]{2,1,0:T(8,128)(2,1)S(1)}, u32[]{:S(2)}, u32[]{:S(2)}) collective-permute-start(bf16[4,64,256]{2,1,0:T(8,128)(2,1)S(1)} %get-tuple-element.102), channel_id=1, source_target_pairs={{0,6},{2,4},{4,2},{6,0},{1,7},{3,5},{5,3},{7,1},{8,14},{10,12},{12... | collective-permute-start | bytes 393224 | tf_op jit(solution)/shard_map/ppermute | solution.py:463
  105.0 18.1 %collective-permute-start.23 = (bf16[256,1024]{1,0:T(8,128)(2,1)S(1)}, bf16[256,1024]{1,0:T(8,128)(2,1)S(1)}, u32[]{:S(2)}, u32[]{:S(2)}) collective-permute-start(bf16[256,1024]{1,0:T(8,128)(2,1)S(1)} %get-tuple-element.115), channel_id=1, source_target_pairs={{0,8},{8,0},{16,24},{24,16},{1,9},{9,1},{17,25},{25,17},{2,10},{10... | collective-permute-start | bytes 1572872 | tf_op jit(solution)/shard_map/ppermute | solution.py:463
  106.5 21.2 %collective-permute-start.24 = (bf16[256,1024]{1,0:T(8,128)(2,1)S(1)}, bf16[256,1024]{1,0:T(8,128)(2,1)S(1)}, u32[]{:S(2)}, u32[]{:S(2)}) collective-permute-start(bf16[256,1024]{1,0:T(8,128)(2,1)S(1)} %get-tuple-element.116), channel_id=1, source_target_pairs={{0,16},{8,24},{16,0},{24,8},{1,17},{9,25},{17,1},{25,9},{2,18},{10... | collective-permute-start | bytes 1572872 | tf_op jit(solution)/shard_map/ppermute | solution.py:463
  110.0 11.0 %collective-permute-start.12 = (bf16[272,256]{1,0:T(8,128)(2,1)S(1)}, bf16[272,256]{1,0:T(8,128)(2,1)S(1)}, u32[]{:S(2)}, u32[]{:S(2)}) collective-permute-start(bf16[272,256]{1,0:T(8,128)(2,1)S(1)} %get-tuple-element.94), channel_id=1, source_target_pairs={{0,4},{2,6},{4,0},{6,2},{1,5},{3,7},{5,1},{7,3},{8,12},{10,14},{12... | collective-permute-start | bytes 417800 | tf_op jit(solution)/shard_map/ppermute | solution.py:463
  111.0 28.5 %collective-permute-start.30 = (bf16[256,1024]{1,0:T(8,128)(2,1)S(1)}, bf16[256,1024]{1,0:T(8,128)(2,1)S(1)}, u32[]{:S(2)}, u32[]{:S(2)}) collective-permute-start(bf16[256,1024]{1,0:T(8,128)(2,1)S(1)} %get-tuple-element.133), channel_id=1, source_target_pairs={{0,24},{8,16},{16,8},{24,0},{1,25},{9,17},{17,9},{25,1},{2,26},{10... | collective-permute-start | bytes 1572872 | tf_op jit(solution)/shard_map/ppermute | solution.py:463
  121.0 33.8 %collective-permute-start.29 = (bf16[512,1024]{1,0:T(8,128)(2,1)S(1)}, bf16[512,1024]{1,0:T(8,128)(2,1)S(1)}, u32[]{:S(2)}, u32[]{:S(2)}) collective-permute-start(bf16[512,1024]{1,0:T(8,128)(2,1)S(1)} %get-tuple-element.126), channel_id=1, source_target_pairs={{0,1},{1,0},{2,3},{3,2},{4,5},{5,4},{6,7},{7,6},{8,9},{9,8},{10,11... | collective-permute-start | bytes 3145736 | tf_op jit(solution)/shard_map/ppermute | solution.py:456
  121.0 11.6 %collective-permute-start.20 = (bf16[272,256]{1,0:T(8,128)(2,1)S(1)}, bf16[272,256]{1,0:T(8,128)(2,1)S(1)}, u32[]{:S(2)}, u32[]{:S(2)}) collective-permute-start(bf16[272,256]{1,0:T(8,128)(2,1)S(1)} %get-tuple-element.112), channel_id=1, source_target_pairs={{0,2},{2,0},{4,6},{6,4},{1,3},{3,1},{5,7},{7,5},{8,10},{10,8},{12,... | collective-permute-start | bytes 417800 | tf_op jit(solution)/shard_map/ppermute | solution.py:463
  123.1 12.3 %collective-permute-start.21 = (bf16[272,256]{1,0:T(8,128)(2,1)S(1)}, bf16[272,256]{1,0:T(8,128)(2,1)S(1)}, u32[]{:S(2)}, u32[]{:S(2)}) collective-permute-start(bf16[272,256]{1,0:T(8,128)(2,1)S(1)} %get-tuple-element.113), channel_id=1, source_target_pairs={{0,4},{2,6},{4,0},{6,2},{1,5},{3,7},{5,1},{7,3},{8,12},{10,14},{12... | collective-permute-start | bytes 417800 | tf_op jit(solution)/shard_map/ppermute | solution.py:463
  127.6 7.8 %collective-permute-start.22 = (bf16[272,256]{1,0:T(8,128)(2,1)S(1)}, bf16[272,256]{1,0:T(8,128)(2,1)S(1)}, u32[]{:S(2)}, u32[]{:S(2)}) collective-permute-start(bf16[272,256]{1,0:T(8,128)(2,1)S(1)} %get-tuple-element.114), channel_id=1, source_target_pairs={{0,6},{2,4},{4,2},{6,0},{1,7},{3,5},{5,3},{7,1},{8,14},{10,12},{12... | collective-permute-start | bytes 417800 | tf_op jit(solution)/shard_map/ppermute | solution.py:463
  132.6 7.6 %collective-permute-start.31 = (bf16[256,256]{1,0:T(8,128)(2,1)S(1)}, bf16[256,256]{1,0:T(8,128)(2,1)S(1)}, u32[]{:S(2)}, u32[]{:S(2)}) collective-permute-start(bf16[256,256]{1,0:T(8,128)(2,1)S(1)} %get-tuple-element.134), channel_id=1, source_target_pairs={{0,8},{8,0},{16,24},{24,16},{1,9},{9,1},{17,25},{25,17},{2,10},{10... | collective-permute-start | bytes 393224 | tf_op jit(solution)/shard_map/ppermute | solution.py:463
  135.4 7.9 %collective-permute-start.32 = (bf16[256,256]{1,0:T(8,128)(2,1)S(1)}, bf16[256,256]{1,0:T(8,128)(2,1)S(1)}, u32[]{:S(2)}, u32[]{:S(2)}) collective-permute-start(bf16[256,256]{1,0:T(8,128)(2,1)S(1)} %get-tuple-element.135), channel_id=1, source_target_pairs={{0,16},{8,24},{16,0},{24,8},{1,17},{9,25},{17,1},{25,9},{2,18},{10... | collective-permute-start | bytes 393224 | tf_op jit(solution)/shard_map/ppermute | solution.py:463
  137.6 11.5 %collective-permute-start.34 = (bf16[304,256]{1,0:T(8,128)(2,1)S(1)}, bf16[304,256]{1,0:T(8,128)(2,1)S(1)}, u32[]{:S(2)}, u32[]{:S(2)}) collective-permute-start(bf16[304,256]{1,0:T(8,128)(2,1)S(1)} %get-tuple-element.137), channel_id=1, source_target_pairs={{0,8},{8,0},{16,24},{24,16},{1,9},{9,1},{17,25},{25,17},{2,10},{10... | collective-permute-start | bytes 466952 | tf_op jit(solution)/shard_map/ppermute | solution.py:463
  139.5 9.6 %collective-permute-start.35 = (bf16[304,256]{1,0:T(8,128)(2,1)S(1)}, bf16[304,256]{1,0:T(8,128)(2,1)S(1)}, u32[]{:S(2)}, u32[]{:S(2)}) collective-permute-start(bf16[304,256]{1,0:T(8,128)(2,1)S(1)} %get-tuple-element.138), channel_id=1, source_target_pairs={{0,16},{8,24},{16,0},{24,8},{1,17},{9,25},{17,1},{25,9},{2,18},{10... | collective-permute-start | bytes 466952 | tf_op jit(solution)/shard_map/ppermute | solution.py:463
  140.2 8.9 %collective-permute-start.36 = (bf16[304,256]{1,0:T(8,128)(2,1)S(1)}, bf16[304,256]{1,0:T(8,128)(2,1)S(1)}, u32[]{:S(2)}, u32[]{:S(2)}) collective-permute-start(bf16[304,256]{1,0:T(8,128)(2,1)S(1)} %get-tuple-element.139), channel_id=1, source_target_pairs={{0,24},{8,16},{16,8},{24,0},{1,25},{9,17},{17,9},{25,1},{2,26},{10... | collective-permute-start | bytes 466952 | tf_op jit(solution)/shard_map/ppermute | solution.py:463
  150.7 12.3 %collective-permute-start.26 = (bf16[512,256]{1,0:T(8,128)(2,1)S(1)}, bf16[512,256]{1,0:T(8,128)(2,1)S(1)}, u32[]{:S(2)}, u32[]{:S(2)}) collective-permute-start(bf16[512,256]{1,0:T(8,128)(2,1)S(1)} %get-tuple-element.120), channel_id=1, source_target_pairs={{0,1},{1,0},{2,3},{3,2},{4,5},{5,4},{6,7},{7,6},{8,9},{9,8},{10,11... | collective-permute-start | bytes 786440 | tf_op jit(solution)/shard_map/ppermute | solution.py:456
  151.8 11.1 %collective-permute-start.28 = (bf16[512,256]{1,0:T(8,128)(2,1)S(1)}, bf16[512,256]{1,0:T(8,128)(2,1)S(1)}, u32[]{:S(2)}, u32[]{:S(2)}) collective-permute-start(bf16[512,256]{1,0:T(8,128)(2,1)S(1)} %get-tuple-element.124), channel_id=1, source_target_pairs={{0,1},{1,0},{2,3},{3,2},{4,5},{5,4},{6,7},{7,6},{8,9},{9,8},{10,11... | collective-permute-start | bytes 786440 | tf_op jit(solution)/shard_map/ppermute | solution.py:456
  152.2 16.2 %collective-permute-start.38 = (bf16[144,768]{1,0:T(8,128)(2,1)S(1)}, bf16[144,768]{1,0:T(8,128)(2,1)S(1)}, u32[]{:S(2)}, u32[]{:S(2)}) collective-permute-start(bf16[144,768]{1,0:T(8,128)(2,1)S(1)} %get-tuple-element.144), channel_id=1, source_target_pairs={{0,2},{2,0},{4,6},{6,4},{1,3},{3,1},{5,7},{7,5},{8,10},{10,8},{12,... | collective-permute-start | bytes 663560 | tf_op jit(solution)/shard_map/ppermute | solution.py:463
  154.8 18.7 %collective-permute-start.39 = (bf16[144,768]{1,0:T(8,128)(2,1)S(1)}, bf16[144,768]{1,0:T(8,128)(2,1)S(1)}, u32[]{:S(2)}, u32[]{:S(2)}) collective-permute-start(bf16[144,768]{1,0:T(8,128)(2,1)S(1)} %get-tuple-element.145), channel_id=1, source_target_pairs={{0,4},{2,6},{4,0},{6,2},{1,5},{3,7},{5,1},{7,3},{8,12},{10,14},{12... | collective-permute-start | bytes 663560 | tf_op jit(solution)/shard_map/ppermute | solution.py:463
  154.8 18.7 %collective-permute-start.40 = (bf16[144,768]{1,0:T(8,128)(2,1)S(1)}, bf16[144,768]{1,0:T(8,128)(2,1)S(1)}, u32[]{:S(2)}, u32[]{:S(2)}) collective-permute-start(bf16[144,768]{1,0:T(8,128)(2,1)S(1)} %get-tuple-element.146), channel_id=1, source_target_pairs={{0,6},{2,4},{4,2},{6,0},{1,7},{3,5},{5,3},{7,1},{8,14},{10,12},{12... | collective-permute-start | bytes 663560 | tf_op jit(solution)/shard_map/ppermute | solution.py:463
  (25 other events, 235.2 us)

commit v4 on v3

--- a/solution.py
+++ b/solution.py
@@ -15,7 +15,7 @@
 EDGE = 16
 NW = 2
 SHADE = 1000
-AV_DONE = 3
+AV_DONE = 2
 E_WHOLE, W_WHOLE, AV_WHOLE, G_WHOLE = False, False, False, False
 F32 = jnp.float32
 PARAMS = dict(vmem_limit_bytes=48 * 1024 * 1024)
@@ -120,9 +120,9 @@
 
 
 def grad_block_kernel(
-    n, x_ref, xs_ref, h1_ref, h2_ref, w_ref, taps_ref, og_ref, ogs_ref, tq_ref, filt_ref, *refs
+    n, x_ref, xs_ref, h1_ref, h2_ref, w_ref, taps_ref, og_ref, ogs_ref, tq_ref, *refs
 ):
-    outs, (z_ref, zh_ref, og_all_ref, send_ref, hold) = refs[:n], refs[n:]
+    outs, (z_ref, zh_ref, og_all_ref, hold) = refs[:n], refs[n:]
     core, tok = lax.axis_index("core"), x_ref.shape[0]
     width = z_ref.shape[1]
     og_all_ref[part_of(core, tok), :] = og_ref[:, part_of(core, width)]
@@ -135,7 +135,6 @@
         e4 = (og_all_ref[:, here].astype(F32) * g).astype(BF)
         put_blocks(tq_ref[...], e4, hold, here)
     hand_rows(hold, outs, pl.ds(0, width))
-    send_ref[...] = filt_ref[:, :, part_of(1 - core, width)]
 
 
 def value_block_kernel(
@@ -340,7 +339,7 @@
 
 def in_last_kernel(nw, *refs):
     dus, gots, owns, others = (refs[i * nw : (i + 1) * nw] for i in range(4))
-    w_ref, acc_ref, after_ref, out_ref, mixed_ref = refs[4 * nw :]
+    w_ref, acc_ref, after_ref, out_ref, mixed_ref, done_ref = refs[4 * nw :]
     core, half = lax.axis_index("core"), w_ref.shape[1] // 6
     tok, width = gots[0].shape
     total = acc_ref[...]
@@ -354,6 +353,7 @@
             at = pl.multiple_of(owner * half + i * width, 128)
             mixed_ref[:, pl.ds(at, width)] = ref[...]
     out_ref[...] = total.astype(BF)
+    done_ref[...] = jnp.zeros(done_ref.shape, F32)
 
 
 def add_all(values):
@@ -481,9 +481,9 @@
 
     act, edge = S((count, wide)), S((EDGE, wide))
     e_parts = parts_of(E_WHOLE, "z", (blocks, rows, wide))
-    *he, zg, zhg, og_all, filt_send = call(
+    *he, zg, zhg, og_all = call(
         functools.partial(grad_block_kernel, len(e_parts)), "grad_block",
-        (x, xs, h1, h2, w_in, taps, og, ogs, tq, filt), e_parts + [act, edge, act, S((span, each, wide))],
+        (x, xs, h1, h2, w_in, taps, og, ogs, tq), e_parts + [act, edge, act],
         mm + mm // 4, [hold_of(wide)],
     )
     ce = swap(he, "z")
@@ -496,7 +496,7 @@
         2 * mm + mm // 4, [hold_of(wide)],
     )
     cw = [swap(hw[i * len(w_parts) : (i + 1) * len(w_parts)], "z") for i in range(nw)]
-    filts = flip(filt_send)
+    filts = flip(lax.dynamic_slice_in_dim(filt, (1 - core) * wide, wide, axis=2))
 
     def span_step(parts, off, *after):
         cols = parts[0].shape[-1]
@@ -551,9 +551,9 @@
         others.append(flip(m_send))
         after, behind = p_g[:1], p_g[:1]
     acc = call(in_first_kernel, "in_first", (du_av, got_av, w_in, *behind), [S((tok, width), F32)], 2 * mm)[0]
-    in_grad, mixed = call(
+    in_grad, mixed, done = call(
         functools.partial(in_last_kernel, nw), "in_last",
-        (*dus, *gots, *owns, *others, w_in, acc, *behind), [S((tok, width))] * 2, mm,
+        (*dus, *gots, *owns, *others, w_in, acc, *behind), [S((tok, width))] * 2 + [S((8, 128), F32)], mm,
     )
 
     cols, half = 3 * wide, high // ncore
@@ -572,7 +572,7 @@
             [pltpu.VMEM((half, 3 * width), BF)],
         )
         total, send, t_own = call(
-            functools.partial(sum_kernel, nz), "sum", (*swap(sent, "z"), in_grad),
+            functools.partial(sum_kernel, nz), "sum", (*swap(sent, "z"), done),
             [S((half, mine_of), F32)] * 2 + [S((3, cols), F32)], mm // 64,
         )
         w_in_grad, taps_grad = call(

time: 179 us -> 178 us (level)
  starting transfers between devices: 60.6 us -> 68.5 us
  waiting for transfers between devices: 63.7 us -> 58.1 us
  local copies, waits for them, and re-layouts: 6.86 us -> 3.49 us
    ppermute x30, starting transfers between devices: 53.1 us -> 63.7 us  [swap(): lax.ppermute(parts[k], axis, [(i, i ^ k) for i in range(size)])]
    ppermute x30, waiting for transfers between devices: 57 us -> 51.8 us  [swap(): lax.ppermute(parts[k], axis, [(i, i ^ k) for i in range(size)])]
    unnamed x28 -> x24, local copies, waits for them, and re-layouts: 6.86 us -> 3.45 us
    ppermute x11, starting transfers between devices: 5.6 us -> 2.88 us  [flip(): return lax.ppermute(value, 'core', [(0, 1), (1, 0)])]
  transfers between devices with their start and end apart: 43 -> 43, of which waited for: 14 -> 11; matrix products, arithmetic and copies ran while one was open for 0% -> 0% of each run, Pallas kernels for 15% -> 19%
where the time goes in v4:
time: 178 us; the launch traced here: 176 us
  starting transfers between devices  68.5 us (38%)
  waiting for transfers between devices  58.1 us (33%)
  Pallas kernels  45.1 us (25%)
  local copies, waits for them, and re-layouts  3.49 us (2%)
    ppermute x30, starting transfers between devices, swap(): lax.ppermute(parts[k], axis, [(i, i ^ k) for i in range(size)])  63.7 us
    ppermute x30, waiting for transfers between devices, swap(): lax.ppermute(parts[k], axis, [(i, i ^ k) for i in range(size)])  51.8 us
    pallas_call x17, Pallas kernels, call(): pl.pallas_call(kernel, out_shape=outs, in_specs=[whole] * len(ins), out_s...  45.1 us
    ppermute x2, waiting for transfers between devices, shards(): h1, h2 = (lax.ppermute(ends, seq, near), lax.ppermute(ends, seq, far))  4.49 us
  transfers between devices with their start and end apart: 43, of which 11 were waited for; matrix products, arithmetic and copies ran while one was open for 0% of the time, Pallas kernels for 19%

profile of v4, /device:TPU:0, one launch (start us, length us, event | category | flops | bytes accessed | tf_op | source)
XLA Modules:
  0.0 176.1 jit_solution(1590590357716323150)
XLA Ops:
  7.0 4.5 %collective-permute-done.2.h2_ref.refs_11_ = bf16[16,1024]{1,0:T(8,128)(2,1)S(1)} collective-permute-done((bf16[16,1024]{1,0:T(8,128)(2,1)S(1)}, bf16[16,1024]{1,0:T(8,128)(2,1)S(1)}, u32[]{:S(2)}, u32[]{:S(2)}) %collective-permute-start.2) | collective-permute-done | bytes 32800 | tf_op jit(solution)/shard_map/ppermute | solution.py:476
  11.6 5.8 %grad_block.1 = (bf16[4,64,512]{2,1,0:T(8,128)(2,1)S(1)}, bf16[4,64,512]{2,1,0:T(8,128)(2,1)S(1)}, bf16[4,64,512]{2,1,0:T(8,128)(2,1)S(1)}, bf16[4,64,512]{2,1,0...) custom-call(bf16[512,1024]{1,0:T(8,128)(2,1)S(1)} %bitcast.8, ...), custom_call_target="tpu_custom_call" | custom-call | flops 1342177280 | bytes 13357056 | tf_op jit(solution)/shard_map/grad_block/pallas_call | solution.py:444
  17.3 3.4 %collective-permute-start.7 = (bf16[4,64,512]{2,1,0:T(8,128)(2,1)S(1)}, bf16[4,64,512]{2,1,0:T(8,128)(2,1)S(1)}, u32[]{:S(2)}, u32[]{:S(2)}) collective-permute-start(bf16[4,64,512]{2,1,0:T(8,128)(2,1)S(1)} %get-tuple-element.86), channel_id=1, source_target_pairs={{0,2},{2,0},{4,6},{6,4},{1,3},{3,1},{5,7},{7,5},{8,10},{10,8},{12,... | collective-permute-start | bytes 786440 | tf_op jit(solution)/shard_map/ppermute | solution.py:463
  20.8 3.0 %collective-permute-start.8 = (bf16[4,64,512]{2,1,0:T(8,128)(2,1)S(1)}, bf16[4,64,512]{2,1,0:T(8,128)(2,1)S(1)}, u32[]{:S(2)}, u32[]{:S(2)}) collective-permute-start(bf16[4,64,512]{2,1,0:T(8,128)(2,1)S(1)} %get-tuple-element.87), channel_id=1, source_target_pairs={{0,4},{2,6},{4,0},{6,2},{1,5},{3,7},{5,1},{7,3},{8,12},{10,14},{12... | collective-permute-start | bytes 786440 | tf_op jit(solution)/shard_map/ppermute | solution.py:463
  23.8 8.2 %value_block.1 = (bf16[4,64,256]{2,1,0:T(8,128)(2,1)S(1)}, bf16[4,64,256]{2,1,0:T(8,128)(2,1)S(1)}, bf16[4,64,256]{2,1,0:T(8,128)(2,1)S(1)}, bf16[4,64,256]{2,1,...) custom-call(bf16[512,1024]{1,0:T(8,128)(2,1)S(1)} %bitcast.9, ...), custom_call_target="tpu_custom_call" | custom-call | flops 2415919104 | bytes 13914112 | tf_op jit(solution)/shard_map/value_block/pallas_call | solution.py:444
  33.5 3.8 %collective-permute-start.5 = (bf16[4,64,256]{2,1,0:T(8,128)(2,1)S(1)}, bf16[4,64,256]{2,1,0:T(8,128)(2,1)S(1)}, u32[]{:S(2)}, u32[]{:S(2)}) collective-permute-start(bf16[4,64,256]{2,1,0:T(8,128)(2,1)S(1)} %get-tuple-element.83), channel_id=1, source_target_pairs={{0,4},{2,6},{4,0},{6,2},{1,5},{3,7},{5,1},{7,3},{8,12},{10,14},{12... | collective-permute-start | bytes 393224 | tf_op jit(solution)/shard_map/ppermute | solution.py:463
  37.4 4.8 %collective-permute-start.17 = (bf16[4,64,256]{2,1,0:T(8,128)(2,1)S(1)}, bf16[4,64,256]{2,1,0:T(8,128)(2,1)S(1)}, u32[]{:S(2)}, u32[]{:S(2)}) collective-permute-start(bf16[4,64,256]{2,1,0:T(8,128)(2,1)S(1)} %get-tuple-element.99), channel_id=1, source_target_pairs={{0,2},{2,0},{4,6},{6,4},{1,3},{3,1},{5,7},{7,5},{8,10},{10,8},{12,... | collective-permute-start | bytes 393224 | tf_op jit(solution)/shard_map/ppermute | solution.py:463
  43.4 11.7 %collective-permute-start.14 = (bf16[272,512]{1,0:T(8,128)(2,1)S(1)}, bf16[272,512]{1,0:T(8,128)(2,1)S(1)}, u32[]{:S(2)}, u32[]{:S(2)}) collective-permute-start(bf16[272,512]{1,0:T(8,128)(2,1)S(1)} %get-tuple-element.95), channel_id=1, source_target_pairs={{0,2},{2,0},{4,6},{6,4},{1,3},{3,1},{5,7},{7,5},{8,10},{10,8},{12,... | collective-permute-start | bytes 835592 | tf_op jit(solution)/shard_map/ppermute | solution.py:463
  55.1 1.6 collective-permute-start.15
  56.7 2.3 %collective-permute-start.16 = (bf16[272,512]{1,0:T(8,128)(2,1)S(1)}, bf16[272,512]{1,0:T(8,128)(2,1)S(1)}, u32[]{:S(2)}, u32[]{:S(2)}) collective-permute-start(bf16[272,512]{1,0:T(8,128)(2,1)S(1)} %get-tuple-element.97), channel_id=1, source_target_pairs={{0,6},{2,4},{4,2},{6,0},{1,7},{3,5},{5,3},{7,1},{8,14},{10,12},{12... | collective-permute-start | bytes 835592 | tf_op jit(solution)/shard_map/ppermute | solution.py:463
  59.1 1.9 %collective-permute-start.18 = (bf16[4,64,256]{2,1,0:T(8,128)(2,1)S(1)}, bf16[4,64,256]{2,1,0:T(8,128)(2,1)S(1)}, u32[]{:S(2)}, u32[]{:S(2)}) collective-permute-start(bf16[4,64,256]{2,1,0:T(8,128)(2,1)S(1)} %get-tuple-element.100), channel_id=1, source_target_pairs={{0,4},{2,6},{4,0},{6,2},{1,5},{3,7},{5,1},{7,3},{8,12},{10,14},{12... | collective-permute-start | bytes 393224 | tf_op jit(solution)/shard_map/ppermute | solution.py:463
  62.6 29.4 %collective-permute-done.18.refs_2_ = bf16[4,64,256]{2,1,0:T(8,128)(2,1)S(1)} collective-permute-done((bf16[4,64,256]{2,1,0:T(8,128)(2,1)S(1)}, bf16[4,64,256]{2,1,0:T(8,128)(2,1)S(1)}, u32[]{:S(2)}, u32[]{:S(2)}) %collective-permute-start.18) | collective-permute-done | bytes 131104 | tf_op jit(solution)/shard_map/ppermute | solution.py:463
  92.8 10.7 %grad_out.1 = (bf16[1024,1024]{1,0:T(8,128)(2,1)}, bf16[512,1024]{1,0:T(8,128)(2,1)S(1)}, f32[3,1024]{1,0:T(4,128)S(1)}, bf16[256,1024]{1,0:T(8,128)(2,1)S(1)}, ...) custom-call(bf16[272,512]{1,0:T(8,128)(2,1)S(1)} %get-tuple-element.90.refs_4_.refs_0_, ...), custom_call_target="tpu_custom_call" | custom-call | flops 2147483 | bytes 10903 | tf_op jit(solution)/shard_map/grad_out/pallas_call | solution.py:444
  103.5 2.0 %collective-permute-start.23 = (bf16[256,1024]{1,0:T(8,128)(2,1)S(1)}, bf16[256,1024]{1,0:T(8,128)(2,1)S(1)}, u32[]{:S(2)}, u32[]{:S(2)}) collective-permute-start(bf16[256,1024]{1,0:T(8,128)(2,1)S(1)} %get-tuple-element.114), channel_id=1, source_target_pairs={{0,8},{8,0},{16,24},{24,16},{1,9},{9,1},{17,25},{25,17},{2,10},{10... | collective-permute-start | bytes 1572872 | tf_op jit(solution)/shard_map/ppermute | solution.py:463
  105.5 2.7 %collective-permute-start.20 = (bf16[272,256]{1,0:T(8,128)(2,1)S(1)}, bf16[272,256]{1,0:T(8,128)(2,1)S(1)}, u32[]{:S(2)}, u32[]{:S(2)}) collective-permute-start(bf16[272,256]{1,0:T(8,128)(2,1)S(1)} %get-tuple-element.111), channel_id=1, source_target_pairs={{0,2},{2,0},{4,6},{6,4},{1,3},{3,1},{5,7},{7,5},{8,10},{10,8},{12,... | collective-permute-start | bytes 417800 | tf_op jit(solution)/shard_map/ppermute | solution.py:463
  108.2 3.0 %collective-permute-start.12 = (bf16[272,256]{1,0:T(8,128)(2,1)S(1)}, bf16[272,256]{1,0:T(8,128)(2,1)S(1)}, u32[]{:S(2)}, u32[]{:S(2)}) collective-permute-start(bf16[272,256]{1,0:T(8,128)(2,1)S(1)} %get-tuple-element.93), channel_id=1, source_target_pairs={{0,4},{2,6},{4,0},{6,2},{1,5},{3,7},{5,1},{7,3},{8,12},{10,14},{12... | collective-permute-start | bytes 417800 | tf_op jit(solution)/shard_map/ppermute | solution.py:463
  111.2 1.5 collective-permute-start.29
  112.7 2.9 %collective-permute-done.20.refs_1_ = bf16[272,256]{1,0:T(8,128)(2,1)S(1)} collective-permute-done((bf16[272,256]{1,0:T(8,128)(2,1)S(1)}, bf16[272,256]{1,0:T(8,128)(2,1)S(1)}, u32[]{:S(2)}, u32[]{:S(2)}) %collective-permute-start.20) | collective-permute-done | bytes 139296 | tf_op jit(solution)/shard_map/ppermute | solution.py:463
  115.6 1.5 collective-permute-start.30
  117.1 2.5 %collective-permute-start.13 = (bf16[272,256]{1,0:T(8,128)(2,1)S(1)}, bf16[272,256]{1,0:T(8,128)(2,1)S(1)}, u32[]{:S(2)}, u32[]{:S(2)}) collective-permute-start(bf16[272,256]{1,0:T(8,128)(2,1)S(1)} %get-tuple-element.94), channel_id=1, source_target_pairs={{0,6},{2,4},{4,2},{6,0},{1,7},{3,5},{5,3},{7,1},{8,14},{10,12},{12... | collective-permute-start | bytes 417800 | tf_op jit(solution)/shard_map/ppermute | solution.py:463
  119.6 4.5 %collective-permute-done.13.refs_3_ = bf16[272,256]{1,0:T(8,128)(2,1)S(1)} collective-permute-done((bf16[272,256]{1,0:T(8,128)(2,1)S(1)}, bf16[272,256]{1,0:T(8,128)(2,1)S(1)}, u32[]{:S(2)}, u32[]{:S(2)}) %collective-permute-start.13) | collective-permute-done | bytes 139296 | tf_op jit(solution)/shard_map/ppermute | solution.py:463
  124.1 3.8 %collective-permute-start.21 = (bf16[272,256]{1,0:T(8,128)(2,1)S(1)}, bf16[272,256]{1,0:T(8,128)(2,1)S(1)}, u32[]{:S(2)}, u32[]{:S(2)}) collective-permute-start(bf16[272,256]{1,0:T(8,128)(2,1)S(1)} %get-tuple-element.112), channel_id=1, source_target_pairs={{0,4},{2,6},{4,0},{6,2},{1,5},{3,7},{5,1},{7,3},{8,12},{10,14},{12... | collective-permute-start | bytes 417800 | tf_op jit(solution)/shard_map/ppermute | solution.py:463
  130.4 5.0 %collective-permute-done.21.refs_2_ = bf16[272,256]{1,0:T(8,128)(2,1)S(1)} collective-permute-done((bf16[272,256]{1,0:T(8,128)(2,1)S(1)}, bf16[272,256]{1,0:T(8,128)(2,1)S(1)}, u32[]{:S(2)}, u32[]{:S(2)}) %collective-permute-start.21) | collective-permute-done | bytes 139296 | tf_op jit(solution)/shard_map/ppermute | solution.py:463
  136.0 1.4 collective-permute-start.32
  139.6 1.6 collective-permute-start.34
  141.7 1.5 collective-permute-start.36
  143.3 1.5 collective-permute-start.33
  144.8 4.6 %collective-permute-done.33.refs_7_ = bf16[256,256]{1,0:T(8,128)(2,1)S(1)} collective-permute-done((bf16[256,256]{1,0:T(8,128)(2,1)S(1)}, bf16[256,256]{1,0:T(8,128)(2,1)S(1)}, u32[]{:S(2)}, u32[]{:S(2)}) %collective-permute-start.33) | collective-permute-done | bytes 131104 | tf_op jit(solution)/shard_map/ppermute | solution.py:463
  152.6 2.3 %collective-permute-start.38 = (bf16[144,768]{1,0:T(8,128)(2,1)S(1)}, bf16[144,768]{1,0:T(8,128)(2,1)S(1)}, u32[]{:S(2)}, u32[]{:S(2)}) collective-permute-start(bf16[144,768]{1,0:T(8,128)(2,1)S(1)} %get-tuple-element.143), channel_id=1, source_target_pairs={{0,2},{2,0},{4,6},{6,4},{1,3},{3,1},{5,7},{7,5},{8,10},{10,8},{12,... | collective-permute-start | bytes 663560 | tf_op jit(solution)/shard_map/ppermute | solution.py:463
  157.7 5.2 %in_first.1.refs_9_ = f32[512,1024]{1,0:T(8,128)S(1)} custom-call(bf16[1024,1024]{1,0:T(8,128)(2,1)S(1)} %copy-done.5, bf16[512,1024]{1,0:T(8,128)(2,1)S(1)} %collective-permute-done.28.got_ref, bf16[1024,3072]{1,0:T(8,128)(2,1)} %refs_8_.8, bf16[304,256]{1,0:T(8,128)(2,1)S(1)} %get-tuple-element.128.after_ref.refs_10_.refs_8_), custom_call_target="tpu_custom_call" | custom-call | flops 2147483648 | bytes 11689984 | tf_op jit(solution)/shard_map/in_first/pallas_call | solution.py:444
  162.8 5.4 %in_last.1 = (bf16[512,1024]{1,0:T(8,128)(2,1)}, bf16[512,1024]{1,0:T(8,128)(2,1)}, f32[8,128]{1,0:T(8,128)S(1)}) custom-call(bf16[1024,256]{1,0:T(8,128)(2,1)S(1)} %get-tuple-element.110.refs_2_.refs_0_, bf16[1024,256]{1,0:T(8,128)(2,1)S(1)} %get-tuple-element.116.refs_2_.refs_1_, bf16[512,256]{1,0:T(8,128)(2,1)S(1)} %collective-permute-done.24.refs_2_, ...), custom_call_target="tpu_custom_call" | custom-call | flops 1073741824 | bytes 13266944 | tf_op jit(solution)/shard_map/in_last/pallas_call | solution.py:444
  168.3 5.3 %collective-permute-done.39.refs_2_ = bf16[144,768]{1,0:T(8,128)(2,1)S(1)} collective-permute-done((bf16[144,768]{1,0:T(8,128)(2,1)S(1)}, bf16[144,768]{1,0:T(8,128)(2,1)S(1)}, u32[]{:S(2)}, u32[]{:S(2)}) %collective-permute-start.39) | collective-permute-done | bytes 221216 | tf_op jit(solution)/shard_map/ppermute | solution.py:463
  (96 shorter events, 25.8 us)
Async XLA Ops:
  0.6 10.9 %collective-permute-start = (bf16[512,1024]{1,0:T(8,128)(2,1)}, bf16[512,1024]{1,0:T(8,128)(2,1)S(1)}, u32[]{:S(2)}, u32[]{:S(2)}) collective-permute-start(bf16[512,1024]{1,0:T(8,128)(2,1)} %bitcast.6), channel_id=1, source_target_pairs={{0,1},{1,0},{2,3},{3,2},{4,5},{5,4},{6,7},{7,6},{8,9},{9,8},{10,11... | collective-permute-start | bytes 3145736 | tf_op jit(solution)/shard_map/ppermute | solution.py:456
  4.6 28.9 %collective-permute-start.10 = (bf16[16,32,512]{2,1,0:T(8,128)(2,1)S(1)}, bf16[16,32,512]{2,1,0:T(8,128)(2,1)S(1)}, u32[]{:S(2)}, u32[]{:S(2)}) collective-permute-start(bf16[16,32,512]{2,1,0:T(8,128)(2,1)S(1)} %constant_dynamic-slice_fusion), channel_id=1, source_target_pairs={{0,1},{1,0},{2,3},{3,2},{4,5},{5,4},{6,7},{7,6},{8,9},{9,8},{10,11... | collective-permute-start | bytes 1572872 | tf_op jit(solution)/shard_map/ppermute | solution.py:456
  17.3 20.0 %collective-permute-start.7 = (bf16[4,64,512]{2,1,0:T(8,128)(2,1)S(1)}, bf16[4,64,512]{2,1,0:T(8,128)(2,1)S(1)}, u32[]{:S(2)}, u32[]{:S(2)}) collective-permute-start(bf16[4,64,512]{2,1,0:T(8,128)(2,1)S(1)} %get-tuple-element.86), channel_id=1, source_target_pairs={{0,2},{2,0},{4,6},{6,4},{1,3},{3,1},{5,7},{7,5},{8,10},{10,8},{12,... | collective-permute-start | bytes 786440 | tf_op jit(solution)/shard_map/ppermute | solution.py:463
  20.8 16.6 %collective-permute-start.8 = (bf16[4,64,512]{2,1,0:T(8,128)(2,1)S(1)}, bf16[4,64,512]{2,1,0:T(8,128)(2,1)S(1)}, u32[]{:S(2)}, u32[]{:S(2)}) collective-permute-start(bf16[4,64,512]{2,1,0:T(8,128)(2,1)S(1)} %get-tuple-element.87), channel_id=1, source_target_pairs={{0,4},{2,6},{4,0},{6,2},{1,5},{3,7},{5,1},{7,3},{8,12},{10,14},{12... | collective-permute-start | bytes 786440 | tf_op jit(solution)/shard_map/ppermute | solution.py:463
  23.8 18.4 %collective-permute-start.9 = (bf16[4,64,512]{2,1,0:T(8,128)(2,1)S(1)}, bf16[4,64,512]{2,1,0:T(8,128)(2,1)S(1)}, u32[]{:S(2)}, u32[]{:S(2)}) collective-permute-start(bf16[4,64,512]{2,1,0:T(8,128)(2,1)S(1)} %get-tuple-element.88), channel_id=1, source_target_pairs={{0,6},{2,4},{4,2},{6,0},{1,7},{3,5},{5,3},{7,1},{8,14},{10,12},{12... | collective-permute-start | bytes 786440 | tf_op jit(solution)/shard_map/ppermute | solution.py:463
  33.0 22.1 %collective-permute-start.4 = (bf16[4,64,256]{2,1,0:T(8,128)(2,1)S(1)}, bf16[4,64,256]{2,1,0:T(8,128)(2,1)S(1)}, u32[]{:S(2)}, u32[]{:S(2)}) collective-permute-start(bf16[4,64,256]{2,1,0:T(8,128)(2,1)S(1)} %get-tuple-element.82), channel_id=1, source_target_pairs={{0,2},{2,0},{4,6},{6,4},{1,3},{3,1},{5,7},{7,5},{8,10},{10,8},{12,... | collective-permute-start | bytes 393224 | tf_op jit(solution)/shard_map/ppermute | solution.py:463
  33.5 23.2 %collective-permute-start.5 = (bf16[4,64,256]{2,1,0:T(8,128)(2,1)S(1)}, bf16[4,64,256]{2,1,0:T(8,128)(2,1)S(1)}, u32[]{:S(2)}, u32[]{:S(2)}) collective-permute-start(bf16[4,64,256]{2,1,0:T(8,128)(2,1)S(1)} %get-tuple-element.83), channel_id=1, source_target_pairs={{0,4},{2,6},{4,0},{6,2},{1,5},{3,7},{5,1},{7,3},{8,12},{10,14},{12... | collective-permute-start | bytes 393224 | tf_op jit(solution)/shard_map/ppermute | solution.py:463
  37.4 21.7 %collective-permute-start.6 = (bf16[4,64,256]{2,1,0:T(8,128)(2,1)S(1)}, bf16[4,64,256]{2,1,0:T(8,128)(2,1)S(1)}, u32[]{:S(2)}, u32[]{:S(2)}) collective-permute-start(bf16[4,64,256]{2,1,0:T(8,128)(2,1)S(1)} %get-tuple-element.84), channel_id=1, source_target_pairs={{0,6},{2,4},{4,2},{6,0},{1,7},{3,5},{5,3},{7,1},{8,14},{10,12},{12... | collective-permute-start | bytes 393224 | tf_op jit(solution)/shard_map/ppermute | solution.py:463
  37.4 23.6 %collective-permute-start.17 = (bf16[4,64,256]{2,1,0:T(8,128)(2,1)S(1)}, bf16[4,64,256]{2,1,0:T(8,128)(2,1)S(1)}, u32[]{:S(2)}, u32[]{:S(2)}) collective-permute-start(bf16[4,64,256]{2,1,0:T(8,128)(2,1)S(1)} %get-tuple-element.99), channel_id=1, source_target_pairs={{0,2},{2,0},{4,6},{6,4},{1,3},{3,1},{5,7},{7,5},{8,10},{10,8},{12,... | collective-permute-start | bytes 393224 | tf_op jit(solution)/shard_map/ppermute | solution.py:463
  43.4 49.3 %collective-permute-start.14 = (bf16[272,512]{1,0:T(8,128)(2,1)S(1)}, bf16[272,512]{1,0:T(8,128)(2,1)S(1)}, u32[]{:S(2)}, u32[]{:S(2)}) collective-permute-start(bf16[272,512]{1,0:T(8,128)(2,1)S(1)} %get-tuple-element.95), channel_id=1, source_target_pairs={{0,2},{2,0},{4,6},{6,4},{1,3},{3,1},{5,7},{7,5},{8,10},{10,8},{12,... | collective-permute-start | bytes 835592 | tf_op jit(solution)/shard_map/ppermute | solution.py:463
  55.1 37.7 %collective-permute-start.15 = (bf16[272,512]{1,0:T(8,128)(2,1)S(1)}, bf16[272,512]{1,0:T(8,128)(2,1)S(1)}, u32[]{:S(2)}, u32[]{:S(2)}) collective-permute-start(bf16[272,512]{1,0:T(8,128)(2,1)S(1)} %get-tuple-element.96), channel_id=1, source_target_pairs={{0,4},{2,6},{4,0},{6,2},{1,5},{3,7},{5,1},{7,3},{8,12},{10,14},{12... | collective-permute-start | bytes 835592 | tf_op jit(solution)/shard_map/ppermute | solution.py:463
  56.7 36.0 %collective-permute-start.16 = (bf16[272,512]{1,0:T(8,128)(2,1)S(1)}, bf16[272,512]{1,0:T(8,128)(2,1)S(1)}, u32[]{:S(2)}, u32[]{:S(2)}) collective-permute-start(bf16[272,512]{1,0:T(8,128)(2,1)S(1)} %get-tuple-element.97), channel_id=1, source_target_pairs={{0,6},{2,4},{4,2},{6,0},{1,7},{3,5},{5,3},{7,1},{8,14},{10,12},{12... | collective-permute-start | bytes 835592 | tf_op jit(solution)/shard_map/ppermute | solution.py:463
  59.1 32.9 %collective-permute-start.18 = (bf16[4,64,256]{2,1,0:T(8,128)(2,1)S(1)}, bf16[4,64,256]{2,1,0:T(8,128)(2,1)S(1)}, u32[]{:S(2)}, u32[]{:S(2)}) collective-permute-start(bf16[4,64,256]{2,1,0:T(8,128)(2,1)S(1)} %get-tuple-element.100), channel_id=1, source_target_pairs={{0,4},{2,6},{4,0},{6,2},{1,5},{3,7},{5,1},{7,3},{8,12},{10,14},{12... | collective-permute-start | bytes 393224 | tf_op jit(solution)/shard_map/ppermute | solution.py:463
  61.0 31.0 %collective-permute-start.19 = (bf16[4,64,256]{2,1,0:T(8,128)(2,1)S(1)}, bf16[4,64,256]{2,1,0:T(8,128)(2,1)S(1)}, u32[]{:S(2)}, u32[]{:S(2)}) collective-permute-start(bf16[4,64,256]{2,1,0:T(8,128)(2,1)S(1)} %get-tuple-element.101), channel_id=1, source_target_pairs={{0,6},{2,4},{4,2},{6,0},{1,7},{3,5},{5,3},{7,1},{8,14},{10,12},{12... | collective-permute-start | bytes 393224 | tf_op jit(solution)/shard_map/ppermute | solution.py:463
  103.5 24.4 %collective-permute-start.23 = (bf16[256,1024]{1,0:T(8,128)(2,1)S(1)}, bf16[256,1024]{1,0:T(8,128)(2,1)S(1)}, u32[]{:S(2)}, u32[]{:S(2)}) collective-permute-start(bf16[256,1024]{1,0:T(8,128)(2,1)S(1)} %get-tuple-element.114), channel_id=1, source_target_pairs={{0,8},{8,0},{16,24},{24,16},{1,9},{9,1},{17,25},{25,17},{2,10},{10... | collective-permute-start | bytes 1572872 | tf_op jit(solution)/shard_map/ppermute | solution.py:463
  105.5 10.1 %collective-permute-start.20 = (bf16[272,256]{1,0:T(8,128)(2,1)S(1)}, bf16[272,256]{1,0:T(8,128)(2,1)S(1)}, u32[]{:S(2)}, u32[]{:S(2)}) collective-permute-start(bf16[272,256]{1,0:T(8,128)(2,1)S(1)} %get-tuple-element.111), channel_id=1, source_target_pairs={{0,2},{2,0},{4,6},{6,4},{1,3},{3,1},{5,7},{7,5},{8,10},{10,8},{12,... | collective-permute-start | bytes 417800 | tf_op jit(solution)/shard_map/ppermute | solution.py:463
  108.2 9.0 %collective-permute-start.11 = (bf16[272,256]{1,0:T(8,128)(2,1)S(1)}, bf16[272,256]{1,0:T(8,128)(2,1)S(1)}, u32[]{:S(2)}, u32[]{:S(2)}) collective-permute-start(bf16[272,256]{1,0:T(8,128)(2,1)S(1)} %get-tuple-element.92), channel_id=1, source_target_pairs={{0,2},{2,0},{4,6},{6,4},{1,3},{3,1},{5,7},{7,5},{8,10},{10,8},{12,... | collective-permute-start | bytes 417800 | tf_op jit(solution)/shard_map/ppermute | solution.py:463
  108.2 11.4 %collective-permute-start.12 = (bf16[272,256]{1,0:T(8,128)(2,1)S(1)}, bf16[272,256]{1,0:T(8,128)(2,1)S(1)}, u32[]{:S(2)}, u32[]{:S(2)}) collective-permute-start(bf16[272,256]{1,0:T(8,128)(2,1)S(1)} %get-tuple-element.93), channel_id=1, source_target_pairs={{0,4},{2,6},{4,0},{6,2},{1,5},{3,7},{5,1},{7,3},{8,12},{10,14},{12... | collective-permute-start | bytes 417800 | tf_op jit(solution)/shard_map/ppermute | solution.py:463
  111.2 28.4 %collective-permute-start.29 = (bf16[256,1024]{1,0:T(8,128)(2,1)S(1)}, bf16[256,1024]{1,0:T(8,128)(2,1)S(1)}, u32[]{:S(2)}, u32[]{:S(2)}) collective-permute-start(bf16[256,1024]{1,0:T(8,128)(2,1)S(1)} %get-tuple-element.131), channel_id=1, source_target_pairs={{0,16},{8,24},{16,0},{24,8},{1,17},{9,25},{17,1},{25,9},{2,18},{10... | collective-permute-start | bytes 1572872 | tf_op jit(solution)/shard_map/ppermute | solution.py:463
  115.6 25.6 %collective-permute-start.30 = (bf16[256,1024]{1,0:T(8,128)(2,1)S(1)}, bf16[256,1024]{1,0:T(8,128)(2,1)S(1)}, u32[]{:S(2)}, u32[]{:S(2)}) collective-permute-start(bf16[256,1024]{1,0:T(8,128)(2,1)S(1)} %get-tuple-element.132), channel_id=1, source_target_pairs={{0,24},{8,16},{16,8},{24,0},{1,25},{9,17},{17,9},{25,1},{2,26},{10... | collective-permute-start | bytes 1572872 | tf_op jit(solution)/shard_map/ppermute | solution.py:463
  119.6 36.7 %collective-permute-start.28 = (bf16[512,1024]{1,0:T(8,128)(2,1)S(1)}, bf16[512,1024]{1,0:T(8,128)(2,1)S(1)}, u32[]{:S(2)}, u32[]{:S(2)}) collective-permute-start(bf16[512,1024]{1,0:T(8,128)(2,1)S(1)} %get-tuple-element.124), channel_id=1, source_target_pairs={{0,1},{1,0},{2,3},{3,2},{4,5},{5,4},{6,7},{7,6},{8,9},{9,8},{10,11... | collective-permute-start | bytes 3145736 | tf_op jit(solution)/shard_map/ppermute | solution.py:456
  124.1 11.3 %collective-permute-start.21 = (bf16[272,256]{1,0:T(8,128)(2,1)S(1)}, bf16[272,256]{1,0:T(8,128)(2,1)S(1)}, u32[]{:S(2)}, u32[]{:S(2)}) collective-permute-start(bf16[272,256]{1,0:T(8,128)(2,1)S(1)} %get-tuple-element.112), channel_id=1, source_target_pairs={{0,4},{2,6},{4,0},{6,2},{1,5},{3,7},{5,1},{7,3},{8,12},{10,14},{12... | collective-permute-start | bytes 417800 | tf_op jit(solution)/shard_map/ppermute | solution.py:463
  127.9 8.1 %collective-permute-start.22 = (bf16[272,256]{1,0:T(8,128)(2,1)S(1)}, bf16[272,256]{1,0:T(8,128)(2,1)S(1)}, u32[]{:S(2)}, u32[]{:S(2)}) collective-permute-start(bf16[272,256]{1,0:T(8,128)(2,1)S(1)} %get-tuple-element.113), channel_id=1, source_target_pairs={{0,6},{2,4},{4,2},{6,0},{1,7},{3,5},{5,3},{7,1},{8,14},{10,12},{12... | collective-permute-start | bytes 417800 | tf_op jit(solution)/shard_map/ppermute | solution.py:463
  136.0 7.3 %collective-permute-start.32 = (bf16[256,256]{1,0:T(8,128)(2,1)S(1)}, bf16[256,256]{1,0:T(8,128)(2,1)S(1)}, u32[]{:S(2)}, u32[]{:S(2)}) collective-permute-start(bf16[256,256]{1,0:T(8,128)(2,1)S(1)} %get-tuple-element.134), channel_id=1, source_target_pairs={{0,16},{8,24},{16,0},{24,8},{1,17},{9,25},{17,1},{25,9},{2,18},{10... | collective-permute-start | bytes 393224 | tf_op jit(solution)/shard_map/ppermute | solution.py:463
  139.6 9.8 %collective-permute-start.34 = (bf16[304,256]{1,0:T(8,128)(2,1)S(1)}, bf16[304,256]{1,0:T(8,128)(2,1)S(1)}, u32[]{:S(2)}, u32[]{:S(2)}) collective-permute-start(bf16[304,256]{1,0:T(8,128)(2,1)S(1)} %get-tuple-element.136), channel_id=1, source_target_pairs={{0,8},{8,0},{16,24},{24,16},{1,9},{9,1},{17,25},{25,17},{2,10},{10... | collective-permute-start | bytes 466952 | tf_op jit(solution)/shard_map/ppermute | solution.py:463
  141.2 8.3 %collective-permute-start.35 = (bf16[304,256]{1,0:T(8,128)(2,1)S(1)}, bf16[304,256]{1,0:T(8,128)(2,1)S(1)}, u32[]{:S(2)}, u32[]{:S(2)}) collective-permute-start(bf16[304,256]{1,0:T(8,128)(2,1)S(1)} %get-tuple-element.137), channel_id=1, source_target_pairs={{0,16},{8,24},{16,0},{24,8},{1,17},{9,25},{17,1},{25,9},{2,18},{10... | collective-permute-start | bytes 466952 | tf_op jit(solution)/shard_map/ppermute | solution.py:463
  141.7 7.8 %collective-permute-start.36 = (bf16[304,256]{1,0:T(8,128)(2,1)S(1)}, bf16[304,256]{1,0:T(8,128)(2,1)S(1)}, u32[]{:S(2)}, u32[]{:S(2)}) collective-permute-start(bf16[304,256]{1,0:T(8,128)(2,1)S(1)} %get-tuple-element.138), channel_id=1, source_target_pairs={{0,24},{8,16},{16,8},{24,0},{1,25},{9,17},{17,9},{25,1},{2,26},{10... | collective-permute-start | bytes 466952 | tf_op jit(solution)/shard_map/ppermute | solution.py:463
  151.1 11.8 %collective-permute-start.25 = (bf16[512,256]{1,0:T(8,128)(2,1)S(1)}, bf16[512,256]{1,0:T(8,128)(2,1)S(1)}, u32[]{:S(2)}, u32[]{:S(2)}) collective-permute-start(bf16[512,256]{1,0:T(8,128)(2,1)S(1)} %get-tuple-element.118), channel_id=1, source_target_pairs={{0,1},{1,0},{2,3},{3,2},{4,5},{5,4},{6,7},{7,6},{8,9},{9,8},{10,11... | collective-permute-start | bytes 786440 | tf_op jit(solution)/shard_map/ppermute | solution.py:456
  152.2 10.6 %collective-permute-start.27 = (bf16[512,256]{1,0:T(8,128)(2,1)S(1)}, bf16[512,256]{1,0:T(8,128)(2,1)S(1)}, u32[]{:S(2)}, u32[]{:S(2)}) collective-permute-start(bf16[512,256]{1,0:T(8,128)(2,1)S(1)} %get-tuple-element.122), channel_id=1, source_target_pairs={{0,1},{1,0},{2,3},{3,2},{4,5},{5,4},{6,7},{7,6},{8,9},{9,8},{10,11... | collective-permute-start | bytes 786440 | tf_op jit(solution)/shard_map/ppermute | solution.py:456
  152.6 15.7 %collective-permute-start.38 = (bf16[144,768]{1,0:T(8,128)(2,1)S(1)}, bf16[144,768]{1,0:T(8,128)(2,1)S(1)}, u32[]{:S(2)}, u32[]{:S(2)}) collective-permute-start(bf16[144,768]{1,0:T(8,128)(2,1)S(1)} %get-tuple-element.143), channel_id=1, source_target_pairs={{0,2},{2,0},{4,6},{6,4},{1,3},{3,1},{5,7},{7,5},{8,10},{10,8},{12,... | collective-permute-start | bytes 663560 | tf_op jit(solution)/shard_map/ppermute | solution.py:463
  154.9 18.7 %collective-permute-start.39 = (bf16[144,768]{1,0:T(8,128)(2,1)S(1)}, bf16[144,768]{1,0:T(8,128)(2,1)S(1)}, u32[]{:S(2)}, u32[]{:S(2)}) collective-permute-start(bf16[144,768]{1,0:T(8,128)(2,1)S(1)} %get-tuple-element.144), channel_id=1, source_target_pairs={{0,4},{2,6},{4,0},{6,2},{1,5},{3,7},{5,1},{7,3},{8,12},{10,14},{12... | collective-permute-start | bytes 663560 | tf_op jit(solution)/shard_map/ppermute | solution.py:463
  156.3 17.3 %collective-permute-start.40 = (bf16[144,768]{1,0:T(8,128)(2,1)S(1)}, bf16[144,768]{1,0:T(8,128)(2,1)S(1)}, u32[]{:S(2)}, u32[]{:S(2)}) collective-permute-start(bf16[144,768]{1,0:T(8,128)(2,1)S(1)} %get-tuple-element.145), channel_id=1, source_target_pairs={{0,6},{2,4},{4,2},{6,0},{1,7},{3,5},{5,3},{7,1},{8,14},{10,12},{12... | collective-permute-start | bytes 663560 | tf_op jit(solution)/shard_map/ppermute | solution.py:463
  (23 other events, 192.1 us)
